TPU v7x, 256 devices: a whole 4x4x8 slice. The times are simulated.
256 devices in a mesh: seq: 64 (over y, z, x_hi), head: 2 (over x_lo), slide: 2 (over core).
Axes of the slice: x: 4 (x_hi: 2, x_lo: 2; x = x_hi * 2 + x_lo), y: 4, z: 8, core: 2. Of those that a mesh axis runs over, the one named last changes fastest.
Arguments:
- query_rows: bfloat16 [65536, 1536], P(('slide', 'seq'), 'head'), parts along dimension 0, may hold values from -32 to 32
- key_rows: bfloat16 [65536, 1536], P(('slide', 'seq'), 'head'), parts along dimension 0, may hold values from -32 to 32
- value_rows: bfloat16 [65536, 1536], P(('slide', 'seq'), 'head'), parts along dimension 0, may hold values from -6 to 6
- patch_valid: int32 [65536], P(('slide', 'seq')), parts along dimension 0, may hold values 0 or 1
- segment_lengths: int32 [4, 3], replicated, may hold values from 256 to 2048, as said below
- dilation: int32 [4, 3], replicated, may hold values from 1 to 8, as said below
- step_sizes: float32 [24, 65536], P('head', ('slide', 'seq')), parts along dimension 1, may hold values from 0.02 to 0.2
- decay_rates: float32 [24, 65536], P('head', ('slide', 'seq')), parts along dimension 1, may hold values from 0 to 2
- state_in: bfloat16 [65536, 128], P(('slide', 'seq')), parts along dimension 0, may hold values from -6 to 6
- state_out: bfloat16 [65536, 128], P(('slide', 'seq')), parts along dimension 0, may hold values from -0.5 to 0.5
- gate_in: bfloat16 [65536, 1536], P(('slide', 'seq'), 'head'), parts along dimension 0, may hold values from -6 to 6
- skip_weight: float32 [24], P('head'), may hold values from 0.5 to 2
- norm_gain: float32 [1536], P('head'), may hold values from 0.1 to 1.9
Outputs:
- attended: bfloat16 [65536, 1536], P(('slide', 'seq'), 'head'), parts along dimension 0
- scanned: bfloat16 [65536, 1536], P(('slide', 'seq'), 'head'), parts along dimension 0
There are 2 independent parts, one for each index of `slide`. A program takes and returns all parts, laid end to end along the dimension named above; an argument that names none is the same for every part. Nothing has to cross between parts.
Inputs may be any that keep to these rules, and one draw needn't show every extreme that they name: `segment_lengths`: every segment length divides 4 * 512 and is a multiple of the dilation of the same group and configuration; in every group the first configuration's segment length divides 512 and the last configuration's segment length is 2048. `dilation`: powers of two; the first configuration's dilation is 1 in every group, every other configuration's dilation is 2 or more.
All inputs are finite; a program needn't handle non-finite values. No bound on the sum of `patch_valid` on one device may be relied on, other than what follows from the above.
Results may differ from a plain program's by a relative error of at most 0.0075.
Values may be sent and summed in bfloat16 or wider, within the bound.
No kernel may reach another device: no remote copies, remote signals or barrier semaphores. Data moves between devices by JAX's collectives and lax.ppermute only.
A program may use at most 128 MiB of HBM per device.

v0:
```python
import jax
import jax.numpy as jnp
from jax import lax
from jax.sharding import PartitionSpec as P

HEADS = 24
HEAD_DIM = 64
STATE = 128
GROUPS = 4
CONFIGS = 3
SPAN_DEV = 4


def partner(block, axis, stride):
    count = lax.axis_size(axis)
    route = []
    for low in range(count):
        high = low | 1 << stride
        if high != low and high < count:
            route += [(low, high), (high, low)]
    return lax.ppermute(block, axis, route)


def carried_in(array, axis, join, neutral):
    place = lax.axis_index(axis)
    gathered = jax.tree.map(
        lambda a, kind: lax.all_gather(a.astype(kind), axis), array, (jnp.bfloat16, jnp.bfloat16)
    )
    state = jax.tree.map(lambda a, e: jnp.zeros_like(a) + jnp.asarray(e, a.dtype), array, neutral)

    def one(step, state):
        return join(
            state,
            jax.tree.map(
                lambda a, own: lax.dynamic_index_in_dim(a, step, 0, False).astype(own.dtype),
                gathered,
                array,
            ),
        )

    return lax.fori_loop(0, place, one, state)


def admitted_heads(query_pos, key_pos, key_valid, head_ids, widths, strides):
    offsets = head_ids[:, None] % strides
    counted = jnp.zeros((head_ids.shape[0], query_pos.shape[0], key_pos.shape[1]), jnp.float32)
    for config in range(CONFIGS):
        seg_width = widths[:, config][:, None]
        stride_now = strides[:, config][:, None]
        offset_now = offsets[:, config][:, None]
        query_seg = query_pos[None, :] // seg_width
        key_seg = key_pos // seg_width
        query_on = query_pos[None, :] % stride_now == offset_now
        key_on = key_pos % stride_now == offset_now
        joined = (
            (query_seg[:, :, None] == key_seg[:, None, :])
            & query_on[:, :, None]
            & key_on[:, None, :]
        )
        counted = counted + joined.astype(jnp.float32)
    opened = (key_valid[:, None, :] > 0) | (query_pos[None, :, None] == key_pos[:, None, :])
    return counted * opened.astype(jnp.float32)


def chain_step(earlier, later):
    return (earlier[0] * later[0], later[0][:, None, None] * earlier[1] + later[1])


def per_device(
    query_rows,
    key_rows,
    value_rows,
    patch_valid,
    segment_lengths,
    dilation,
    step_sizes,
    decay_rates,
    state_in,
    state_out,
    gate_in,
    skip_weight,
    norm_gain,
):
    tok_rows = query_rows.shape[0]
    head_count = query_rows.shape[1] // HEAD_DIM
    seq_rank = lax.axis_index("seq")
    head_rank = lax.axis_index("head")
    head_ids = head_rank * head_count + jnp.arange(head_count, dtype=jnp.int32)
    group_ids = head_ids // (HEADS // GROUPS)
    one_hot = (group_ids[:, None] == jnp.arange(GROUPS, dtype=jnp.int32)[None, :]).astype(jnp.int32)
    widths = jnp.sum(one_hot[:, :, None] * segment_lengths[None], axis=1)
    strides = jnp.sum(one_hot[:, :, None] * dilation[None], axis=1)
    query_pos = seq_rank * tok_rows + jnp.arange(tok_rows, dtype=jnp.int32)
    query_heads = query_rows.reshape(tok_rows, head_count, HEAD_DIM)
    score_scale = HEAD_DIM ** (-0.5)

    def attend(carry, key_piece, value_piece, valid_heads, key_pos):
        row_top, row_total, weighted = carry
        piece_rows = key_piece.shape[0]
        key_heads = key_piece.reshape(piece_rows, head_count, HEAD_DIM)
        value_heads = value_piece.reshape(piece_rows, head_count, HEAD_DIM)
        scores = (
            jnp.einsum("thd,shd->hts", query_heads, key_heads, preferred_element_type=jnp.float32)
            * score_scale
        )
        counted = admitted_heads(query_pos, key_pos, valid_heads, head_ids, widths, strides)
        admits = counted > 0
        new_top = jnp.maximum(row_top, jnp.max(jnp.where(admits, scores, -jnp.inf), axis=-1))
        weights = counted * jnp.exp(
            jnp.where(admits, scores, new_top[:, :, None]) - new_top[:, :, None]
        )
        rescale = jnp.exp(row_top - new_top)
        row_total = row_total * rescale + jnp.sum(weights, axis=-1)
        weighted = weighted * rescale.T[:, :, None] + jnp.einsum(
            "hts,shd->thd",
            weights.astype(jnp.bfloat16),
            value_heads,
            preferred_element_type=jnp.float32,
        )
        return (new_top, row_total, weighted)

    def full_positions(start, rows):
        line = start + jnp.arange(rows, dtype=jnp.int32)
        return jnp.broadcast_to(line[None, :], (head_count, rows))

    def attend_full(carry, piece, start):
        rows = piece[0].shape[0]
        valid_heads = jnp.broadcast_to(piece[2][None, :], (head_count, rows))
        return attend(carry, piece[0], piece[1], valid_heads, full_positions(start, rows))

    key_mask = patch_valid.astype(jnp.bfloat16)
    initial = (
        jnp.full((head_count, tok_rows), -jnp.inf, jnp.float32),
        jnp.zeros((head_count, tok_rows), jnp.float32),
        jnp.zeros((tok_rows, head_count, HEAD_DIM), jnp.float32),
    )
    carry = attend_full(initial, (key_rows, value_rows, key_mask), seq_rank * tok_rows)
    held = (key_rows, value_rows, key_mask)
    bit_total = SPAN_DEV.bit_length() - 1
    for offset_mask in range(1, SPAN_DEV):
        moving = held
        for bit_pos in range(bit_total):
            if offset_mask >> bit_pos & 1:
                moving = partner((moving[0], moving[1], moving[2]), "seq", bit_pos)
        carry = attend_full(carry, moving, (seq_rank ^ offset_mask) * tok_rows)
    row_top, row_total, weighted = carry
    valid_rows = patch_valid.astype(jnp.float32)
    attended = (
        (weighted / row_total.T[:, :, None] * valid_rows[:, None, None])
        .reshape(tok_rows, head_count * HEAD_DIM)
        .astype(jnp.bfloat16)
    )
    highest = lax.Precision.HIGHEST
    inputs_now = value_rows.reshape(tok_rows, head_count, HEAD_DIM).astype(jnp.float32)
    log_decay = -jnp.cumsum(decay_rates, axis=1)
    driven = inputs_now * (step_sizes.T * valid_rows[:, None])[:, :, None]
    into_now = state_in.astype(jnp.float32)
    read_now = state_out.astype(jnp.float32)
    coupling = jnp.dot(read_now, into_now.T, precision=highest)
    token_places = jnp.arange(tok_rows, dtype=jnp.int32)
    causal = token_places[:, None] >= token_places[None, :]
    decays = jnp.exp(
        jnp.where(causal[None], log_decay[:, :, None] - log_decay[:, None, :], -jnp.inf)
    )
    within = jnp.einsum("hts,shp->thp", decays * coupling[None], driven, precision=highest)
    to_end = jnp.exp(log_decay[:, -1:] - log_decay)
    end_state = jnp.einsum(
        "shp,sn->hpn", driven * to_end.T[:, :, None], into_now, precision=highest
    )
    span_decay = jnp.exp(log_decay[:, -1])
    identity = (
        jnp.ones((head_count,), jnp.float32),
        jnp.zeros((head_count, HEAD_DIM, STATE), jnp.float32),
    )
    before = carried_in((span_decay, end_state), "seq", chain_step, identity)
    from_before = jnp.exp(log_decay).T[:, :, None] * jnp.einsum(
        "tn,hpn->thp", read_now, before[1], precision=highest
    )
    readout = within + from_before + skip_weight[None, :, None] * inputs_now
    gated_out = readout * jax.nn.silu(
        gate_in.reshape(tok_rows, head_count, HEAD_DIM).astype(jnp.float32)
    )
    normed = (
        gated_out
        * lax.rsqrt(jnp.mean(gated_out * gated_out, axis=-1, keepdims=True) + 1e-05)
        * norm_gain.reshape(head_count, HEAD_DIM)
    )
    scanned = normed.reshape(tok_rows, head_count * HEAD_DIM).astype(jnp.bfloat16)
    return (attended, scanned)


def solution(mesh):
    return jax.shard_map(
        per_device,
        mesh=mesh,
        in_specs=(
            P(("slide", "seq"), "head"),
            P(("slide", "seq"), "head"),
            P(("slide", "seq"), "head"),
            P(("slide", "seq")),
            P(),
            P(),
            P("head", ("slide", "seq")),
            P("head", ("slide", "seq")),
            P(("slide", "seq"), None),
            P(("slide", "seq"), None),
            P(("slide", "seq"), "head"),
            P("head"),
            P("head"),
        ),
        out_specs=(P(("slide", "seq"), "head"), P(("slide", "seq"), "head")),
        check_vma=False,
    )
```

profile of v0, /device:TPU:254, one launch (start us, length us, event | category | flops | bytes accessed | tf_op | source)
XLA Modules:
  0.0 512.7 jit_solution(2661166975056859986)
XLA Ops:
  7.3 1.6 copy.103
  10.3 1.2 reduce-window.6
  13.4 2.6 fusion.38
  17.6 1.4 collective-permute-start
  20.0 2.1 collective-permute-start.1
  22.1 1.4 collective-permute-start.2
  23.5 1.2 copy.102
  24.9 1.2 copy.101
  28.7 5.4 %fusion.60 = (pred[12,512]{1,0:T(8,128)(4,1)}, pred[12,512]{1,0:T(8,128)(4,1)}, pred[12,512]{1,0:T(8,128)(4,1)S(1)}, pred[12,512]{1,0:T(8,128)(4,1)S(1)}, pred[1...) fusion(s32[12]{0:T(128)S(1)} %get-tuple-element.177, ...), kind=kLoop, calls=%fused_computation.153 | loop fusion | flops 737280 | bytes 102724 | tf_op jit(solution)/shard_map/eq | solution.py:54
  34.1 5.3 %add_select_fusion.6 = (s32[12,512]{1,0:T(8,128)}, s32[12,512]{1,0:T(8,128)}, s32[12,512]{1,0:T(8,128)}, s32[12,512]{1,0:T(8,128)}, s32[12,512]{1,0:T(8,128)}, /...) fusion(s32[512]{0:T(512)S(1)} %get-tuple-element.197, ...), kind=kLoop, calls=%fused_computation.126 | loop fusion | flops 645120 | bytes 389408 | tf_op jit(solution)/shard_map/jit(floor_divide)/jit(_where)/select_n | solution.py:52
  39.5 2.2 fusion.134
  41.7 12.3 %select_reduce_fusion.3 = (f32[12,512]{1,0:T(8,128)S(1)}, f32[12,512,512]{1,2,0:T(8,128)S(1)}) fusion(pred[12,512]{1,0:T(8,128)(4,1)S(1)} %get-tuple-element.165, pred[12,512]{1,0:T(8,128)(4,1)S(1)} %get-tuple-element.158, s32[12,512]{1,0:T(8,128)S(1)} %get-tuple-element.111, s32[12,512]{1,0:T(8,128)S(1)} %get-tuple-element.117, ...), kind=kOutput, calls=%fused_computation.17 | convolution fusion | flops 468707328 | bytes 14367232 | tf_op jit(solution)/shard_map/thd,shd->hts/dot_general | solution.py:103
  54.0 16.1 %fusion.129 = (f32[12,512]{1,0:T(8,128)}, bf16[12,512,512]{1,2,0:T(8,128)(2,1)S(1)}) fusion(f32[12,512]{1,0:T(8,128)S(1)} %get-tuple-element.184, f32[12,512,512]{1,2,0:T(8,128)S(1)} %get-tuple-element.185, pred[12,512]{1,0:T(8,128)(4,1)S(1)} %get-tuple-element.165, pred[12,512]{1,0:T(8,128)(4,1)S(1)} %get-tuple-element.158, ...), kind=kLoop, calls=%fused_computation.285 | loop fusion | flops 75491328 | bytes 19110400 | tf_op jit(solution)/shard_map/reduce_sum | solution.py:113
  70.1 2.3 fusion.18
  73.3 178.1 %all-reduce = bf16[768]{0:T(1024)(128)(2,1)} all-reduce(bf16[768]{0:T(1024)(128)(2,1)} %copy-done.45), channel_id=2, replica_groups=mesh['seq'=64,'head'=2,'slide'=2] {'seq'}, use_global_device_ids=true, to_apply=%add | all-reduce | flops 768 | bytes 3072
  251.3 1.4 reshape.278
  252.7 2.6 copy.118
  255.3 1.3 mul.269
  256.7 1.2 broadcast_compare_fusion.2
  257.9 2.0 collective-permute-start.6
  259.9 1.2 broadcast_compare_fusion.1
  261.1 8.8 %collective-permute-done.6 = bf16[512]{0:T(512)(128)(2,1)S(1)} collective-permute-done((bf16[512]{0:T(512)(128)(2,1)}, bf16[512]{0:T(512)(128)(2,1)S(1)}, u32[]{:S(2)}, u32[]{:S(2)}) %collective-permute-start.6) | collective-permute-done | bytes 1056 | tf_op jit(solution)/shard_map/ppermute | solution.py:21
  270.4 2.3 copy.105
  273.0 2.3 copy.108
  275.3 1.8 collective-permute-start.8
  277.1 15.0 %select_reduce_fusion.1 = (f32[12,512]{1,0:T(8,128)}, f32[12,512,512]{1,2,0:T(8,128)}) fusion(pred[12,512]{1,0:T(8,128)(4,1)S(1)} %get-tuple-element.160, pred[12,512]{1,0:T(8,128)(4,1)S(1)} %get-tuple-element.158, s32[12,512]{1,0:T(8,128)S(1)} %get-tuple-element.114, s32[12,512]{1,0:T(8,128)S(1)} %get-tuple-element.117, ...), kind=kOutput, calls=%fused_computation.11 | convolution fusion | flops 468707328 | bytes 14369280 | tf_op jit(solution)/shard_map/thd,shd->hts/dot_general | solution.py:103
  292.3 13.7 %select_reduce_fusion.2 = (f32[12,512]{1,0:T(8,128)}, f32[12,512,512]{1,2,0:T(8,128)}) fusion(pred[12,512]{1,0:T(8,128)(4,1)S(1)} %copy-done.26, pred[12,512]{1,0:T(8,128)(4,1)S(1)} %get-tuple-element.158, s32[12,512]{1,0:T(8,128)S(1)} %copy-done.11, s32[12,512]{1,0:T(8,128)S(1)} %get-tuple-element.117, pred[12,512]{1,0:T(8,128)(4,1)S(1)} %copy-done.28, ...), kind=kOutput, calls=%fused_computation.14 | convolution fusion | flops 468707328 | bytes 14369280 | tf_op jit(solution)/shard_map/thd,shd->hts/dot_general | solution.py:103
  306.0 1.4 copy.106
  307.4 1.4 copy.109
  308.8 2.3 copy.111
  311.1 2.3 copy.112
  313.5 12.4 %select_reduce_fusion = (f32[12,512]{1,0:T(8,128)S(1)}, f32[12,512,512]{1,2,0:T(8,128)S(1)}) fusion(pred[12,512]{1,0:T(8,128)(4,1)} %get-tuple-element.157, pred[12,512]{1,0:T(8,128)(4,1)S(1)} %get-tuple-element.158, s32[12,512]{1,0:T(8,128)} %get-tuple-element.107, s32[12,512]{1,0:T(8,128)S(1)} %get-tuple-element.117, ...), kind=kOutput, calls=%fused_computation.8 | convolution fusion | flops 468707328 | bytes 14369280 | tf_op jit(solution)/shard_map/thd,shd->hts/dot_general | solution.py:103
  326.1 15.3 %fusion.132 = (f32[12,512]{1,0:T(8,128)S(1)}, bf16[12,512,512]{1,2,0:T(8,128)(2,1)S(1)}) fusion(f32[12,512]{1,0:T(8,128)S(1)} %get-tuple-element.85, f32[12,512,512]{1,2,0:T(8,128)S(1)} %get-tuple-element.181, pred[12,512]{1,0:T(8,128)(4,1)S(1)} %copy-done.31, pred[12,512]{1,0:T(8,128)(4,1)S(1)} %get-tuple-element.158, s32[12,512]{1,0:T(8,128)S(1)} %copy-done.19, ...), kind=kLoop, calls=%fused_computation.288 | loop fusion | flops 75491328 | bytes 19112448 | tf_op jit(solution)/shard_map/reduce_sum | solution.py:113
  341.6 17.0 %fusion.130 = (f32[12,512]{1,0:T(8,128)S(1)}, bf16[12,512,512]{1,2,0:T(8,128)(2,1)S(1)}) fusion(f32[12,512]{1,0:T(8,128)S(1)} %get-tuple-element.87, f32[12,512,512]{1,2,0:T(8,128)} %get-tuple-element.187, pred[12,512]{1,0:T(8,128)(4,1)S(1)} %copy-done.27, pred[12,512]{1,0:T(8,128)(4,1)S(1)} %get-tuple-element.158, s32[12,512]{1,0:T(8,128)S(1)} %copy-done.12, ...), kind=kLoop, calls=%fused_computation.286 | loop fusion | flops 75491328 | bytes 19112448 | tf_op jit(solution)/shard_map/reduce_sum | solution.py:113
  358.6 15.5 %fusion.131 = (f32[12,512]{1,0:T(8,128)S(1)}, bf16[12,512,512]{1,2,0:T(8,128)(2,1)S(1)}) fusion(f32[12,512]{1,0:T(8,128)S(1)} %get-tuple-element.86, f32[12,512,512]{1,2,0:T(8,128)S(1)} %bitcast.243, pred[12,512]{1,0:T(8,128)(4,1)S(1)} %get-tuple-element.160, pred[12,512]{1,0:T(8,128)(4,1)S(1)} %get-tuple-element.158, s32[12,512]{1,0:T(8,128)S(1)} %get-tuple-element.114, ...), kind=kLoop, calls=%fused_computation.287 | loop fusion | flops 75491328 | bytes 19112448 | tf_op jit(solution)/shard_map/reduce_sum | solution.py:113
  374.2 1.2 fusion.16
  375.4 1.2 fusion.14
  377.0 1.3 fusion.30
  378.3 1.2 copy.119
  379.5 112.0 %while.12 = (s32[]{:T(128)}, f32[12,64,128]{2,1,0:T(8,128)S(1)}, s32[]{:T(128)}, bf16[64,12]{1,0:T(8,128)(2,1)}, bf16[64,12,64,128]{3,2,1,0:T(8,128)(2,1)}, /*index=5*/s32[]{:T(128)}, s32[]{:T(128)}, s32[]{:T(128)}) while((s32[]{:T(128)}, f32[12,64,128]{2,1,0:T(8,128)S(1)}, s32[]{:T(128)}, bf16[64,12]{1,0:T(8,128)(2,1)}, ...), condition=%wide.region_13.18_spmd, body=%wide.region_12.17_spmd.sunk | while | flops 294929 | bytes 983287 | solution.py:41
  383.9 1.1 convert_add_fusion.2
  387.5 1.1 convert_add_fusion.2
  391.0 1.1 convert_add_fusion.2
  399.9 1.1 convert_add_fusion.2
  401.7 1.1 convert_add_fusion.2
  419.5 1.1 convert_add_fusion.2
  492.4 11.8 %multiply_reduce_fusion = (f32[512,12]{0,1:T(8,128)S(1)}, f32[512,12,64]{0,2,1:T(8,128)S(1)}) fusion(f32[512,12,64]{0,2,1:T(8,128)S(1)} %bitcast.250, bf16[512,12,64]{0,2,1:T(8,128)(2,1)S(1)} %bitcast.246, f32[12]{0:T(128)S(1)} %copy-done.52, f32[12,64,512]{2,1,0:T(8,128)S(1)} %fusion.44, f32[512,12]{0,1:T(8,128)S(1)} %copy-done.34, ...), kind=kOutput, calls=%fused_computation.55 | convolution fusion | flops 2430855168 | bytes 6914096 | tf_op jit(solution)/shard_map/hts,shp->thp/dot_general | solution.py:165
  504.5 1.2 copy.120
  (293 shorter events, 115.0 us)
Async XLA Ops:
  7.2 32.3 %copy-start = (bf16[512,128]{1,0:T(8,128)(2,1)S(1)}, bf16[512,128]{1,0:T(8,128)(2,1)}, u32[]{:S(2)}) copy-start(bf16[512,128]{1,0:T(8,128)(2,1)} %param.32) | copy-start | bytes 393220
  7.2 17.5 %copy-start.46 = (s32[4,3]{1,0:T(4,128)S(1)}, s32[4,3]{1,0:T(4,128)}, u32[]{:S(2)}) copy-start(s32[4,3]{1,0:T(4,128)} %param.28) | copy-start | bytes 148
  7.2 17.6 %copy-start.47 = (s32[4,3]{1,0:T(4,128)S(1)}, s32[4,3]{1,0:T(4,128)}, u32[]{:S(2)}) copy-start(s32[4,3]{1,0:T(4,128)} %param.27) | copy-start | bytes 148
  7.2 17.6 %copy-start.3 = (bf16[512,768]{1,0:T(8,128)(2,1)S(1)}, bf16[512,768]{1,0:T(8,128)(2,1)}, u32[]{:S(2)}) copy-start(bf16[512,768]{1,0:T(8,128)(2,1)} %param.23) | copy-start | bytes 2359300
  7.2 372.2 %all-gather.4.cloned.1.call-start = ((), (), s32[]{:S(2)}) async-start(), calls=%async_computation | async-start | bytes 12779520 | tf_op jit(solution)/shard_map/all_gather | solution.py:27
  8.9 17.2 %copy-start.53 = (u32[256]{0:T(256)S(1)}, u32[256]{0:T(256)}, u32[]{:S(2)}) copy-start(u32[256]{0:T(256)} %constant.107) | copy-start | bytes 3076
  9.6 18.8 %copy-start.42 = (f32[512]{0:T(512)}, f32[512]{0:T(512)S(1)}, u32[]{:S(2)}) copy-start(f32[512]{0:T(512)S(1)} %convert_element_type.140) | copy-start | bytes 6148
  13.4 28.3 %copy-start.35 = (f32[512,12]{0,1:T(8,128)}, f32[512,12]{0,1:T(8,128)S(1)}, u32[]{:S(2)}) copy-start(f32[512,12]{0,1:T(8,128)S(1)} %multiply_bitcast_fusion) | copy-start | bytes 73732
  16.6 241.3 %collective-permute-start.3 = (bf16[512]{0:T(512)(128)(2,1)}, bf16[512]{0:T(512)(128)(2,1)}, u32[]{:S(2)}, u32[]{:S(2)}) collective-permute-start(bf16[512]{0:T(512)(128)(2,1)} %get-tuple-element.89), channel_id=1, source_target_pairs={{0,8},{8,0},{4,12},{12,4},{16,24},{24,16},{20,28},{28,20},{32,40},... | collective-permute-start | bytes 3080 | tf_op jit(solution)/shard_map/ppermute | solution.py:21
  17.6 239.1 %collective-permute-start = (bf16[512]{0:T(512)(128)(2,1)}, bf16[512]{0:T(512)(128)(2,1)}, u32[]{:S(2)}, u32[]{:S(2)}) collective-permute-start(bf16[512]{0:T(512)(128)(2,1)} %get-tuple-element.89), channel_id=1, source_target_pairs={{0,4},{4,0},{8,12},{12,8},{16,20},{20,16},{24,28},{28,24},{32,36},... | collective-permute-start | bytes 3080 | tf_op jit(solution)/shard_map/ppermute | solution.py:21
  19.0 254.0 %collective-permute-start.4 = (bf16[512,768]{1,0:T(8,128)(2,1)S(1)}, bf16[512,768]{1,0:T(8,128)(2,1)}, u32[]{:S(2)}, u32[]{:S(2)}) collective-permute-start(bf16[512,768]{1,0:T(8,128)(2,1)S(1)} %copy-done.4), channel_id=1, source_target_pairs={{0,8},{8,0},{4,12},{12,4},{16,24},{24,16},{20,28},{28,20},{32,40},... | collective-permute-start | bytes 2359304 | tf_op jit(solution)/shard_map/ppermute | solution.py:21
  20.0 250.4 %collective-permute-start.1 = (bf16[512,768]{1,0:T(8,128)(2,1)S(1)}, bf16[512,768]{1,0:T(8,128)(2,1)}, u32[]{:S(2)}, u32[]{:S(2)}) collective-permute-start(bf16[512,768]{1,0:T(8,128)(2,1)S(1)} %copy-done.4), channel_id=1, source_target_pairs={{0,4},{4,0},{8,12},{12,8},{16,20},{20,16},{24,28},{28,24},{32,36},... | collective-permute-start | bytes 2359304 | tf_op jit(solution)/shard_map/ppermute | solution.py:21
  22.1 253.2 %collective-permute-start.2 = (bf16[512,768]{1,0:T(8,128)(2,1)S(1)}, bf16[512,768]{1,0:T(8,128)(2,1)}, u32[]{:S(2)}, u32[]{:S(2)}) collective-permute-start(bf16[512,768]{1,0:T(8,128)(2,1)S(1)} %copy-done.5), channel_id=1, source_target_pairs={{0,4},{4,0},{8,12},{12,8},{16,20},{20,16},{24,28},{28,24},{32,36},... | collective-permute-start | bytes 2359304 | tf_op jit(solution)/shard_map/ppermute | solution.py:21
  28.3 25.6 %copy-start.40 = (s32[512]{0:T(512)}, s32[512]{0:T(512)S(1)}, u32[]{:S(2)}) copy-start(s32[512]{0:T(512)S(1)} %iota_add_fusion) | copy-start | bytes 6148
  28.4 25.6 %copy-start.37 = (s32[512]{0:T(512)}, s32[512]{0:T(512)S(1)}, u32[]{:S(2)}) copy-start(s32[512]{0:T(512)S(1)} %iota_add_fusion.2) | copy-start | bytes 6148
  72.5 204.6 %copy-start.6 = (bf16[512,768]{0,1:T(8,128)(2,1)S(1)}, bf16[512,768]{0,1:T(8,128)(2,1)}, u32[]{:S(2)}) copy-start(bf16[512,768]{0,1:T(8,128)(2,1)} %copy.101) | copy-start | bytes 2359300
  256.7 50.7 %collective-permute-start.5 = (bf16[512,768]{1,0:T(8,128)(2,1)S(1)}, bf16[512,768]{1,0:T(8,128)(2,1)}, u32[]{:S(2)}, u32[]{:S(2)}) collective-permute-start(bf16[512,768]{1,0:T(8,128)(2,1)S(1)} %copy-done.5), channel_id=1, source_target_pairs={{0,8},{8,0},{4,12},{12,4},{16,24},{24,16},{20,28},{28,20},{32,40},... | collective-permute-start | bytes 2359304 | tf_op jit(solution)/shard_map/ppermute | solution.py:21
  257.9 12.1 %collective-permute-start.6 = (bf16[512]{0:T(512)(128)(2,1)}, bf16[512]{0:T(512)(128)(2,1)S(1)}, u32[]{:S(2)}, u32[]{:S(2)}) collective-permute-start(bf16[512]{0:T(512)(128)(2,1)} %collective-permute-done), channel_id=1, source_target_pairs={{0,8},{8,0},{4,12},{12,4},{16,24},{24,16},{20,28},{28,20},{32,40},... | collective-permute-start | bytes 3080 | tf_op jit(solution)/shard_map/ppermute | solution.py:21
  272.7 36.1 %collective-permute-start.7 = (bf16[512,768]{1,0:T(8,128)(2,1)}, bf16[512,768]{1,0:T(8,128)(2,1)}, u32[]{:S(2)}, u32[]{:S(2)}) collective-permute-start(bf16[512,768]{1,0:T(8,128)(2,1)} %collective-permute-done.1), channel_id=1, source_target_pairs={{0,8},{8,0},{4,12},{12,4},{16,24},{24,16},{20,28},{28,20},{32,40},... | collective-permute-start | bytes 2359304 | tf_op jit(solution)/shard_map/ppermute | solution.py:21
  275.3 35.8 %collective-permute-start.8 = (bf16[512,768]{1,0:T(8,128)(2,1)}, bf16[512,768]{1,0:T(8,128)(2,1)}, u32[]{:S(2)}, u32[]{:S(2)}) collective-permute-start(bf16[512,768]{1,0:T(8,128)(2,1)} %collective-permute-done.2), channel_id=1, source_target_pairs={{0,8},{8,0},{4,12},{12,4},{16,24},{24,16},{20,28},{28,20},{32,40},... | collective-permute-start | bytes 2359304 | tf_op jit(solution)/shard_map/ppermute | solution.py:21
  277.1 15.1 %copy-start.8 = (bf16[512,768]{0,1:T(8,128)(2,1)S(1)}, bf16[512,768]{0,1:T(8,128)(2,1)}, u32[]{:S(2)}) copy-start(bf16[512,768]{0,1:T(8,128)(2,1)} %copy.105) | copy-start | bytes 2359300
  277.1 15.1 %copy-start.11 = (s32[12,512]{1,0:T(8,128)S(1)}, s32[12,512]{1,0:T(8,128)}, u32[]{:S(2)}) copy-start(s32[12,512]{1,0:T(8,128)} %get-tuple-element.108) | copy-start | bytes 73732
  277.1 15.1 %copy-start.13 = (s32[12,512]{1,0:T(8,128)S(1)}, s32[12,512]{1,0:T(8,128)}, u32[]{:S(2)}) copy-start(s32[12,512]{1,0:T(8,128)} %get-tuple-element.109) | copy-start | bytes 73732
  277.1 15.1 %copy-start.15 = (s32[12,512]{1,0:T(8,128)S(1)}, s32[12,512]{1,0:T(8,128)}, u32[]{:S(2)}) copy-start(s32[12,512]{1,0:T(8,128)} %get-tuple-element.110) | copy-start | bytes 73732
  277.1 15.1 %copy-start.24 = (pred[12,512]{1,0:T(8,128)(4,1)S(1)}, pred[12,512]{1,0:T(8,128)(4,1)}, u32[]{:S(2)}) copy-start(pred[12,512]{1,0:T(8,128)(4,1)} %get-tuple-element.162) | copy-start | bytes 18436
  277.1 15.1 %copy-start.26 = (pred[12,512]{1,0:T(8,128)(4,1)S(1)}, pred[12,512]{1,0:T(8,128)(4,1)}, u32[]{:S(2)}) copy-start(pred[12,512]{1,0:T(8,128)(4,1)} %get-tuple-element.163) | copy-start | bytes 18436
  277.1 15.1 %copy-start.28 = (pred[12,512]{1,0:T(8,128)(4,1)S(1)}, pred[12,512]{1,0:T(8,128)(4,1)}, u32[]{:S(2)}) copy-start(pred[12,512]{1,0:T(8,128)(4,1)} %get-tuple-element.164) | copy-start | bytes 18436
  277.1 15.1 %copy-start.38 = (s32[512]{0:T(512)S(1)}, s32[512]{0:T(512)}, u32[]{:S(2)}) copy-start(s32[512]{0:T(512)} %copy-done.37) | copy-start | bytes 6148
  326.0 15.4 %copy-start.12 = (s32[12,512]{1,0:T(8,128)S(1)}, s32[12,512]{1,0:T(8,128)}, u32[]{:S(2)}) copy-start(s32[12,512]{1,0:T(8,128)} %get-tuple-element.108) | copy-start | bytes 73732
  326.0 15.4 %copy-start.14 = (s32[12,512]{1,0:T(8,128)S(1)}, s32[12,512]{1,0:T(8,128)}, u32[]{:S(2)}) copy-start(s32[12,512]{1,0:T(8,128)} %get-tuple-element.109) | copy-start | bytes 73732
  326.0 15.4 %copy-start.16 = (s32[12,512]{1,0:T(8,128)S(1)}, s32[12,512]{1,0:T(8,128)}, u32[]{:S(2)}) copy-start(s32[12,512]{1,0:T(8,128)} %get-tuple-element.110) | copy-start | bytes 73732
  326.0 15.4 %copy-start.25 = (pred[12,512]{1,0:T(8,128)(4,1)S(1)}, pred[12,512]{1,0:T(8,128)(4,1)}, u32[]{:S(2)}) copy-start(pred[12,512]{1,0:T(8,128)(4,1)} %get-tuple-element.162) | copy-start | bytes 18436
  326.0 15.4 %copy-start.27 = (pred[12,512]{1,0:T(8,128)(4,1)S(1)}, pred[12,512]{1,0:T(8,128)(4,1)}, u32[]{:S(2)}) copy-start(pred[12,512]{1,0:T(8,128)(4,1)} %get-tuple-element.163) | copy-start | bytes 18436
  326.1 15.4 %copy-start.29 = (pred[12,512]{1,0:T(8,128)(4,1)S(1)}, pred[12,512]{1,0:T(8,128)(4,1)}, u32[]{:S(2)}) copy-start(pred[12,512]{1,0:T(8,128)(4,1)} %get-tuple-element.164) | copy-start | bytes 18436
  326.1 15.4 %copy-start.39 = (s32[512]{0:T(512)S(1)}, s32[512]{0:T(512)}, u32[]{:S(2)}) copy-start(s32[512]{0:T(512)} %copy-done.37) | copy-start | bytes 6148
  326.1 15.4 %copy-start.50 = (pred[512]{0:T(512)(128)(4,1)S(1)}, pred[512]{0:T(512)(128)(4,1)}, u32[]{:S(2)}) copy-start(pred[512]{0:T(512)(128)(4,1)} %broadcast_compare_fusion.2) | copy-start | bytes 1540
  326.1 32.5 %slice-start = ((s8[12582912]{0:T(1024)(128)(4,1)}), s8[4194304]{0:T(1024)(128)(4,1)S(1)}, s32[]{:S(2)}) async-start(s8[12582912]{0:T(1024)(128)(4,1)} %bitcast.242), calls=%async_computation.1 | async-start | bytes 8388608
  326.1 32.5 %slice-start.1 = ((s8[12582912]{0:T(1024)(128)(4,1)}), s8[4194304]{0:T(1024)(128)(4,1)S(1)}, s32[]{:S(2)}) async-start(s8[12582912]{0:T(1024)(128)(4,1)} %bitcast.242), calls=%async_computation.2 | async-start | bytes 8388608
  341.5 17.0 %slice-start.2 = ((s8[12582912]{0:T(1024)(128)(4,1)}), s8[4194304]{0:T(1024)(128)(4,1)S(1)}, s32[]{:S(2)}) async-start(s8[12582912]{0:T(1024)(128)(4,1)} %bitcast.242), calls=%async_computation.3 | async-start | bytes 8388608
  341.5 17.0 %copy-start.10 = (s32[12,512]{1,0:T(8,128)S(1)}, s32[12,512]{1,0:T(8,128)}, u32[]{:S(2)}) copy-start(s32[12,512]{1,0:T(8,128)} %get-tuple-element.116) | copy-start | bytes 73732
  341.5 17.0 %copy-start.23 = (pred[12,512]{1,0:T(8,128)(4,1)S(1)}, pred[12,512]{1,0:T(8,128)(4,1)}, u32[]{:S(2)}) copy-start(pred[12,512]{1,0:T(8,128)(4,1)} %get-tuple-element.167) | copy-start | bytes 18436
  341.5 17.0 %copy-start.48 = (pred[512]{0:T(512)(128)(4,1)S(1)}, pred[512]{0:T(512)(128)(4,1)}, u32[]{:S(2)}) copy-start(pred[512]{0:T(512)(128)(4,1)} %broadcast_compare_fusion.1) | copy-start | bytes 1540
  358.6 15.6 %copy-start.20 = (f32[12,512]{1,0:T(8,128)S(1)}, f32[12,512]{1,0:T(8,128)}, u32[]{:S(2)}) copy-start(f32[12,512]{1,0:T(8,128)} %get-tuple-element.77) | copy-start | bytes 73732
  379.5 112.9 %copy-start.2 = (f32[512,768]{0,1:T(8,128)S(1)}, f32[512,768]{0,1:T(8,128)}, u32[]{:S(2)}) copy-start(f32[512,768]{0,1:T(8,128)} %copy.118) | copy-start | bytes 4718596
  379.5 112.9 %copy-start.9 = (pred[512,512]{0,1:T(8,128)(4,1)S(1)}, pred[512,512]{0,1:T(8,128)(4,1)}, u32[]{:S(2)}) copy-start(pred[512,512]{0,1:T(8,128)(4,1)} %iota_compare_fusion) | copy-start | bytes 786436
  379.5 112.9 %copy-start.34 = (f32[512,12]{0,1:T(8,128)S(1)}, f32[512,12]{0,1:T(8,128)}, u32[]{:S(2)}) copy-start(f32[512,12]{0,1:T(8,128)} %get-tuple-element.90) | copy-start | bytes 73732
  379.5 112.9 %copy-start.36 = (f32[512,12]{0,1:T(8,128)S(1)}, f32[512,12]{0,1:T(8,128)}, u32[]{:S(2)}) copy-start(f32[512,12]{0,1:T(8,128)} %copy-done.35) | copy-start | bytes 73732
  379.5 112.9 %copy-start.52 = (f32[12]{0:T(128)S(1)}, f32[12]{0:T(128)}, u32[]{:S(2)}) copy-start(f32[12]{0:T(128)} %param.34) | copy-start | bytes 148
  (19 other events, 198.0 us)
Sparse Core Ops, SparseCore 0:
  16.1 178.0 all-gather.3
where the time goes:
time: 521 us; the launch traced here: 513 us
  other arithmetic  193 us (37%)
  blocking collectives  178 us (34%)
  matrix products  76.8 us (15%)
  local copies, waits for them, and re-layouts  26.9 us (5%)
  between operations  16 us (3%)
  starting transfers between devices  11 us (2%)
  waiting for transfers between devices  8.82 us (2%)
    unnamed x1, blocking collectives  178 us
    add x63, other arithmetic, chain_step(): later[0][:, None, None] * earlier[1] + later[1]  66.7 us
    reduce_sum x4, other arithmetic, attend(): row_total = row_total * rescale + jnp.sum(weights, axis=-1)  64 us
    dot_general x4, matrix products, attend(): jnp.einsum('thd,shd->hts', query_heads, key_heads, preferred_element_type...  53.5 us
    convert_element_type x63, other arithmetic, one(): lax.dynamic_index_in_dim(a, step, 0, False).astype(own.dtype)  43.3 us
    ppermute x6, local copies, waits for them, and re-layouts, partner(): return lax.ppermute(block, axis, route)  12 us
    dot_general x1, matrix products, per_device(): jnp.einsum('hts,shp->thp', decays * coupling[None], driven, precision=hig...  11.8 us
    ppermute x9, starting transfers between devices, partner(): return lax.ppermute(block, axis, route)  11 us
  transfers between devices with their start and end apart: 10, of which 1 were waited for; matrix products, arithmetic and copies ran while one was open for 32% of the time, Pallas kernels for 0%

commit v1 on v0

v1 whole, which is shorter than its diff:
```python
import functools
import math

import jax
import jax.numpy as jnp
import numpy as np
from jax import lax
from jax.experimental import pallas as pl
from jax.experimental.pallas import tpu as pltpu
from jax.sharding import PartitionSpec as P

HEAD_DIM = 64
STATE = 128
HEADS_PER_GROUP = 6
SPAN_DEV = 4
ROWS = 512
HALF = 256
PAIRS = 6
HEADS_HERE = 12
QUARTER = 192
PIECE = 208
NEG = -1e30
F32 = jnp.float32
BF16 = jnp.bfloat16

LN2_HI = float(np.float32(jnp.bfloat16(math.log(2.0))))
LN2_LO = float(np.float32(jnp.bfloat16(math.log(2.0) - LN2_HI)))
LN3_HI = float(np.float32(jnp.bfloat16(math.log(3.0))))
LN3_LO = float(np.float32(jnp.bfloat16(math.log(3.0) - LN3_HI)))

VMEM = pl.BlockSpec(memory_space=pltpu.VMEM)
SMEM = pl.BlockSpec(memory_space=pltpu.SMEM)


def iota(shape, dim):
    return lax.broadcasted_iota(jnp.int32, shape, dim)


def dot(a, b):
    return lax.dot_general(a, b, (((1,), (0,)), ((), ())), preferred_element_type=F32)


def dot_t(a, b):
    return lax.dot_general(a, b, (((1,), (1,)), ((), ())), preferred_element_type=F32)


def t_dot(a, b):
    return lax.dot_general(a, b, (((0,), (0,)), ((), ())), preferred_element_type=F32)


def one(mask, kind=F32):
    return jnp.where(mask, 1.0, 0.0).astype(kind)


def residue_of(block):
    return ((block & 1) << 2) | (block & 2) | (block >> 2)


def sorting():
    row = iota((ROWS, ROWS), 0)
    token = 8 * (row & 63) + residue_of(row >> 6)
    return one(iota((ROWS, ROWS), 1) == token, BF16)


def split(x, parts):
    out = []
    for _ in range(parts):
        head = x.astype(BF16)
        out.append(head)
        x = x - head.astype(F32)
    return out


def params(mib=40):
    return pltpu.CompilerParams(vmem_limit_bytes=mib * 1024 * 1024)


def pack_kernel(k_ref, v_ref, valid_ref, out_ref):
    sort = sorting()
    low = (iota((HALF, 2 * HEAD_DIM * PAIRS), 1) & 127) < HEAD_DIM
    for at, ref in ((0, k_ref), (HALF, v_ref)):
        rows = dot(sort, ref[...])
        out_ref[at : at + HALF, :] = jnp.where(low, rows[:HALF], rows[HALF:]).astype(BF16)
    valid = jnp.broadcast_to(valid_ref[...].astype(F32), (16, ROWS)).astype(BF16)
    line = dot_t(valid, sort)
    out_ref[ROWS : ROWS + 16, :] = jnp.concatenate(
        [line, jnp.zeros((16, 2 * HEAD_DIM * PAIRS - ROWS), F32)], axis=1
    ).astype(BF16)


def plan_bias(head, seg_ref, dil_ref, near):
    group = head // HEADS_PER_GROUP
    r1, r2 = dil_ref[group, 1], dil_ref[group, 2]
    w0, w1 = seg_ref[group, 0], seg_ref[group, 1]
    shape = (128, 128)
    key, lane = iota(shape, 0), iota(shape, 1)
    query = lane & 15
    if near is None:
        key_at, query_at = residue_of(key >> 1), residue_of(query >> 1)
    else:
        key_at = residue_of((key >> 1) & 3) + (head & 1)
        query_at = residue_of((query >> 1) & 3) + (head & 1)
    same = (key & 1) == (query & 1)
    key_off, query_off = key_at - head, query_at - head

    def on(stride):
        return (key_off & (stride - 1)) + (query_off & (stride - 1)) == 0

    if near is None:
        count = (
            one(same | (w0 >= ROWS)) + one(on(r1) & (same | (w1 >= ROWS))) + one(on(r2))
        )
    else:
        reach = 2 * ROWS if near else 4 * ROWS
        count = one(on(r1) & (w1 >= reach)) + one(on(r2))
    high = jnp.where(count == 0, NEG, jnp.where(count == 2, LN2_HI, jnp.where(count == 3, LN3_HI, 0.0)))
    low = jnp.where(count == 2, LN2_LO, jnp.where(count == 3, LN3_LO, 0.0))
    value = jnp.where(lane < 16, high, jnp.where(lane < 32, low, 0.0))
    return jnp.where(key < 16, value, 0.0).astype(BF16)


def query_side(rows):
    row, lane = iota((rows, 128), 0), iota((rows, 128), 1)
    return one(((row >> 5) == (lane & 15)) & (lane < 32) | (lane == 32), BF16)


def key_side(rows):
    row, lane = iota((rows, 128), 0), iota((rows, 128), 1)
    return one((row >> 5) == lane, BF16)


def local_kernel(
    q_ref, k_ref, v_ref, valid_ref, seg_ref, dil_ref, rank_ref,
    qe_ref, oe_ref, le_ref, me_ref, oo_ref,
    sort_ref, vbias_ref, vcol_ref,
):
    pair = pl.program_id(0)

    @pl.when(pair == 0)
    def _():
        sort_ref[...] = sorting()
        valid = jnp.broadcast_to(valid_ref[...].astype(F32), (128, ROWS)).astype(BF16)
        column = dot_t(sort_ref[...], valid)
        vcol_ref[...] = column
        vbias_ref[...] = jnp.where(iota((ROWS, 128), 1) == 32, (1.0 - column) * NEG, 0.0)

    sort = sort_ref[...]
    packed = dot(sort, jnp.concatenate([q_ref[...], k_ref[...], v_ref[...]], axis=1))
    query = packed[:, :128] * (HEAD_DIM**-0.5)
    key = packed[:, 128:256].astype(BF16)
    value = jnp.concatenate([packed[:, 256:].astype(BF16), jnp.ones((ROWS, 128), BF16)], axis=1)
    lane = iota((ROWS, 128), 1)
    q_side, k_side = query_side(ROWS), key_side(ROWS)
    results = []
    for part in range(2):
        head = rank_ref[0] * HEADS_HERE + 2 * pair + part
        mine = (lane < HEAD_DIM) if part == 0 else (lane >= HEAD_DIM)
        bias = dot(k_side, plan_bias(head, seg_ref, dil_ref, None))
        mine_query = jnp.where(mine, query, 0.0)
        left = jnp.concatenate([mine_query.astype(BF16), q_side], axis=1)
        right = jnp.concatenate([key, (bias + vbias_ref[...]).astype(BF16)], axis=1)
        own = jnp.sum(
            mine_query * key.astype(F32) + jnp.where(lane == 32, 0.0, q_side.astype(F32) * bias),
            axis=1,
            keepdims=True,
        )
        scores = dot_t(left, right)
        scores = jnp.where(iota((ROWS, ROWS), 0) == iota((ROWS, ROWS), 1), own, scores)
        top = jnp.max(scores, axis=1, keepdims=True)
        weights = jnp.exp(scores - top).astype(BF16)
        results.append((dot(weights, value), top))
    low = lane < HEAD_DIM
    (out0, top0), (out1, top1) = results
    out = jnp.where(low, out0[:, :128], out1[:, :128])
    total = jnp.where(low, out0[:, 128:], out1[:, 128:])
    top = jnp.where(low, top0, top1)
    low = low[:HALF]
    qe_ref[...] = jnp.where(low, query[:HALF], query[HALF:]).astype(BF16)
    oe_ref[...] = jnp.where(low, out[:HALF], out[HALF:])
    le_ref[...] = jnp.where(low, total[:HALF], total[HALF:])
    me_ref[...] = jnp.where(low, top[:HALF], top[HALF:])
    done = out / total * vcol_ref[...]
    oo_ref[...] = jnp.where(low, done[HALF:], done[:HALF]).astype(BF16)


def remote_kernel(
    qe_ref, oe_ref, le_ref, me_ref, oo_ref,
    k1_ref, v1_ref, k2_ref, v2_ref, k3_ref, v3_ref, f1_ref, f2_ref, f3_ref,
    valid_ref, seg_ref, dil_ref, rank_ref,
    out_ref, sort_ref, vcol_ref, vbias_ref,
):
    pair = pl.program_id(0)
    keys = 3 * HALF

    @pl.when(pair == 0)
    def _():
        sort_ref[...] = sorting()
        valid = jnp.broadcast_to(valid_ref[...].astype(F32), (128, ROWS)).astype(BF16)
        vcol_ref[...] = dot_t(sort_ref[...], valid)
        spread = one((iota((16, 128), 0) == 0) & (iota((16, 128), 1) == 32), BF16)
        for at, ref in enumerate((f1_ref, f2_ref, f3_ref)):
            for parity in range(2):
                line = (1.0 - ref[:, parity * HALF : (parity + 1) * HALF].astype(F32)) * NEG
                vbias_ref[parity, at * HALF : (at + 1) * HALF, :] = t_dot(line.astype(BF16), spread)

    key = jnp.concatenate([k1_ref[...], k2_ref[...], k3_ref[...]], axis=0)
    value = jnp.concatenate([v1_ref[...], v2_ref[...], v3_ref[...]], axis=0)
    value = jnp.concatenate([value, jnp.ones((keys, 128), BF16)], axis=1)
    lane = iota((HALF, 128), 1)
    q_side, k_side = query_side(HALF), key_side(HALF)
    results = []
    for part in range(2):
        head = rank_ref[0] * HEADS_HERE + 2 * pair + part
        mine = (lane < HEAD_DIM) if part == 0 else (lane >= HEAD_DIM)
        close = dot(k_side, plan_bias(head, seg_ref, dil_ref, True))
        far = dot(k_side, plan_bias(head, seg_ref, dil_ref, False))
        bias = jnp.concatenate([close, far, far], axis=0) + vbias_ref[part]
        left = jnp.concatenate([jnp.where(mine, qe_ref[...], jnp.zeros((), BF16)), q_side], axis=1)
        right = jnp.concatenate([key, bias.astype(BF16)], axis=1)
        scores = dot_t(left, right)
        before = me_ref[:, part * HEAD_DIM : part * HEAD_DIM + 1]
        top = jnp.maximum(jnp.max(scores, axis=1, keepdims=True), before)
        weights = jnp.exp(scores - top).astype(BF16)
        results.append((dot(weights, value), top))
    low = lane < HEAD_DIM
    (out0, top0), (out1, top1) = results
    rescale = jnp.exp(me_ref[...] - jnp.where(low, top0, top1))
    out = jnp.where(low, out0[:, :128], out1[:, :128]) + oe_ref[...] * rescale
    total = jnp.where(low, out0[:, 128:], out1[:, 128:]) + le_ref[...] * rescale
    valid = jnp.where(low, vcol_ref[:HALF, :], vcol_ref[HALF:, :])
    done = (out / total * valid).astype(BF16)
    other = oo_ref[...]
    rows = jnp.concatenate([jnp.where(low, done, other), jnp.where(low, other, done)], axis=0)
    out_ref[...] = t_dot(sort_ref[...], rows).astype(BF16)


def state_kernel(v_ref, steps_ref, rates_ref, valid_ref, into_ref, place_ref, *out_refs):
    full_ref = out_refs[4]
    later = one(iota((ROWS, ROWS), 0) > iota((ROWS, ROWS), 1), BF16)
    rates = jnp.concatenate([rates_ref[...], jnp.zeros((4, ROWS), F32)], axis=0)
    sums = dot(jnp.concatenate(split(rates, 3), axis=0), later)
    to_end = sums[:16] + sums[16:32] + sums[32:]
    steps = jnp.concatenate([steps_ref[...], jnp.zeros((4, ROWS), F32)], axis=0)
    weight = jnp.exp(-to_end) * steps * valid_ref[...].astype(F32)
    width = HEADS_HERE * HEAD_DIM
    spread = one((iota((32, width), 0) & 15) == (iota((32, width), 1) >> 6), BF16)
    scale = t_dot(jnp.concatenate(split(weight, 2), axis=0), spread)
    driven = (v_ref[...].astype(F32) * scale).astype(BF16)
    full_ref[...] = t_dot(driven, into_ref[...])
    decay = jnp.exp(-jnp.sum(rates, axis=1, keepdims=True))
    decay = jnp.concatenate(split(jnp.broadcast_to(decay, (16, STATE)), 2), axis=0)
    row, source = iota((16, 32), 0), iota((16, 32), 1)
    for step in range(4):
        part = place_ref[0] ^ step
        wanted = jnp.where(row < 3, part * 3 + row, jnp.where(row < 6, 13 + part * 3 + row, -1))
        start = pl.multiple_of(part * QUARTER, 64)
        out_refs[step][:QUARTER, :] = full_ref[pl.ds(start, QUARTER), :].astype(BF16)
        out_refs[step][QUARTER:, :] = dot(one(source == wanted, BF16), decay).astype(BF16)


def decay_rows(ref_value):
    tail = ref_value[QUARTER:].astype(F32)
    return [tail[k : k + 1] + tail[k + 3 : k + 4] for k in range(3)]


def spread_rows(decays):
    return jnp.concatenate([jnp.broadcast_to(d, (HEAD_DIM, STATE)) for d in decays], axis=0)


def pack_piece(state, decays):
    high, low = zip(*(split(d, 2) for d in decays))
    tail = jnp.concatenate(
        [d.astype(F32) for d in high + low] + [jnp.zeros((10, STATE), F32)], axis=0
    )
    return jnp.concatenate([state, tail], axis=0).astype(BF16)


def block_kernel(place_ref, a0, a1, a2, a3, total_ref, before_ref, fade_ref, held):
    for step, ref in enumerate((a0, a1, a2, a3)):
        held[place_ref[0] ^ step] = ref[...].astype(F32)
    state = jnp.zeros((QUARTER, STATE), F32)
    decays = [jnp.ones((1, STATE), F32)] * 3
    for at in range(4):
        before_ref[at] = state
        fade_ref[at] = spread_rows(decays)
        now = decay_rows(held[at])
        state = state * spread_rows(now) + held[at, :QUARTER, :]
        decays = [a * b for a, b in zip(decays, now)]
    total_ref[...] = pack_piece(state, decays)


def chain(place, held):
    state = jnp.zeros((QUARTER, STATE), F32)
    decays = [jnp.ones((1, STATE), F32)] * 3
    before, before_decays = state, decays
    for at in range(4):
        here = place == at
        before = jnp.where(here, state, before)
        before_decays = [jnp.where(here, a, b) for a, b in zip(decays, before_decays)]
        now = decay_rows(held[at])
        state = state * spread_rows(now) + held[at, :QUARTER, :]
        decays = [a * b for a, b in zip(decays, now)]
    return before, before_decays, state, decays


def line_kernel(place_ref, a0, a1, a2, a3, total_ref, before_ref, fade_ref, held):
    for step, ref in enumerate((a0, a1, a2, a3)):
        held[(place_ref[1] - step) & 3] = ref[...].astype(F32)
    before, before_decays, state, decays = chain(place_ref[1], held)
    before_ref[...] = before
    fade_ref[...] = spread_rows(before_decays)
    total_ref[...] = pack_piece(state, decays)


def plane_kernel(place_ref, a0, a1, a2, a3, line_before, line_fade, block_before, block_fade, *rest):
    outs, held = rest[:4], rest[4]
    for step, ref in enumerate((a0, a1, a2, a3)):
        held[(place_ref[2] - step) & 3] = ref[...].astype(F32)
    before = chain(place_ref[2], held)[0]
    start = line_fade[...] * before + line_before[...]
    for step in range(4):
        part = place_ref[0] ^ step
        outs[step][...] = (block_fade[part] * start + block_before[part]).astype(BF16)


def within_kernel(
    v_ref, gate_ref, steps_ref, rates_ref, valid_ref, into_ref, read_ref, skip_ref,
    base_ref, lift_ref, couple_ref, col_ref, row_ref,
):
    pair = pl.program_id(0)

    @pl.when(pair == 0)
    def _():
        couple_ref[...] = dot_t(read_ref[...], into_ref[...])
        upto = one(iota((ROWS, ROWS), 0) <= iota((ROWS, ROWS), 1), BF16)
        rates = jnp.concatenate([rates_ref[...], jnp.zeros((4, ROWS), F32)], axis=0)
        sums = dot(jnp.concatenate(split(rates, 3), axis=0), upto)
        fall = -(sums[:16] + sums[16:32] + sums[32:])
        steps = jnp.concatenate([steps_ref[...], jnp.ones((4, ROWS), F32)], axis=0)
        col_ref[...] = fall
        row_ref[...] = jnp.where(valid_ref[...] > 0, fall - jnp.log(steps), -NEG)

    value = v_ref[...]
    lane = iota((ROWS, 128), 1)
    results = []
    falls = []
    tile = 128
    causal = iota((tile, tile), 0) >= iota((tile, tile), 1)
    for part in range(2):
        head = 2 * pair + part
        fall = jnp.broadcast_to(col_ref[pl.ds(head, 1), :], (128, ROWS)).T
        line = row_ref[pl.ds(head, 1), :]
        pieces = []
        for at in range(ROWS // tile):
            fall_now = fall[at * tile : (at + 1) * tile]
            weights = []
            for src in range(at + 1):
                gap = fall_now - line[:, src * tile : (src + 1) * tile]
                if src == at:
                    gap = jnp.where(causal, gap, NEG)
                weights.append(
                    (
                        jnp.exp(gap)
                        * couple_ref[at * tile : (at + 1) * tile, src * tile : (src + 1) * tile]
                    ).astype(BF16)
                )
            pieces.append(dot(jnp.concatenate(weights, axis=1), value[: (at + 1) * tile]))
        results.append(jnp.concatenate(pieces, axis=0))
        falls.append(fall)
    low = lane < HEAD_DIM
    gate = gate_ref[...].astype(F32)
    gate = gate / (1.0 + jnp.exp(-gate))
    skip = jnp.where(low, skip_ref[2 * pair], skip_ref[2 * pair + 1])
    within = jnp.where(low, results[0], results[1])
    base_ref[...] = (within + skip * value.astype(F32)) * gate
    lift_ref[...] = jnp.exp(jnp.where(low, falls[0], falls[1])) * gate


def finish_kernel(place_ref, f0, f1, f2, f3, read_ref, base_ref, lift_ref, gain_ref, out_ref, held):
    @pl.when(pl.program_id(0) == 0)
    def _():
        for step, ref in enumerate((f0, f1, f2, f3)):
            part = place_ref[0] ^ step
            held[pl.ds(pl.multiple_of(part * QUARTER, 64), QUARTER), :] = ref[...]

    start = pl.multiple_of(pl.program_id(0) * 128, 128)
    carried = dot_t(read_ref[...], held[pl.ds(start, 128), :])
    gated = base_ref[...] + lift_ref[...] * carried
    together = one((iota((128, 128), 0) >> 6) == (iota((128, 128), 1) >> 6), BF16)
    high, low = split(gated * gated, 2)
    mean = (dot(high, together) + dot(low, together)) * (1.0 / HEAD_DIM)
    out_ref[...] = (gated * lax.rsqrt(mean + 1e-05) * gain_ref[...]).astype(BF16)


def per_device(
    query_rows,
    key_rows,
    value_rows,
    patch_valid,
    segment_lengths,
    dilation,
    step_sizes,
    decay_rates,
    state_in,
    state_out,
    gate_in,
    skip_weight,
    norm_gain,
):
    width = HEADS_HERE * HEAD_DIM
    count = lax.axis_size("seq")
    seq_rank = lax.axis_index("seq").astype(jnp.int32)
    rank = jnp.reshape(lax.axis_index("head").astype(jnp.int32), (1,))
    place = jnp.stack([seq_rank & 3, (seq_rank >> 2) & 3, seq_rank >> 4])
    valid = patch_valid.reshape(1, ROWS)
    gain = norm_gain.reshape(1, width)

    def shape(*dims, kind=BF16):
        return jax.ShapeDtypeStruct(dims, kind)

    def cross(block, mask):
        return lax.ppermute(block, "seq", [(i, i ^ mask) for i in range(count)])

    def turn(block, step, span):
        unit, inner = span // 4, span
        route = [(i, i // inner * inner + (i % inner + step * unit) % inner) for i in range(count)]
        return lax.ppermute(block, "seq", route)

    packed = pl.pallas_call(
        pack_kernel,
        out_shape=shape(ROWS + 16, width),
        in_specs=[VMEM] * 3,
        out_specs=VMEM,
        compiler_params=params(),
        name="pack",
    )(key_rows, value_rows, valid)
    arrived = [cross(packed, mask) for mask in range(1, SPAN_DEV)]

    pieces = pl.pallas_call(
        state_kernel,
        out_shape=[shape(PIECE, STATE)] * 4,
        in_specs=[VMEM] * 5 + [SMEM],
        out_specs=[VMEM] * 4,
        scratch_shapes=[pltpu.VMEM((width, STATE), F32)],
        compiler_params=params(),
        name="state",
    )(value_rows, step_sizes, decay_rates, valid, state_in, place)
    pieces = [pieces[0]] + [cross(pieces[mask], mask) for mask in range(1, SPAN_DEV)]
    hold = [pltpu.VMEM((4, PIECE, STATE), F32)]
    total, block_before, block_fade = pl.pallas_call(
        block_kernel,
        out_shape=[shape(PIECE, STATE), shape(4, QUARTER, STATE, kind=F32), shape(4, QUARTER, STATE, kind=F32)],
        in_specs=[SMEM] + [VMEM] * 4,
        out_specs=[VMEM] * 3,
        scratch_shapes=hold,
        compiler_params=params(),
        name="block",
    )(place, *pieces)
    totals = [total] + [turn(total, step, 16) for step in range(1, 4)]
    total, line_before, line_fade = pl.pallas_call(
        line_kernel,
        out_shape=[shape(PIECE, STATE), shape(QUARTER, STATE, kind=F32), shape(QUARTER, STATE, kind=F32)],
        in_specs=[SMEM] + [VMEM] * 4,
        out_specs=[VMEM] * 3,
        scratch_shapes=hold,
        compiler_params=params(),
        name="line",
    )(place, *totals)
    totals = [total] + [turn(total, step, 64) for step in range(1, 4)]
    carried = pl.pallas_call(
        plane_kernel,
        out_shape=[shape(QUARTER, STATE)] * 4,
        in_specs=[SMEM] + [VMEM] * 8,
        out_specs=[VMEM] * 4,
        scratch_shapes=hold,
        compiler_params=params(),
        name="plane",
    )(place, *totals, line_before, line_fade, block_before, block_fade)
    carried = [carried[0]] + [cross(carried[mask], mask) for mask in range(1, SPAN_DEV)]

    def lanes(rows, row_block=0):
        return pl.BlockSpec((rows, 128), lambda pair: (row_block, pair))

    def whole(*dims):
        return pl.BlockSpec(dims, lambda pair: (0,) * len(dims))

    kept = pl.pallas_call(
        local_kernel,
        grid=(PAIRS,),
        out_shape=[shape(HALF, width)] + [shape(HALF, width, kind=F32)] * 3 + [shape(HALF, width)],
        in_specs=[lanes(ROWS)] * 3 + [whole(1, ROWS), SMEM, SMEM, SMEM],
        out_specs=[lanes(HALF)] * 5,
        scratch_shapes=[pltpu.VMEM((ROWS, ROWS), BF16), pltpu.VMEM((ROWS, 128), F32), pltpu.VMEM((ROWS, 128), F32)],
        compiler_params=params(),
        name="local",
    )(query_rows, key_rows, value_rows, valid, segment_lengths, dilation, rank)

    base, lift = pl.pallas_call(
        within_kernel,
        grid=(PAIRS,),
        out_shape=[shape(ROWS, width, kind=F32)] * 2,
        in_specs=[lanes(ROWS)] * 2
        + [whole(HEADS_HERE, ROWS)] * 2
        + [whole(1, ROWS), whole(ROWS, STATE), whole(ROWS, STATE), SMEM],
        out_specs=[lanes(ROWS)] * 2,
        scratch_shapes=[pltpu.VMEM((ROWS, ROWS), F32), pltpu.VMEM((16, ROWS), F32), pltpu.VMEM((16, ROWS), F32)],
        compiler_params=params(),
        name="within",
    )(value_rows, gate_in, step_sizes, decay_rates, valid, state_in, state_out, skip_weight)

    scanned = pl.pallas_call(
        finish_kernel,
        grid=(PAIRS,),
        out_shape=shape(ROWS, width),
        in_specs=[SMEM]
        + [whole(QUARTER, STATE)] * 4
        + [whole(ROWS, STATE), lanes(ROWS), lanes(ROWS), lanes(1)],
        out_specs=lanes(ROWS),
        scratch_shapes=[pltpu.VMEM((width, STATE), BF16)],
        compiler_params=params(),
        name="finish",
    )(place, *carried, state_out, base, lift, gain)

    flags = pl.BlockSpec((16, width), lambda pair: (ROWS // 16, 0))
    attended = pl.pallas_call(
        remote_kernel,
        grid=(PAIRS,),
        out_shape=shape(ROWS, width),
        in_specs=[lanes(HALF)] * 5
        + [lanes(HALF), lanes(HALF, 1)] * 3
        + [flags] * 3
        + [whole(1, ROWS), SMEM, SMEM, SMEM],
        out_specs=lanes(ROWS),
        scratch_shapes=[
            pltpu.VMEM((ROWS, ROWS), BF16),
            pltpu.VMEM((ROWS, 128), F32),
            pltpu.VMEM((2, 3 * HALF, 128), F32),
        ],
        compiler_params=params(),
        name="remote",
    )(
        *kept,
        *[block for block in arrived for _ in range(2)],
        *arrived,
        valid,
        segment_lengths,
        dilation,
        rank,
    )
    return (attended, scanned)


def solution(mesh):
    return jax.shard_map(
        per_device,
        mesh=mesh,
        in_specs=(
            P(("slide", "seq"), "head"),
            P(("slide", "seq"), "head"),
            P(("slide", "seq"), "head"),
            P(("slide", "seq")),
            P(),
            P(),
            P("head", ("slide", "seq")),
            P("head", ("slide", "seq")),
            P(("slide", "seq"), None),
            P(("slide", "seq"), None),
            P(("slide", "seq"), "head"),
            P("head"),
            P("head"),
        ),
        out_specs=(P(("slide", "seq"), "head"), P(("slide", "seq"), "head")),
        check_vma=False,
    )
```

time: 521 us -> 127 us (0.24)
  the two profiles are of different devices: /device:TPU:254 before, /device:TPU:88 now
where the time goes in v1:
time: 127 us
  Pallas kernels  43 us (34%)
  starting transfers between devices  37.6 us (30%)
  waiting for transfers between devices  37 us (29%)
  local copies, waits for them, and re-layouts  8.11 us (6%)
    ppermute x9, waiting for transfers between devices, cross(): return lax.ppermute(block, 'seq', [(i, i ^ mask) for i in range(count)])  26.2 us
    ppermute x9, starting transfers between devices, cross(): return lax.ppermute(block, 'seq', [(i, i ^ mask) for i in range(count)])  26.1 us
    pallas_call x1, Pallas kernels, per_device(): pl.pallas_call(remote_kernel, grid=(PAIRS,), out_shape=shape(ROWS, width)...  14.5 us
    pallas_call x1, Pallas kernels, per_device(): pl.pallas_call(local_kernel, grid=(PAIRS,), out_shape=[shape(HALF, width)...  13.2 us
    ppermute x6, starting transfers between devices, turn(): return lax.ppermute(block, 'seq', route)  11.6 us
    ppermute x6, waiting for transfers between devices, turn(): return lax.ppermute(block, 'seq', route)  10.9 us
    unnamed x38, local copies, waits for them, and re-layouts  7.35 us
    pallas_call x1, Pallas kernels, per_device(): pl.pallas_call(finish_kernel, grid=(PAIRS,), out_shape=shape(ROWS, width)...  4.73 us
  transfers between devices with their start and end apart: 15, of which 9 were waited for; matrix products, arithmetic and copies ran while one was open for 1% of the time, Pallas kernels for 21%

profile of v1, /device:TPU:88, one launch (start us, length us, event | category | flops | bytes accessed | tf_op | source)
XLA Modules:
  0.0 126.7 jit_solution(7865274698902986364)
XLA Ops:
  0.6 1.1 copy-done
  1.8 1.1 copy-done.2
  2.9 0.7 copy-done.10
  3.6 2.0 %pack.1 = bf16[528,768]{1,0:T(8,128)(2,1)} custom-call(bf16[512,768]{1,0:T(8,128)(2,1)S(1)} %copy-done.2, bf16[512,768]{1,0:T(8,128)(2,1)S(1)} %copy-done, s32[1,512]{1,0:T(1,128)S(1)} %bitcast.5), custom_call_target="tpu_custom_call" | custom-call | tf_op jit(solution)/shard_map/pack/pallas_call | solution.py:429
  5.6 3.0 %collective-permute-start = (bf16[528,768]{1,0:T(8,128)(2,1)}, bf16[528,768]{1,0:T(8,128)(2,1)S(1)}, u32[]{:S(2)}, u32[]{:S(2)}) collective-permute-start(bf16[528,768]{1,0:T(8,128)(2,1)} %pack.1), channel_id=1, source_target_pairs={{0,4},{4,0},{8,12},{12,8},{16,20},{20,16},{24,28},{28,24},{32,36},... | collective-permute-start | bytes 2433032 | tf_op jit(solution)/shard_map/ppermute | solution.py:422
  8.6 1.9 %collective-permute-start.1 = (bf16[528,768]{1,0:T(8,128)(2,1)}, bf16[528,768]{1,0:T(8,128)(2,1)S(1)}, u32[]{:S(2)}, u32[]{:S(2)}) collective-permute-start(bf16[528,768]{1,0:T(8,128)(2,1)} %pack.1), channel_id=1, source_target_pairs={{0,8},{4,12},{8,0},{12,4},{16,24},{20,28},{24,16},{28,20},{32,40},... | collective-permute-start | bytes 2433032 | tf_op jit(solution)/shard_map/ppermute | solution.py:422
  10.5 0.1 collective-permute-start.2
  10.6 0.1 pad_add_fusion.place_ref
  10.7 1.5 %state.1 = (bf16[208,128]{1,0:T(8,128)(2,1)S(1)}, bf16[208,128]{1,0:T(8,128)(2,1)S(1)}, bf16[208,128]{1,0:T(8,128)(2,1)S(1)}, bf16[208,128]{1,0:T(8,128)(2,1)S(1)}) custom-call(bf16[512,768]{1,0:T(8,128)(2,1)S(1)} %copy-done.1, f32[12,512]{1,0:T(8,128)S(1)} %copy-done.8, f32[12,512]{1,0:T(8,128)S(1)} %copy-done.9, s32[1,512]{1,0:T(1,128)S(1)} %bitcast.6, ...), custom_call_target="tpu_custom_call" | custom-call | tf_op jit(solution)/shard_map/state/pallas_call | solution.py:439
  12.2 3.1 %collective-permute-start.3 = (bf16[208,128]{1,0:T(8,128)(2,1)S(1)}, bf16[208,128]{1,0:T(8,128)(2,1)S(1)}, u32[]{:S(2)}, u32[]{:S(2)}) collective-permute-start(bf16[208,128]{1,0:T(8,128)(2,1)S(1)} %get-tuple-element.29), channel_id=1, source_target_pairs={{0,4},{4,0},{8,12},{12,8},{16,20},{20,16},{24,28},{28,24},{32,36},... | collective-permute-start | bytes 159752 | tf_op jit(solution)/shard_map/ppermute | solution.py:422
  15.3 1.9 %collective-permute-start.4 = (bf16[208,128]{1,0:T(8,128)(2,1)S(1)}, bf16[208,128]{1,0:T(8,128)(2,1)S(1)}, u32[]{:S(2)}, u32[]{:S(2)}) collective-permute-start(bf16[208,128]{1,0:T(8,128)(2,1)S(1)} %get-tuple-element.30), channel_id=1, source_target_pairs={{0,8},{4,12},{8,0},{12,4},{16,24},{20,28},{24,16},{28,20},{32,40},... | collective-permute-start | bytes 159752 | tf_op jit(solution)/shard_map/ppermute | solution.py:422
  17.2 12.0 %collective-permute-done.3.a1 = bf16[208,128]{1,0:T(8,128)(2,1)S(1)} collective-permute-done((bf16[208,128]{1,0:T(8,128)(2,1)S(1)}, bf16[208,128]{1,0:T(8,128)(2,1)S(1)}, u32[]{:S(2)}, u32[]{:S(2)}) %collective-permute-start.3) | collective-permute-done | bytes 53280 | tf_op jit(solution)/shard_map/ppermute | solution.py:422
  29.2 4.8 %collective-permute-start.5 = (bf16[208,128]{1,0:T(8,128)(2,1)S(1)}, bf16[208,128]{1,0:T(8,128)(2,1)S(1)}, u32[]{:S(2)}, u32[]{:S(2)}) collective-permute-start(bf16[208,128]{1,0:T(8,128)(2,1)S(1)} %get-tuple-element.31), channel_id=1, source_target_pairs={{0,12},{4,8},{8,4},{12,0},{16,28},{20,24},{24,20},{28,16},{32,44},... | collective-permute-start | bytes 159752 | tf_op jit(solution)/shard_map/ppermute | solution.py:422
  34.0 13.6 %collective-permute-done.4.a2 = bf16[208,128]{1,0:T(8,128)(2,1)S(1)} collective-permute-done((bf16[208,128]{1,0:T(8,128)(2,1)S(1)}, bf16[208,128]{1,0:T(8,128)(2,1)S(1)}, u32[]{:S(2)}, u32[]{:S(2)}) %collective-permute-start.4) | collective-permute-done | bytes 53280 | tf_op jit(solution)/shard_map/ppermute | solution.py:422
  47.6 0.5 collective-permute-done.5.a3
  48.1 0.6 block.1
  48.8 4.4 %collective-permute-start.6 = (bf16[208,128]{1,0:T(8,128)(2,1)S(1)}, bf16[208,128]{1,0:T(8,128)(2,1)S(1)}, u32[]{:S(2)}, u32[]{:S(2)}) collective-permute-start(bf16[208,128]{1,0:T(8,128)(2,1)S(1)} %get-tuple-element.32.a0), channel_id=1, source_target_pairs={{0,16},{4,20},{8,24},{12,28},{16,32},{20,36},{24,40},{28,44},{32,4... | collective-permute-start | bytes 159752 | tf_op jit(solution)/shard_map/ppermute | solution.py:427
  53.1 1.0 collective-permute-start.7
  54.1 0.8 collective-permute-done.6.a1
  54.9 2.0 %collective-permute-start.8 = (bf16[208,128]{1,0:T(8,128)(2,1)S(1)}, bf16[208,128]{1,0:T(8,128)(2,1)S(1)}, u32[]{:S(2)}, u32[]{:S(2)}) collective-permute-start(bf16[208,128]{1,0:T(8,128)(2,1)S(1)} %get-tuple-element.32.a0), channel_id=1, source_target_pairs={{0,48},{4,52},{8,56},{12,60},{16,0},{20,4},{24,8},{28,12},{32,16},... | collective-permute-start | bytes 159752 | tf_op jit(solution)/shard_map/ppermute | solution.py:427
  57.0 4.2 %collective-permute-done.7.a2 = bf16[208,128]{1,0:T(8,128)(2,1)S(1)} collective-permute-done((bf16[208,128]{1,0:T(8,128)(2,1)S(1)}, bf16[208,128]{1,0:T(8,128)(2,1)S(1)}, u32[]{:S(2)}, u32[]{:S(2)}) %collective-permute-start.7) | collective-permute-done | bytes 53280 | tf_op jit(solution)/shard_map/ppermute | solution.py:427
  61.2 0.5 collective-permute-done.8.a3
  61.7 0.6 line.1
  62.3 0.3 collective-permute-start.9
  62.6 2.6 %collective-permute-start.10 = (bf16[208,128]{1,0:T(8,128)(2,1)S(1)}, bf16[208,128]{1,0:T(8,128)(2,1)S(1)}, u32[]{:S(2)}, u32[]{:S(2)}) collective-permute-start(bf16[208,128]{1,0:T(8,128)(2,1)S(1)} %get-tuple-element.33.a0), channel_id=1, source_target_pairs={{0,128},{4,132},{8,136},{12,140},{16,144},{20,148},{24,152},{28,15... | collective-permute-start | bytes 159752 | tf_op jit(solution)/shard_map/ppermute | solution.py:427
  65.2 1.3 %collective-permute-done.9.a1 = bf16[208,128]{1,0:T(8,128)(2,1)S(1)} collective-permute-done((bf16[208,128]{1,0:T(8,128)(2,1)S(1)}, bf16[208,128]{1,0:T(8,128)(2,1)S(1)}, u32[]{:S(2)}, u32[]{:S(2)}) %collective-permute-start.9) | collective-permute-done | bytes 53280 | tf_op jit(solution)/shard_map/ppermute | solution.py:427
  66.5 1.3 collective-permute-start.11
  67.8 0.7 collective-permute-done.10.a2
  68.4 3.4 %collective-permute-done.11.a3 = bf16[208,128]{1,0:T(8,128)(2,1)S(1)} collective-permute-done((bf16[208,128]{1,0:T(8,128)(2,1)S(1)}, bf16[208,128]{1,0:T(8,128)(2,1)S(1)}, u32[]{:S(2)}, u32[]{:S(2)}) %collective-permute-start.11) | collective-permute-done | bytes 53280 | tf_op jit(solution)/shard_map/ppermute | solution.py:427
  71.9 1.3 %plane.1 = (bf16[192,128]{1,0:T(8,128)(2,1)S(1)}, bf16[192,128]{1,0:T(8,128)(2,1)S(1)}, bf16[192,128]{1,0:T(8,128)(2,1)}, bf16[192,128]{1,0:T(8,128)(2,1)}) custom-call(s32[3]{0:T(128)S(1)} %pad_add_fusion.place_ref, bf16[208,128]{1,0:T(8,128)(2,1)S(1)} %get-tuple-element.33.a0, bf16[208,128]{1,0:T(8,128)(2,1)S(1)} %collective-permute-done.9.a1, ...), custom_call_target="tpu_custom_call" | custom-call | tf_op jit(solution)/shard_map/plane/pallas_call | solution.py:470
  73.2 0.6 copy-done.12
  73.8 3.0 %collective-permute-start.12 = (bf16[192,128]{1,0:T(8,128)(2,1)S(1)}, bf16[192,128]{1,0:T(8,128)(2,1)S(1)}, u32[]{:S(2)}, u32[]{:S(2)}) collective-permute-start(bf16[192,128]{1,0:T(8,128)(2,1)S(1)} %get-tuple-element.39), channel_id=1, source_target_pairs={{0,4},{4,0},{8,12},{12,8},{16,20},{20,16},{24,28},{28,24},{32,36},... | collective-permute-start | bytes 147464 | tf_op jit(solution)/shard_map/ppermute | solution.py:422
  76.8 3.2 %collective-permute-start.13 = (bf16[192,128]{1,0:T(8,128)(2,1)}, bf16[192,128]{1,0:T(8,128)(2,1)}, u32[]{:S(2)}, u32[]{:S(2)}) collective-permute-start(bf16[192,128]{1,0:T(8,128)(2,1)} %get-tuple-element.40), channel_id=1, source_target_pairs={{0,8},{4,12},{8,0},{12,4},{16,24},{20,28},{24,16},{28,20},{32,40},... | collective-permute-start | bytes 147464 | tf_op jit(solution)/shard_map/ppermute | solution.py:422
  80.0 0.0 collective-permute-done.12.f1
  80.0 0.6 copy-done.14
  80.6 5.0 %collective-permute-start.14 = (bf16[192,128]{1,0:T(8,128)(2,1)}, bf16[192,128]{1,0:T(8,128)(2,1)}, u32[]{:S(2)}, u32[]{:S(2)}) collective-permute-start(bf16[192,128]{1,0:T(8,128)(2,1)} %get-tuple-element.41), channel_id=1, source_target_pairs={{0,12},{4,8},{8,4},{12,0},{16,28},{20,24},{24,20},{28,16},{32,44},... | collective-permute-start | bytes 147464 | tf_op jit(solution)/shard_map/ppermute | solution.py:422
  85.6 0.8 reshape.15.gain_ref
  86.4 1.1 copy-done.4
  87.5 0.7 copy-done.18
  88.2 4.6 %within.1 = (f32[512,768]{1,0:T(8,128)S(1)}, f32[512,768]{1,0:T(8,128)S(1)}) custom-call(bf16[512,768]{1,0:T(8,128)(2,1)S(1)} %copy-done.1, bf16[512,768]{1,0:T(8,128)(2,1)S(1)} %copy-done.4, f32[12,512]{1,0:T(8,128)S(1)} %copy-done.8, f32[12,512]{1,0:T(8,128)S(1)} %copy-done.9, s32[1,512]{1,0:T(1,128)S(1)} %bitcast.7, bf16[512,128]{1,0:T(8,128)(2,1)S(1)} %copy-done.6, ...), custom_call_target="tpu_custom_call" | custom-call | tf_op jit(solution)/shard_map/within/pallas_call | solution.py:498
  92.8 0.0 copy-start.16
  92.8 0.7 copy-done.16
  93.5 0.7 copy-done.17
  94.2 13.2 %local.1 = (bf16[256,768]{1,0:T(8,128)(2,1)S(1)}, f32[256,768]{1,0:T(8,128)S(1)}, f32[256,768]{1,0:T(8,128)S(1)}, f32[256,768]{1,0:T(8,128)S(1)}, bf16[256,768]{1,0:T(8,128)(2,1)S(1)}) custom-call(bf16[512,768]{1,0:T(8,128)(2,1)S(1)} %copy-done.5, bf16[512,768]{1,0:T(8,128)(2,1)S(1)} %copy-done.3, bf16[512,768]{1,0:T(8,128)(2,1)S(1)} %copy-done.1, ...), custom_call_target="tpu_custom_call" | custom-call | tf_op jit(solution)/shard_map/local/pallas_call | solution.py:487
  107.5 4.7 %finish.1 = bf16[512,768]{1,0:T(8,128)(2,1)} custom-call(s32[3]{0:T(128)S(1)} %pad_add_fusion.place_ref, bf16[192,128]{1,0:T(8,128)(2,1)S(1)} %copy-done.13, bf16[192,128]{1,0:T(8,128)(2,1)S(1)} %copy-done.15, bf16[192,128]{1,0:T(8,128)(2,1)} %collective-permute-done.13.f2, bf16[192,128]{1,0:T(8,128)(2,1)} %collective-permute-done.14.f3, ...), custom_call_target="tpu_custom_call" | custom-call | tf_op jit(solution)/shard_map/finish/pallas_call | solution.py:511
  112.2 0.0 collective-permute-done.k1_ref.v1_ref.f1_ref
  112.2 0.0 collective-permute-done.2.k3_ref.v3_ref.f3_ref
  112.2 14.5 %remote.1 = bf16[512,768]{1,0:T(8,128)(2,1)} custom-call(bf16[256,768]{1,0:T(8,128)(2,1)S(1)} %get-tuple-element.23.qe_ref, f32[256,768]{1,0:T(8,128)S(1)} %get-tuple-element.24.oe_ref, f32[256,768]{1,0:T(8,128)S(1)} %get-tuple-element.25.le_ref, f32[256,768]{1,0:T(8,128)S(1)} %get-tuple-element.26.me_ref, bf16[256,768]{1,0:T(8,128)(2,1)S(1)} %get-tuple-element.27.oo_ref, ...), custom_call_target="tpu_custom_call" | custom-call | tf_op jit(solution)/shard_map/remote/pallas_call | solution.py:525
  (31 shorter events, 0.1 us)
Async XLA Ops:
  0.6 1.1 copy-start
  1.8 1.1 copy-start.2
  2.9 0.7 copy-start.10
  3.6 7.1 %copy-start.1 = (bf16[512,768]{1,0:T(8,128)(2,1)S(1)}, bf16[512,768]{1,0:T(8,128)(2,1)}, u32[]{:S(2)}) copy-start(bf16[512,768]{1,0:T(8,128)(2,1)} %v_ref.7) | copy-start | bytes 2359300
  3.6 7.1 %copy-start.6 = (bf16[512,128]{1,0:T(8,128)(2,1)S(1)}, bf16[512,128]{1,0:T(8,128)(2,1)}, u32[]{:S(2)}) copy-start(bf16[512,128]{1,0:T(8,128)(2,1)} %into_ref.3) | copy-start | bytes 393220
  3.6 7.1 %copy-start.8 = (f32[12,512]{1,0:T(8,128)S(1)}, f32[12,512]{1,0:T(8,128)}, u32[]{:S(2)}) copy-start(f32[12,512]{1,0:T(8,128)} %steps_ref.3) | copy-start | bytes 73732
  3.6 7.1 %copy-start.9 = (f32[12,512]{1,0:T(8,128)S(1)}, f32[12,512]{1,0:T(8,128)}, u32[]{:S(2)}) copy-start(f32[12,512]{1,0:T(8,128)} %rates_ref.3) | copy-start | bytes 73732
  3.6 7.1 %copy-start.11 = (s32[512]{0:T(512)S(1)}, s32[512]{0:T(512)}, u32[]{:S(2)}) copy-start(s32[512]{0:T(512)} %param.16) | copy-start | bytes 6148
  5.6 80.8 %copy-start.7 = (bf16[512,128]{1,0:T(8,128)(2,1)S(1)}, bf16[512,128]{1,0:T(8,128)(2,1)}, u32[]{:S(2)}) copy-start(bf16[512,128]{1,0:T(8,128)(2,1)} %read_ref.3) | copy-start | bytes 393220
  5.6 106.6 %collective-permute-start = (bf16[528,768]{1,0:T(8,128)(2,1)}, bf16[528,768]{1,0:T(8,128)(2,1)S(1)}, u32[]{:S(2)}, u32[]{:S(2)}) collective-permute-start(bf16[528,768]{1,0:T(8,128)(2,1)} %pack.1), channel_id=1, source_target_pairs={{0,4},{4,0},{8,12},{12,8},{16,20},{20,16},{24,28},{28,24},{32,36},... | collective-permute-start | bytes 2433032 | tf_op jit(solution)/shard_map/ppermute | solution.py:422
  8.6 103.6 %collective-permute-start.1 = (bf16[528,768]{1,0:T(8,128)(2,1)}, bf16[528,768]{1,0:T(8,128)(2,1)S(1)}, u32[]{:S(2)}, u32[]{:S(2)}) collective-permute-start(bf16[528,768]{1,0:T(8,128)(2,1)} %pack.1), channel_id=1, source_target_pairs={{0,8},{4,12},{8,0},{12,4},{16,24},{20,28},{24,16},{28,20},{32,40},... | collective-permute-start | bytes 2433032 | tf_op jit(solution)/shard_map/ppermute | solution.py:422
  10.5 101.7 %collective-permute-start.2 = (bf16[528,768]{1,0:T(8,128)(2,1)}, bf16[528,768]{1,0:T(8,128)(2,1)S(1)}, u32[]{:S(2)}, u32[]{:S(2)}) collective-permute-start(bf16[528,768]{1,0:T(8,128)(2,1)} %pack.1), channel_id=1, source_target_pairs={{0,12},{4,8},{8,4},{12,0},{16,28},{20,24},{24,20},{28,16},{32,44},... | collective-permute-start | bytes 2433032 | tf_op jit(solution)/shard_map/ppermute | solution.py:422
  12.2 17.1 %collective-permute-start.3 = (bf16[208,128]{1,0:T(8,128)(2,1)S(1)}, bf16[208,128]{1,0:T(8,128)(2,1)S(1)}, u32[]{:S(2)}, u32[]{:S(2)}) collective-permute-start(bf16[208,128]{1,0:T(8,128)(2,1)S(1)} %get-tuple-element.29), channel_id=1, source_target_pairs={{0,4},{4,0},{8,12},{12,8},{16,20},{20,16},{24,28},{28,24},{32,36},... | collective-permute-start | bytes 159752 | tf_op jit(solution)/shard_map/ppermute | solution.py:422
  15.3 32.4 %collective-permute-start.4 = (bf16[208,128]{1,0:T(8,128)(2,1)S(1)}, bf16[208,128]{1,0:T(8,128)(2,1)S(1)}, u32[]{:S(2)}, u32[]{:S(2)}) collective-permute-start(bf16[208,128]{1,0:T(8,128)(2,1)S(1)} %get-tuple-element.30), channel_id=1, source_target_pairs={{0,8},{4,12},{8,0},{12,4},{16,24},{20,28},{24,16},{28,20},{32,40},... | collective-permute-start | bytes 159752 | tf_op jit(solution)/shard_map/ppermute | solution.py:422
  29.2 18.9 %collective-permute-start.5 = (bf16[208,128]{1,0:T(8,128)(2,1)S(1)}, bf16[208,128]{1,0:T(8,128)(2,1)S(1)}, u32[]{:S(2)}, u32[]{:S(2)}) collective-permute-start(bf16[208,128]{1,0:T(8,128)(2,1)S(1)} %get-tuple-element.31), channel_id=1, source_target_pairs={{0,12},{4,8},{8,4},{12,0},{16,28},{20,24},{24,20},{28,16},{32,44},... | collective-permute-start | bytes 159752 | tf_op jit(solution)/shard_map/ppermute | solution.py:422
  48.8 6.1 %collective-permute-start.6 = (bf16[208,128]{1,0:T(8,128)(2,1)S(1)}, bf16[208,128]{1,0:T(8,128)(2,1)S(1)}, u32[]{:S(2)}, u32[]{:S(2)}) collective-permute-start(bf16[208,128]{1,0:T(8,128)(2,1)S(1)} %get-tuple-element.32.a0), channel_id=1, source_target_pairs={{0,16},{4,20},{8,24},{12,28},{16,32},{20,36},{24,40},{28,44},{32,4... | collective-permute-start | bytes 159752 | tf_op jit(solution)/shard_map/ppermute | solution.py:427
  53.1 8.0 %collective-permute-start.7 = (bf16[208,128]{1,0:T(8,128)(2,1)S(1)}, bf16[208,128]{1,0:T(8,128)(2,1)S(1)}, u32[]{:S(2)}, u32[]{:S(2)}) collective-permute-start(bf16[208,128]{1,0:T(8,128)(2,1)S(1)} %get-tuple-element.32.a0), channel_id=1, source_target_pairs={{0,32},{4,36},{8,40},{12,44},{16,48},{20,52},{24,56},{28,60},{32,0... | collective-permute-start | bytes 159752 | tf_op jit(solution)/shard_map/ppermute | solution.py:427
  54.9 6.7 %collective-permute-start.8 = (bf16[208,128]{1,0:T(8,128)(2,1)S(1)}, bf16[208,128]{1,0:T(8,128)(2,1)S(1)}, u32[]{:S(2)}, u32[]{:S(2)}) collective-permute-start(bf16[208,128]{1,0:T(8,128)(2,1)S(1)} %get-tuple-element.32.a0), channel_id=1, source_target_pairs={{0,48},{4,52},{8,56},{12,60},{16,0},{20,4},{24,8},{28,12},{32,16},... | collective-permute-start | bytes 159752 | tf_op jit(solution)/shard_map/ppermute | solution.py:427
  62.3 4.2 %collective-permute-start.9 = (bf16[208,128]{1,0:T(8,128)(2,1)S(1)}, bf16[208,128]{1,0:T(8,128)(2,1)S(1)}, u32[]{:S(2)}, u32[]{:S(2)}) collective-permute-start(bf16[208,128]{1,0:T(8,128)(2,1)S(1)} %get-tuple-element.33.a0), channel_id=1, source_target_pairs={{0,64},{4,68},{8,72},{12,76},{16,80},{20,84},{24,88},{28,92},{32,9... | collective-permute-start | bytes 159752 | tf_op jit(solution)/shard_map/ppermute | solution.py:427
  62.6 5.8 %collective-permute-start.10 = (bf16[208,128]{1,0:T(8,128)(2,1)S(1)}, bf16[208,128]{1,0:T(8,128)(2,1)S(1)}, u32[]{:S(2)}, u32[]{:S(2)}) collective-permute-start(bf16[208,128]{1,0:T(8,128)(2,1)S(1)} %get-tuple-element.33.a0), channel_id=1, source_target_pairs={{0,128},{4,132},{8,136},{12,140},{16,144},{20,148},{24,152},{28,15... | collective-permute-start | bytes 159752 | tf_op jit(solution)/shard_map/ppermute | solution.py:427
  66.5 5.3 %collective-permute-start.11 = (bf16[208,128]{1,0:T(8,128)(2,1)S(1)}, bf16[208,128]{1,0:T(8,128)(2,1)S(1)}, u32[]{:S(2)}, u32[]{:S(2)}) collective-permute-start(bf16[208,128]{1,0:T(8,128)(2,1)S(1)} %get-tuple-element.33.a0), channel_id=1, source_target_pairs={{0,192},{4,196},{8,200},{12,204},{16,208},{20,212},{24,216},{28,22... | collective-permute-start | bytes 159752 | tf_op jit(solution)/shard_map/ppermute | solution.py:427
  73.1 0.6 copy-start.12
  73.8 6.2 %collective-permute-start.12 = (bf16[192,128]{1,0:T(8,128)(2,1)S(1)}, bf16[192,128]{1,0:T(8,128)(2,1)S(1)}, u32[]{:S(2)}, u32[]{:S(2)}) collective-permute-start(bf16[192,128]{1,0:T(8,128)(2,1)S(1)} %get-tuple-element.39), channel_id=1, source_target_pairs={{0,4},{4,0},{8,12},{12,8},{16,20},{20,16},{24,28},{28,24},{32,36},... | collective-permute-start | bytes 147464 | tf_op jit(solution)/shard_map/ppermute | solution.py:422
  76.8 30.6 %collective-permute-start.13 = (bf16[192,128]{1,0:T(8,128)(2,1)}, bf16[192,128]{1,0:T(8,128)(2,1)}, u32[]{:S(2)}, u32[]{:S(2)}) collective-permute-start(bf16[192,128]{1,0:T(8,128)(2,1)} %get-tuple-element.40), channel_id=1, source_target_pairs={{0,8},{4,12},{8,0},{12,4},{16,24},{20,28},{24,16},{28,20},{32,40},... | collective-permute-start | bytes 147464 | tf_op jit(solution)/shard_map/ppermute | solution.py:422
  80.0 0.6 copy-start.14
  80.6 26.8 %collective-permute-start.14 = (bf16[192,128]{1,0:T(8,128)(2,1)}, bf16[192,128]{1,0:T(8,128)(2,1)}, u32[]{:S(2)}, u32[]{:S(2)}) collective-permute-start(bf16[192,128]{1,0:T(8,128)(2,1)} %get-tuple-element.41), channel_id=1, source_target_pairs={{0,12},{4,8},{8,4},{12,0},{16,28},{20,24},{24,20},{28,16},{32,44},... | collective-permute-start | bytes 147464 | tf_op jit(solution)/shard_map/ppermute | solution.py:422
  85.6 7.2 %copy-start.3 = (bf16[512,768]{1,0:T(8,128)(2,1)S(1)}, bf16[512,768]{1,0:T(8,128)(2,1)}, u32[]{:S(2)}) copy-start(bf16[512,768]{1,0:T(8,128)(2,1)} %k_ref.3) | copy-start | bytes 2359300
  86.4 1.1 copy-start.4
  87.5 0.7 copy-start.18
  88.2 4.6 %copy-start.5 = (bf16[512,768]{1,0:T(8,128)(2,1)S(1)}, bf16[512,768]{1,0:T(8,128)(2,1)}, u32[]{:S(2)}) copy-start(bf16[512,768]{1,0:T(8,128)(2,1)} %q_ref.1) | copy-start | bytes 2359300
  92.8 14.7 %copy-start.13 = (bf16[192,128]{1,0:T(8,128)(2,1)S(1)}, bf16[192,128]{1,0:T(8,128)(2,1)}, u32[]{:S(2)}) copy-start(bf16[192,128]{1,0:T(8,128)(2,1)} %copy-done.12) | copy-start | bytes 147460
  92.8 14.7 %copy-start.15 = (bf16[192,128]{1,0:T(8,128)(2,1)S(1)}, bf16[192,128]{1,0:T(8,128)(2,1)}, u32[]{:S(2)}) copy-start(bf16[192,128]{1,0:T(8,128)(2,1)} %copy-done.14) | copy-start | bytes 147460
  92.8 0.7 copy-start.16
  93.5 0.7 copy-start.17

commit v2 on v1

v2 whole, which is shorter than its diff:
```python
import functools
import math

import jax
import jax.numpy as jnp
import numpy as np
from jax import lax
from jax.experimental import pallas as pl
from jax.experimental.pallas import tpu as pltpu
from jax.sharding import PartitionSpec as P

HEAD_DIM = 64
STATE = 128
HEADS_PER_GROUP = 6
SPAN_DEV = 4
ROWS = 512
HALF = 256
PAIRS = 6
HEADS_HERE = 12
QUARTER = 192
WIDTH = HEADS_HERE * HEAD_DIM
PIECE = 208
NEG = -1e30
F32 = jnp.float32
BF16 = jnp.bfloat16

LN2_HI = float(np.float32(jnp.bfloat16(math.log(2.0))))
LN2_LO = float(np.float32(jnp.bfloat16(math.log(2.0) - LN2_HI)))
LN3_HI = float(np.float32(jnp.bfloat16(math.log(3.0))))
LN3_LO = float(np.float32(jnp.bfloat16(math.log(3.0) - LN3_HI)))

VMEM = pl.BlockSpec(memory_space=pltpu.VMEM)
SMEM = pl.BlockSpec(memory_space=pltpu.SMEM)


def iota(shape, dim):
    return lax.broadcasted_iota(jnp.int32, shape, dim)


def dot(a, b):
    return lax.dot_general(a, b, (((1,), (0,)), ((), ())), preferred_element_type=F32)


def dot_t(a, b):
    return lax.dot_general(a, b, (((1,), (1,)), ((), ())), preferred_element_type=F32)


def t_dot(a, b):
    return lax.dot_general(a, b, (((0,), (0,)), ((), ())), preferred_element_type=F32)


def one(mask, kind=F32):
    return jnp.where(mask, 1.0, 0.0).astype(kind)


def residue_of(block):
    return ((block & 1) << 2) | (block & 2) | (block >> 2)


def sorting():
    row = iota((ROWS, ROWS), 0)
    token = 8 * (row & 63) + residue_of(row >> 6)
    return one(iota((ROWS, ROWS), 1) == token, BF16)


def unsorting():
    column = iota((ROWS, ROWS), 1)
    token = 8 * (column & 63) + residue_of(column >> 6)
    return one(iota((ROWS, ROWS), 0) == token, BF16)


def split(x, parts):
    out = []
    for _ in range(parts):
        head = x.astype(BF16)
        out.append(head)
        x = x - head.astype(F32)
    return out


def params(mib=14):
    return pltpu.CompilerParams(vmem_limit_bytes=mib * 1024 * 1024)


def pack_kernel(k_ref, v_ref, valid_ref, out_ref):
    sort = sorting()
    unsort = unsorting()
    low = (iota((HALF, WIDTH), 1) & 127) < HEAD_DIM
    rows = dot(sort, k_ref[...])
    out_ref[:HALF, :] = jnp.where(low, rows[:HALF], rows[HALF:]).astype(BF16)
    columns = t_dot(v_ref[...], unsort)
    even = (iota((WIDTH, HALF), 0) & 127) < HEAD_DIM
    columns = jnp.where(even, columns[:, :HALF], columns[:, HALF:]).astype(BF16)
    for at in range(0, WIDTH, HALF):
        out_ref[HALF:ROWS, at : at + HALF] = columns[at : at + HALF]
    valid = jnp.broadcast_to(valid_ref[...].astype(F32), (16, ROWS)).astype(BF16)
    line = dot_t(valid, sort)
    out_ref[ROWS : ROWS + 16, :] = jnp.concatenate(
        [line, jnp.zeros((16, WIDTH - ROWS), F32)], axis=1
    ).astype(BF16)


def log_count(count):
    high = jnp.where(count == 0, NEG, jnp.where(count == 2, LN2_HI, jnp.where(count == 3, LN3_HI, 0.0)))
    low = jnp.where(count == 2, LN2_LO, jnp.where(count == 3, LN3_LO, 0.0))
    return high, low


def plan_of(head, seg_ref, dil_ref):
    group = head // HEADS_PER_GROUP
    return dil_ref[group, 1], dil_ref[group, 2], seg_ref[group, 0], seg_ref[group, 1]


def local_plan(head, seg_ref, dil_ref):
    r1, r2, w0, w1 = plan_of(head, seg_ref, dil_ref)
    key, query = iota((16, ROWS), 0), iota((16, ROWS), 1) >> 5
    same = (key & 1) == (query & 1)
    key_off, query_off = residue_of(key >> 1) - head, residue_of(query >> 1) - head

    def on(stride):
        return (key_off & (stride - 1)) + (query_off & (stride - 1)) == 0

    count = one(same | (w0 >= ROWS)) + one(on(r1) & (same | (w1 >= ROWS))) + one(on(r2))
    return jnp.concatenate([*log_count(count), jnp.ones((16, ROWS), F32)], axis=0)


def remote_plan(head, seg_ref, dil_ref):
    r1, r2, _, w1 = plan_of(head, seg_ref, dil_ref)
    row = iota((8, HALF), 0)
    shift = (head & 1) - head
    key_off = residue_of(row & 3) + shift
    query_off = residue_of(iota((8, HALF), 1) >> 6) + shift

    def on(stride):
        return (key_off & (stride - 1)) + (query_off & (stride - 1)) == 0

    parts = []
    for reach in (2 * ROWS, 4 * ROWS):
        high, low = log_count(one(on(r1) & (w1 >= reach)) + one(on(r2)))
        parts.append(jnp.where(row < 4, high, low))
    return jnp.concatenate(parts + [jnp.ones((16, HALF), F32)], axis=0)


def own_bias(head, dil_ref):
    group = head // HEADS_PER_GROUP
    off = residue_of(iota((1, ROWS), 1) >> 6) - head
    count = 1 + jnp.where((off & (dil_ref[group, 1] - 1)) == 0, 1, 0)
    count = count + jnp.where((off & (dil_ref[group, 2] - 1)) == 0, 1, 0)
    return jnp.where(count == 1, 0.0, jnp.where(count == 2, LN2_HI + LN2_LO, LN3_HI + LN3_LO))


def softmax_columns(keys, queries, values, own, before):
    scores = dot(keys, queries)
    if own is not None:
        tile = 128
        diagonal = iota((tile, tile), 0) == iota((tile, tile), 1)
        rows = []
        for at in range(0, scores.shape[0], tile):
            line = scores[at : at + tile]
            here = jnp.where(diagonal, own[:, at : at + tile], line[:, at : at + tile])
            parts = [line[:, :at], here, line[:, at + tile :]]
            rows.append(jnp.concatenate([x for x in parts if x.shape[1]], axis=1))
        scores = jnp.concatenate(rows, axis=0)
    top = jnp.max(scores, axis=0, keepdims=True)
    if before is not None:
        top = jnp.maximum(top, before)
    values = jnp.concatenate([values, jnp.ones((16, values.shape[1]), BF16)], axis=0)
    out = dot(values, jnp.exp(scores - top).astype(BF16))
    return out[:HEAD_DIM], out[HEAD_DIM : HEAD_DIM + 1], top


def all_queries(rows, part, plan):
    blank = jnp.zeros((HEAD_DIM, rows.shape[1]), BF16)
    pieces = [rows, blank] if part == 0 else [blank, rows]
    rest = jnp.zeros((128 - plan.shape[0], rows.shape[1]), BF16)
    return jnp.concatenate(pieces + [plan.astype(BF16), rest], axis=0)


def local_kernel(
    q_ref, k_ref, v_ref, valid_ref, seg_ref, dil_ref, rank_ref,
    qe_ref, plan_ref, oe_ref, stat_ref, oo_ref, ve_ref,
    unsort_ref, sq_ref, sk_ref, sv_ref,
):
    unsort_ref[...] = unsorting()
    valid = jnp.broadcast_to(valid_ref[...].astype(F32), (128, ROWS)).astype(BF16)
    flags = dot(valid, unsort_ref[...])
    ve_ref[...] = flags[:8]
    row, lane = iota((ROWS, 128), 0), iota((ROWS, 128), 1)
    key_side = one(((row >> 5) == (lane & 15)) & (lane < 32))
    key_side = jnp.where(lane == 32, (1.0 - flags.T) * NEG, key_side).astype(BF16)
    sq_ref[...] = t_dot(q_ref[...], unsort_ref[...]) * (HEAD_DIM**-0.5)
    sk_ref[...] = t_dot(k_ref[...], unsort_ref[...])
    sv_ref[...] = t_dot(v_ref[...], unsort_ref[...]).astype(BF16)
    for pair in range(PAIRS):
        both = slice(pair * 128, (pair + 1) * 128)
        key = sk_ref[both, :].T.astype(BF16)
        keys = jnp.concatenate([key, key_side], axis=1)
        stats = []
        for part in range(2):
            head = rank_ref[0] * HEADS_HERE + 2 * pair + part
            start = pair * 128 + part * HEAD_DIM
            now = slice(start, start + HEAD_DIM)
            query = sq_ref[now, :]
            queries = all_queries(query.astype(BF16), part, local_plan(head, seg_ref, dil_ref))
            own = jnp.sum(query * sk_ref[now, :], axis=0, keepdims=True) + own_bias(head, dil_ref)
            out, total, top = softmax_columns(keys, queries, sv_ref[now, :], own, None)
            inside = slice(part * HALF, (part + 1) * HALF)
            outside = slice((1 - part) * HALF, (2 - part) * HALF)
            qe_ref[now, :] = query[:, inside].astype(BF16)
            oe_ref[now, :] = out[:, inside]
            oo_ref[now, :] = (out[:, outside] / total[:, outside] * flags[:1, outside]).astype(BF16)
            stats += [top[:, inside], total[:, inside]]
            at = (2 * pair + part) * 32
            plan_ref[at : at + 32, :] = remote_plan(head, seg_ref, dil_ref).astype(BF16)
        stat_ref[pair * 8 : pair * 8 + 8, :] = jnp.concatenate(stats + [jnp.zeros((4, HALF), F32)], axis=0)


def remote_kernel(
    qe_ref, plan_ref, oe_ref, stat_ref, oo_ref, ve_ref, kv1_ref, kv2_ref, kv3_ref,
    out_ref, rows_ref,
):
    blocks = (kv1_ref, kv2_ref, kv3_ref)
    spread = one((iota((16, 128), 0) == 0) & (iota((16, 128), 1) == 16), BF16)
    row, lane = iota((HALF, 128), 0), iota((HALF, 128), 1)
    sides = []
    for parity in range(2):
        pieces = []
        for at, ref in enumerate(blocks):
            flags = ref[ROWS : ROWS + 16, parity * HALF : (parity + 1) * HALF].astype(F32)
            line = ((1.0 - flags) * NEG).astype(BF16)
            wanted = (lane & 3) == (row >> 6)
            wanted = wanted & (lane < 8) if at == 0 else wanted & (lane >= 8) & (lane < 16)
            pieces.append(t_dot(line, spread) + one(wanted))
        sides.append(jnp.concatenate(pieces, axis=0).astype(BF16))
    for pair in range(PAIRS):
        both = slice(pair * 128, (pair + 1) * 128)
        place = slice(HALF + (pair & 1) * 128, HALF + (pair & 1) * 128 + 128)
        chunk = slice((pair >> 1) * HALF, (pair >> 1) * HALF + HALF)
        key = jnp.concatenate([ref[:HALF, both] for ref in blocks], axis=0)
        value = jnp.concatenate([ref[place, chunk] for ref in blocks], axis=1)
        for part in range(2):
            start = pair * 128 + part * HEAD_DIM
            now = slice(start, start + HEAD_DIM)
            at = (2 * pair + part) * 32
            keys = jnp.concatenate([key, sides[part]], axis=1)
            queries = all_queries(qe_ref[now, :], part, plan_ref[at : at + 32, :])
            stat = pair * 8 + 2 * part
            before = stat_ref[stat : stat + 1, :]
            out, total, top = softmax_columns(
                keys, queries, value[part * HEAD_DIM : (part + 1) * HEAD_DIM], None, before
            )
            rescale = jnp.exp(before - top)
            out = out + oe_ref[now, :] * rescale
            total = total + stat_ref[stat + 1 : stat + 2, :] * rescale
            done = out / total * ve_ref[:1, part * HALF : (part + 1) * HALF]
            rows_ref[now, part * HALF : (part + 1) * HALF] = done.astype(BF16)
            rows_ref[now, (1 - part) * HALF : (2 - part) * HALF] = oo_ref[now, :]
    out_ref[...] = dot_t(unsorting(), rows_ref[...]).astype(BF16)


def state_kernel(v_ref, steps_ref, rates_ref, valid_ref, into_ref, place_ref, *out_refs):
    full_ref = out_refs[4]
    later = one(iota((ROWS, ROWS), 0) > iota((ROWS, ROWS), 1), BF16)
    rates = jnp.concatenate([rates_ref[...], jnp.zeros((4, ROWS), F32)], axis=0)
    sums = dot(jnp.concatenate(split(rates, 3), axis=0), later)
    to_end = sums[:16] + sums[16:32] + sums[32:]
    steps = jnp.concatenate([steps_ref[...], jnp.zeros((4, ROWS), F32)], axis=0)
    weight = jnp.exp(-to_end) * steps * valid_ref[...].astype(F32)
    width = HEADS_HERE * HEAD_DIM
    spread = one((iota((32, width), 0) & 15) == (iota((32, width), 1) >> 6), BF16)
    scale = t_dot(jnp.concatenate(split(weight, 2), axis=0), spread)
    driven = (v_ref[...].astype(F32) * scale).astype(BF16)
    full_ref[...] = t_dot(driven, into_ref[...])
    decay = jnp.exp(-jnp.sum(rates, axis=1, keepdims=True))
    decay = jnp.concatenate(split(jnp.broadcast_to(decay, (16, STATE)), 2), axis=0)
    row, source = iota((16, 32), 0), iota((16, 32), 1)
    for step in range(4):
        part = place_ref[0] ^ step
        wanted = jnp.where(row < 3, part * 3 + row, jnp.where(row < 6, 13 + part * 3 + row, -1))
        start = pl.multiple_of(part * QUARTER, 64)
        out_refs[step][:QUARTER, :] = full_ref[pl.ds(start, QUARTER), :].astype(BF16)
        out_refs[step][QUARTER:, :] = dot(one(source == wanted, BF16), decay).astype(BF16)


def decay_rows(ref_value):
    tail = ref_value[QUARTER:].astype(F32)
    return [tail[k : k + 1] + tail[k + 3 : k + 4] for k in range(3)]


def spread_rows(decays):
    return jnp.concatenate([jnp.broadcast_to(d, (HEAD_DIM, STATE)) for d in decays], axis=0)


def pack_piece(state, decays):
    high, low = zip(*(split(d, 2) for d in decays))
    tail = jnp.concatenate(
        [d.astype(F32) for d in high + low] + [jnp.zeros((10, STATE), F32)], axis=0
    )
    return jnp.concatenate([state, tail], axis=0).astype(BF16)


def block_kernel(place_ref, a0, a1, a2, a3, total_ref, before_ref, fade_ref, held):
    for step, ref in enumerate((a0, a1, a2, a3)):
        held[place_ref[0] ^ step] = ref[...].astype(F32)
    state = jnp.zeros((QUARTER, STATE), F32)
    decays = [jnp.ones((1, STATE), F32)] * 3
    for at in range(4):
        before_ref[at] = state
        fade_ref[at] = spread_rows(decays)
        now = decay_rows(held[at])
        state = state * spread_rows(now) + held[at, :QUARTER, :]
        decays = [a * b for a, b in zip(decays, now)]
    total_ref[...] = pack_piece(state, decays)


def chain(place, held):
    state = jnp.zeros((QUARTER, STATE), F32)
    decays = [jnp.ones((1, STATE), F32)] * 3
    before, before_decays = state, decays
    for at in range(4):
        here = place == at
        before = jnp.where(here, state, before)
        before_decays = [jnp.where(here, a, b) for a, b in zip(decays, before_decays)]
        now = decay_rows(held[at])
        state = state * spread_rows(now) + held[at, :QUARTER, :]
        decays = [a * b for a, b in zip(decays, now)]
    return before, before_decays, state, decays


def line_kernel(place_ref, a0, a1, a2, a3, total_ref, before_ref, fade_ref, held):
    for step, ref in enumerate((a0, a1, a2, a3)):
        held[(place_ref[1] - step) & 3] = ref[...].astype(F32)
    before, before_decays, state, decays = chain(place_ref[1], held)
    before_ref[...] = before
    fade_ref[...] = spread_rows(before_decays)
    total_ref[...] = pack_piece(state, decays)


def plane_kernel(place_ref, a0, a1, a2, a3, line_before, line_fade, block_before, block_fade, *rest):
    outs, held = rest[:4], rest[4]
    for step, ref in enumerate((a0, a1, a2, a3)):
        held[(place_ref[2] - step) & 3] = ref[...].astype(F32)
    before = chain(place_ref[2], held)[0]
    start = line_fade[...] * before + line_before[...]
    for step in range(4):
        part = place_ref[0] ^ step
        outs[step][...] = (block_fade[part] * start + block_before[part]).astype(BF16)


def within_kernel(
    v_ref, gate_ref, steps_ref, rates_ref, valid_ref, into_ref, read_ref, skip_ref,
    base_ref, lift_ref, couple_ref, col_ref, row_ref,
):
    pair = pl.program_id(0)

    @pl.when(pair == 0)
    def _():
        couple_ref[...] = dot_t(read_ref[...], into_ref[...])
        upto = one(iota((ROWS, ROWS), 0) <= iota((ROWS, ROWS), 1), BF16)
        rates = jnp.concatenate([rates_ref[...], jnp.zeros((4, ROWS), F32)], axis=0)
        sums = dot(jnp.concatenate(split(rates, 3), axis=0), upto)
        fall = -(sums[:16] + sums[16:32] + sums[32:])
        steps = jnp.concatenate([steps_ref[...], jnp.ones((4, ROWS), F32)], axis=0)
        col_ref[...] = fall
        row_ref[...] = jnp.where(valid_ref[...] > 0, fall - jnp.log(steps), -NEG)

    value = v_ref[...]
    lane = iota((ROWS, 128), 1)
    results = []
    falls = []
    tile = 128
    causal = iota((tile, tile), 0) >= iota((tile, tile), 1)
    for part in range(2):
        head = 2 * pair + part
        fall = jnp.broadcast_to(col_ref[pl.ds(head, 1), :], (128, ROWS)).T
        line = row_ref[pl.ds(head, 1), :]
        pieces = []
        for at in range(ROWS // tile):
            fall_now = fall[at * tile : (at + 1) * tile]
            weights = []
            for src in range(at + 1):
                gap = fall_now - line[:, src * tile : (src + 1) * tile]
                if src == at:
                    gap = jnp.where(causal, gap, NEG)
                weights.append(
                    (
                        jnp.exp(gap)
                        * couple_ref[at * tile : (at + 1) * tile, src * tile : (src + 1) * tile]
                    ).astype(BF16)
                )
            pieces.append(dot(jnp.concatenate(weights, axis=1), value[: (at + 1) * tile]))
        results.append(jnp.concatenate(pieces, axis=0))
        falls.append(fall)
    low = lane < HEAD_DIM
    gate = gate_ref[...].astype(F32)
    gate = gate / (1.0 + jnp.exp(-gate))
    skip = jnp.where(low, skip_ref[2 * pair], skip_ref[2 * pair + 1])
    within = jnp.where(low, results[0], results[1])
    base_ref[...] = (within + skip * value.astype(F32)) * gate
    lift_ref[...] = jnp.exp(jnp.where(low, falls[0], falls[1])) * gate


def finish_kernel(place_ref, f0, f1, f2, f3, read_ref, base_ref, lift_ref, gain_ref, out_ref, held):
    @pl.when(pl.program_id(0) == 0)
    def _():
        for step, ref in enumerate((f0, f1, f2, f3)):
            part = place_ref[0] ^ step
            held[pl.ds(pl.multiple_of(part * QUARTER, 64), QUARTER), :] = ref[...]

    together = one((iota((128, 128), 0) >> 6) == (iota((128, 128), 1) >> 6), BF16)
    for pair in range(PAIRS):
        now = slice(pair * 128, (pair + 1) * 128)
        carried = dot_t(read_ref[...], held[now, :])
        gated = base_ref[:, now] + lift_ref[:, now] * carried
        high, low = split(gated * gated, 2)
        mean = (dot(high, together) + dot(low, together)) * (1.0 / HEAD_DIM)
        out_ref[:, now] = (gated * lax.rsqrt(mean + 1e-05) * gain_ref[:, now]).astype(BF16)


def shape(*dims, kind=BF16):
    return jax.ShapeDtypeStruct(dims, kind)


def lanes(rows, row_block=0):
    return pl.BlockSpec((rows, 128), lambda pair: (row_block, pair))


def whole(*dims):
    return pl.BlockSpec(dims, lambda pair: (0,) * len(dims))


def call_pack(key_rows, value_rows, valid):
    return pl.pallas_call(
        pack_kernel,
        out_shape=shape(ROWS + 16, WIDTH),
        in_specs=[VMEM] * 3,
        out_specs=VMEM,
        compiler_params=params(),
        name="pack",
    )(key_rows, value_rows, valid)


def call_state(*args):
    return pl.pallas_call(
        state_kernel,
        out_shape=[shape(PIECE, STATE)] * 4,
        in_specs=[VMEM] * 5 + [SMEM],
        out_specs=[VMEM] * 4,
        scratch_shapes=[pltpu.VMEM((WIDTH, STATE), F32)],
        compiler_params=params(),
        name="state",
    )(*args)


HOLD = [pltpu.VMEM((4, PIECE, STATE), F32)]


def call_block(place, *pieces):
    return pl.pallas_call(
        block_kernel,
        out_shape=[shape(PIECE, STATE), shape(4, QUARTER, STATE, kind=F32), shape(4, QUARTER, STATE, kind=F32)],
        in_specs=[SMEM] + [VMEM] * 4,
        out_specs=[VMEM] * 3,
        scratch_shapes=HOLD,
        compiler_params=params(),
        name="block",
    )(place, *pieces)


def call_line(place, *totals):
    return pl.pallas_call(
        line_kernel,
        out_shape=[shape(PIECE, STATE), shape(QUARTER, STATE, kind=F32), shape(QUARTER, STATE, kind=F32)],
        in_specs=[SMEM] + [VMEM] * 4,
        out_specs=[VMEM] * 3,
        scratch_shapes=HOLD,
        compiler_params=params(),
        name="line",
    )(place, *totals)


def call_plane(place, *args):
    return pl.pallas_call(
        plane_kernel,
        out_shape=[shape(QUARTER, STATE)] * 4,
        in_specs=[SMEM] + [VMEM] * 8,
        out_specs=[VMEM] * 4,
        scratch_shapes=HOLD,
        compiler_params=params(),
        name="plane",
    )(place, *args)


KEPT = [
    shape(WIDTH, HALF),
    shape(HEADS_HERE * 32, HALF),
    shape(WIDTH, HALF, kind=F32),
    shape(8 * PAIRS, HALF, kind=F32),
    shape(WIDTH, HALF),
    shape(8, ROWS, kind=F32),
]


def call_local(*args):
    return pl.pallas_call(
        local_kernel,
        out_shape=KEPT,
        in_specs=[VMEM] * 4 + [SMEM] * 3,
        out_specs=[VMEM] * 6,
        scratch_shapes=[
            pltpu.VMEM((ROWS, ROWS), BF16),
            pltpu.VMEM((WIDTH, ROWS), F32),
            pltpu.VMEM((WIDTH, ROWS), F32),
            pltpu.VMEM((WIDTH, ROWS), BF16),
        ],
        compiler_params=params(24),
        name="local",
    )(*args)


def call_within(*args):
    return pl.pallas_call(
        within_kernel,
        grid=(PAIRS,),
        out_shape=[shape(ROWS, WIDTH, kind=F32)] * 2,
        in_specs=[lanes(ROWS)] * 2
        + [whole(HEADS_HERE, ROWS)] * 2
        + [whole(1, ROWS), whole(ROWS, STATE), whole(ROWS, STATE), SMEM],
        out_specs=[lanes(ROWS)] * 2,
        scratch_shapes=[pltpu.VMEM((ROWS, ROWS), F32), pltpu.VMEM((16, ROWS), F32), pltpu.VMEM((16, ROWS), F32)],
        compiler_params=params(),
        name="within",
    )(*args)


def call_finish(*args):
    def rows(width):
        return pl.BlockSpec((HALF, width), lambda at: (at, 0))

    return pl.pallas_call(
        finish_kernel,
        grid=(ROWS // HALF,),
        out_shape=shape(ROWS, WIDTH),
        in_specs=[SMEM]
        + [whole(QUARTER, STATE)] * 4
        + [rows(STATE), rows(WIDTH), rows(WIDTH), whole(1, WIDTH)],
        out_specs=rows(WIDTH),
        scratch_shapes=[pltpu.VMEM((WIDTH, STATE), BF16)],
        compiler_params=params(),
        name="finish",
    )(*args)


def call_remote(kept, arrived):
    return pl.pallas_call(
        remote_kernel,
        out_shape=shape(ROWS, WIDTH),
        in_specs=[VMEM] * 9,
        out_specs=VMEM,
        scratch_shapes=[pltpu.VMEM((WIDTH, ROWS), BF16)],
        compiler_params=params(24),
        name="remote",
    )(*kept, *arrived)


def per_device(
    query_rows,
    key_rows,
    value_rows,
    patch_valid,
    segment_lengths,
    dilation,
    step_sizes,
    decay_rates,
    state_in,
    state_out,
    gate_in,
    skip_weight,
    norm_gain,
):
    count = lax.axis_size("seq")
    seq_rank = lax.axis_index("seq").astype(jnp.int32)
    rank = jnp.reshape(lax.axis_index("head").astype(jnp.int32), (1,))
    place = jnp.stack([seq_rank & 3, (seq_rank >> 2) & 3, seq_rank >> 4])
    valid = patch_valid.reshape(1, ROWS)
    gain = norm_gain.reshape(1, WIDTH)

    def cross(block, mask):
        return lax.ppermute(block, "seq", [(i, i ^ mask) for i in range(count)])

    def turn(block, step, span):
        unit = span // 4
        route = [(i, i // span * span + (i % span + step * unit) % span) for i in range(count)]
        return lax.ppermute(block, "seq", route)

    after = lax.optimization_barrier

    pieces = call_state(value_rows, step_sizes, decay_rates, valid, state_in, place)
    packed, pieces = after((call_pack(key_rows, value_rows, valid), pieces))
    pieces = [pieces[0]] + [cross(pieces[mask], mask) for mask in range(1, SPAN_DEV)]
    near = cross(packed, 1)
    total, block_before, block_fade = call_block(place, *pieces)
    totals = [total] + [turn(total, step, 16) for step in range(1, 4)]
    packed, totals[1] = after((packed, totals[1]))
    arrived = [near] + [cross(packed, mask) for mask in range(2, SPAN_DEV)]
    base, lift = call_within(
        value_rows, gate_in, step_sizes, decay_rates, after((valid, total))[0], state_in, state_out, skip_weight
    )
    totals, base = after((totals, base))
    total, line_before, line_fade = call_line(place, *totals)
    kept = call_local(
        query_rows, key_rows, value_rows, after((valid, total))[0], segment_lengths, dilation, rank
    )
    totals = [total] + [turn(total, step, 64) for step in range(1, 4)]
    totals, kept = after((totals, kept))
    carried = call_plane(place, *totals, line_before, line_fade, block_before, block_fade)
    carried = [carried[0]] + [cross(carried[mask], mask) for mask in range(1, SPAN_DEV)]
    scanned = call_finish(place, *carried, state_out, base, lift, gain)
    attended = call_remote(kept, arrived)
    return (attended, scanned)


def solution(mesh):
    return jax.shard_map(
        per_device,
        mesh=mesh,
        in_specs=(
            P(("slide", "seq"), "head"),
            P(("slide", "seq"), "head"),
            P(("slide", "seq"), "head"),
            P(("slide", "seq")),
            P(),
            P(),
            P("head", ("slide", "seq")),
            P("head", ("slide", "seq")),
            P(("slide", "seq"), None),
            P(("slide", "seq"), None),
            P(("slide", "seq"), "head"),
            P("head"),
            P("head"),
        ),
        out_specs=(P(("slide", "seq"), "head"), P(("slide", "seq"), "head")),
        check_vma=False,
    )
```

time: 127 us -> 114 us (0.90)
  the two profiles are of different devices: /device:TPU:88 before, /device:TPU:32 now
where the time goes in v2:
time: 114 us
  waiting for transfers between devices  51.6 us (45%)
  Pallas kernels  30.4 us (27%)
  starting transfers between devices  23.3 us (20%)
  local copies, waits for them, and re-layouts  7.48 us (7%)
    ppermute x6, waiting for transfers between devices, turn(): return lax.ppermute(block, 'seq', route)  34.9 us
    ppermute x9, waiting for transfers between devices, cross(): return lax.ppermute(block, 'seq', [(i, i ^ mask) for i in range(count)])  16.6 us
    ppermute x6, starting transfers between devices, turn(): return lax.ppermute(block, 'seq', route)  15 us
    pallas_call x1, Pallas kernels, call_remote(): pl.pallas_call(remote_kernel, out_shape=shape(ROWS, WIDTH), in_specs=[VME...  9.16 us
    ppermute x9, starting transfers between devices, cross(): return lax.ppermute(block, 'seq', [(i, i ^ mask) for i in range(count)])  8.29 us
    pallas_call x1, Pallas kernels, call_local(): pl.pallas_call(local_kernel, out_shape=KEPT, in_specs=[VMEM] * 4 + [SMEM]...  7.79 us
    unnamed x48, local copies, waits for them, and re-layouts  7.48 us
    pallas_call x1, Pallas kernels, call_within(): pl.pallas_call(within_kernel, grid=(PAIRS,), out_shape=[shape(ROWS, WIDTH...  4.6 us
  transfers between devices with their start and end apart: 15, of which 8 were waited for; matrix products, arithmetic and copies ran while one was open for 0% of the time, Pallas kernels for 15%

profile of v2, /device:TPU:32, one launch (start us, length us, event | category | flops | bytes accessed | tf_op | source)
XLA Modules:
  0.0 113.7 jit_solution(10544647182401377987)
XLA Ops:
  0.6 0.1 pad_add_fusion.place_ref
  0.7 1.1 copy-done
  1.9 1.1 copy-done.2
  3.0 0.7 copy-done.18
  3.7 0.0 copy-start.6
  3.7 0.0 copy-start.9
  3.7 0.0 copy-start.22
  3.7 2.0 %pack.1 = bf16[528,768]{1,0:T(8,128)(2,1)} custom-call(bf16[512,768]{1,0:T(8,128)(2,1)S(1)} %copy-done.2, bf16[512,768]{1,0:T(8,128)(2,1)S(1)} %copy-done, s32[1,512]{1,0:T(1,128)S(1)} %bitcast.5), custom_call_target="tpu_custom_call" | custom-call | tf_op jit(solution)/shard_map/pack/pallas_call | solution.py:433
  5.8 0.0 copy-start.3
  5.8 0.0 copy-start.19
  5.8 0.0 copy-start.20
  5.8 1.5 %state.1 = (bf16[208,128]{1,0:T(8,128)(2,1)S(1)}, bf16[208,128]{1,0:T(8,128)(2,1)S(1)}, bf16[208,128]{1,0:T(8,128)(2,1)S(1)}, bf16[208,128]{1,0:T(8,128)(2,1)S(1)}) custom-call(bf16[512,768]{1,0:T(8,128)(2,1)S(1)} %copy-done.1, f32[12,512]{1,0:T(8,128)S(1)} %copy-done.14, f32[12,512]{1,0:T(8,128)S(1)} %copy-done.15, s32[1,512]{1,0:T(1,128)S(1)} %bitcast.6, ...), custom_call_target="tpu_custom_call" | custom-call | tf_op jit(solution)/shard_map/state/pallas_call | solution.py:444
  7.3 3.1 %collective-permute-start = (bf16[208,128]{1,0:T(8,128)(2,1)S(1)}, bf16[208,128]{1,0:T(8,128)(2,1)S(1)}, u32[]{:S(2)}, u32[]{:S(2)}) collective-permute-start(bf16[208,128]{1,0:T(8,128)(2,1)S(1)} %get-tuple-element.53), channel_id=1, source_target_pairs={{0,4},{4,0},{8,12},{12,8},{16,20},{20,16},{24,28},{28,24},{32,36},... | collective-permute-start | bytes 159752 | tf_op jit(solution)/shard_map/ppermute | solution.py:589
  10.4 0.1 collective-permute-start.1
  10.5 1.9 %collective-permute-start.2 = (bf16[208,128]{1,0:T(8,128)(2,1)S(1)}, bf16[208,128]{1,0:T(8,128)(2,1)S(1)}, u32[]{:S(2)}, u32[]{:S(2)}) collective-permute-start(bf16[208,128]{1,0:T(8,128)(2,1)S(1)} %get-tuple-element.55), channel_id=1, source_target_pairs={{0,12},{4,8},{8,4},{12,0},{16,28},{20,24},{24,20},{28,16},{32,44},... | collective-permute-start | bytes 159752 | tf_op jit(solution)/shard_map/ppermute | solution.py:589
  12.4 0.6 collective-permute-done.a1
  13.0 1.5 %collective-permute-done.1.a2 = bf16[208,128]{1,0:T(8,128)(2,1)S(1)} collective-permute-done((bf16[208,128]{1,0:T(8,128)(2,1)S(1)}, bf16[208,128]{1,0:T(8,128)(2,1)S(1)}, u32[]{:S(2)}, u32[]{:S(2)}) %collective-permute-start.1) | collective-permute-done | bytes 53280 | tf_op jit(solution)/shard_map/ppermute | solution.py:589
  14.5 2.5 %collective-permute-done.2.a3 = bf16[208,128]{1,0:T(8,128)(2,1)S(1)} collective-permute-done((bf16[208,128]{1,0:T(8,128)(2,1)S(1)}, bf16[208,128]{1,0:T(8,128)(2,1)S(1)}, u32[]{:S(2)}, u32[]{:S(2)}) %collective-permute-start.2) | collective-permute-done | bytes 53280 | tf_op jit(solution)/shard_map/ppermute | solution.py:589
  17.1 0.6 block.1
  17.7 0.0 copy-start.12
  17.7 0.7 copy-done.12
  18.4 3.3 %collective-permute-start.3 = (bf16[208,128]{1,0:T(8,128)(2,1)S(1)}, bf16[208,128]{1,0:T(8,128)(2,1)S(1)}, u32[]{:S(2)}, u32[]{:S(2)}) collective-permute-start(bf16[208,128]{1,0:T(8,128)(2,1)S(1)} %get-tuple-element.61.a0), channel_id=1, source_target_pairs={{0,16},{4,20},{8,24},{12,28},{16,32},{20,36},{24,40},{28,44},{32,4... | collective-permute-start | bytes 159752 | tf_op jit(solution)/shard_map/ppermute | solution.py:594
  21.7 1.0 collective-permute-start.9
  22.7 4.7 %collective-permute-done.3.a1 = bf16[208,128]{1,0:T(8,128)(2,1)S(1)} collective-permute-done((bf16[208,128]{1,0:T(8,128)(2,1)S(1)}, bf16[208,128]{1,0:T(8,128)(2,1)S(1)}, u32[]{:S(2)}, u32[]{:S(2)}) %collective-permute-start.3) | collective-permute-done | bytes 53280 | tf_op jit(solution)/shard_map/ppermute | solution.py:594
  27.4 0.6 collective-permute-start.10
  28.0 1.4 %collective-permute-start.11 = (bf16[528,768]{1,0:T(8,128)(2,1)}, bf16[528,768]{1,0:T(8,128)(2,1)}, u32[]{:S(2)}, u32[]{:S(2)}) collective-permute-start(bf16[528,768]{1,0:T(8,128)(2,1)} %pack.1), channel_id=1, source_target_pairs={{0,12},{4,8},{8,4},{12,0},{16,28},{20,24},{24,20},{28,16},{32,44},... | collective-permute-start | bytes 2433032 | tf_op jit(solution)/shard_map/ppermute | solution.py:589
  29.4 5.0 %collective-permute-start.4 = (bf16[208,128]{1,0:T(8,128)(2,1)S(1)}, bf16[208,128]{1,0:T(8,128)(2,1)S(1)}, u32[]{:S(2)}, u32[]{:S(2)}) collective-permute-start(bf16[208,128]{1,0:T(8,128)(2,1)S(1)} %get-tuple-element.61.a0), channel_id=1, source_target_pairs={{0,32},{4,36},{8,40},{12,44},{16,48},{20,52},{24,56},{28,60},{32,0... | collective-permute-start | bytes 159752 | tf_op jit(solution)/shard_map/ppermute | solution.py:594
  34.4 0.4 collective-permute-start.5
  34.8 4.6 %within.1 = (f32[512,768]{1,0:T(8,128)S(1)}, f32[512,768]{1,0:T(8,128)S(1)}) custom-call(bf16[512,768]{1,0:T(8,128)(2,1)S(1)} %copy-done.1, bf16[512,768]{1,0:T(8,128)(2,1)S(1)} %copy-done.6, f32[12,512]{1,0:T(8,128)S(1)} %copy-done.14, f32[12,512]{1,0:T(8,128)S(1)} %copy-done.15, s32[1,512]{1,0:T(1,128)S(1)} %bitcast.7, bf16[512,128]{1,0:T(8,128)(2,1)S(1)} %copy-done.8, ...), custom_call_target="tpu_custom_call" | custom-call | tf_op jit(solution)/shard_map/within/pallas_call | solution.py:522
  39.4 1.2 %copy-done.4 = f32[512,768]{1,0:T(8,128)} copy-done((f32[512,768]{1,0:T(8,128)}, f32[512,768]{1,0:T(8,128)S(1)}, u32[]{:S(2)}) %copy-start.4) | copy-done | bytes 1572888
  40.6 29.4 %collective-permute-done.4.a2 = bf16[208,128]{1,0:T(8,128)(2,1)S(1)} collective-permute-done((bf16[208,128]{1,0:T(8,128)(2,1)S(1)}, bf16[208,128]{1,0:T(8,128)(2,1)S(1)}, u32[]{:S(2)}, u32[]{:S(2)}) %collective-permute-start.4) | collective-permute-done | bytes 53280 | tf_op jit(solution)/shard_map/ppermute | solution.py:594
  70.0 0.6 line.1
  70.6 1.7 %collective-permute-start.6 = (bf16[208,128]{1,0:T(8,128)(2,1)S(1)}, bf16[208,128]{1,0:T(8,128)(2,1)S(1)}, u32[]{:S(2)}, u32[]{:S(2)}) collective-permute-start(bf16[208,128]{1,0:T(8,128)(2,1)S(1)} %get-tuple-element.80.a0), channel_id=1, source_target_pairs={{0,64},{4,68},{8,72},{12,76},{16,80},{20,84},{24,88},{28,92},{32,9... | collective-permute-start | bytes 159752 | tf_op jit(solution)/shard_map/ppermute | solution.py:594
  72.3 2.9 %collective-permute-start.7 = (bf16[208,128]{1,0:T(8,128)(2,1)S(1)}, bf16[208,128]{1,0:T(8,128)(2,1)}, u32[]{:S(2)}, u32[]{:S(2)}) collective-permute-start(bf16[208,128]{1,0:T(8,128)(2,1)S(1)} %get-tuple-element.80.a0), channel_id=1, source_target_pairs={{0,128},{4,132},{8,136},{12,140},{16,144},{20,148},{24,152},{28,15... | collective-permute-start | bytes 159752 | tf_op jit(solution)/shard_map/ppermute | solution.py:594
  75.2 0.9 collective-permute-done.6.a1
  76.0 0.6 copy-done.16
  76.6 1.8 %collective-permute-start.8 = (bf16[208,128]{1,0:T(8,128)(2,1)S(1)}, bf16[208,128]{1,0:T(8,128)(2,1)}, u32[]{:S(2)}, u32[]{:S(2)}) collective-permute-start(bf16[208,128]{1,0:T(8,128)(2,1)S(1)} %get-tuple-element.80.a0), channel_id=1, source_target_pairs={{0,192},{4,196},{8,200},{12,204},{16,208},{20,212},{24,216},{28,22... | collective-permute-start | bytes 159752 | tf_op jit(solution)/shard_map/ppermute | solution.py:594
  78.5 0.0 copy-start.7
  78.5 1.1 copy-done.7
  79.6 7.8 %local.1 = (bf16[768,256]{1,0:T(8,128)(2,1)S(1)}, bf16[384,256]{1,0:T(8,128)(2,1)S(1)}, f32[768,256]{1,0:T(8,128)S(1)}, f32[48,256]{1,0:T(8,128)S(1)}, bf16[768,...) custom-call(bf16[512,768]{1,0:T(8,128)(2,1)S(1)} %copy-done.7, bf16[512,768]{1,0:T(8,128)(2,1)S(1)} %copy-done.3, ...), custom_call_target="tpu_custom_call" | custom-call | tf_op jit(solution)/shard_map/local/pallas_call | solution.py:505
  87.5 0.8 copy-done.17
  88.3 1.0 plane.1
  89.2 0.1 collective-permute-start.12
  89.4 0.1 collective-permute-start.13
  89.4 5.5 %collective-permute-done.12.f1 = bf16[192,128]{1,0:T(8,128)(2,1)S(1)} collective-permute-done((bf16[192,128]{1,0:T(8,128)(2,1)S(1)}, bf16[192,128]{1,0:T(8,128)(2,1)S(1)}, u32[]{:S(2)}, u32[]{:S(2)}) %collective-permute-start.12) | collective-permute-done | bytes 49184 | tf_op jit(solution)/shard_map/ppermute | solution.py:589
  94.9 6.5 %collective-permute-done.14.f3 = bf16[192,128]{1,0:T(8,128)(2,1)S(1)} collective-permute-done((bf16[192,128]{1,0:T(8,128)(2,1)S(1)}, bf16[192,128]{1,0:T(8,128)(2,1)S(1)}, u32[]{:S(2)}, u32[]{:S(2)}) %collective-permute-start.14) | collective-permute-done | bytes 49184 | tf_op jit(solution)/shard_map/ppermute | solution.py:589
  101.4 3.1 %finish.1 = bf16[512,768]{1,0:T(8,128)(2,1)} custom-call(s32[3]{0:T(128)S(1)} %pad_add_fusion.place_ref, bf16[192,128]{1,0:T(8,128)(2,1)S(1)} %get-tuple-element.88.f0, bf16[192,128]{1,0:T(8,128)(2,1)S(1)} %collective-permute-done.12.f1, bf16[192,128]{1,0:T(8,128)(2,1)S(1)} %collective-permute-done.13.f2, bf16[192,128]{1,0:T(8,128)(2,1)S(1)} %collective-permute-done.14.f3, ...), custom_call_target="tpu_custom_call" | custom-call | tf_op jit(solution)/shard_map/finish/pallas_call | solution.py:540
  104.5 9.2 %remote.1 = bf16[512,768]{1,0:T(8,128)(2,1)} custom-call(bf16[768,256]{1,0:T(8,128)(2,1)S(1)} %get-tuple-element.73.qe_ref, bf16[384,256]{1,0:T(8,128)(2,1)S(1)} %get-tuple-element.74.plan_ref, f32[768,256]{1,0:T(8,128)S(1)} %get-tuple-element.75.oe_ref, f32[48,256]{1,0:T(8,128)S(1)} %get-tuple-element.76.stat_ref, ...), custom_call_target="tpu_custom_call" | custom-call | tf_op jit(solution)/shard_map/remote/pallas_call | solution.py:555
  (41 shorter events, 0.1 us)
Async XLA Ops:
  0.7 1.1 copy-start
  1.8 1.1 copy-start.2
  3.0 0.7 copy-start.18
  3.7 2.1 %copy-start.1 = (bf16[512,768]{1,0:T(8,128)(2,1)S(1)}, bf16[512,768]{1,0:T(8,128)(2,1)}, u32[]{:S(2)}) copy-start(bf16[512,768]{1,0:T(8,128)(2,1)} %v_ref.7) | copy-start | bytes 2359300
  3.7 2.1 %copy-start.8 = (bf16[512,128]{1,0:T(8,128)(2,1)S(1)}, bf16[512,128]{1,0:T(8,128)(2,1)}, u32[]{:S(2)}) copy-start(bf16[512,128]{1,0:T(8,128)(2,1)} %into_ref.3) | copy-start | bytes 393220
  3.7 2.1 %copy-start.14 = (f32[12,512]{1,0:T(8,128)S(1)}, f32[12,512]{1,0:T(8,128)}, u32[]{:S(2)}) copy-start(f32[12,512]{1,0:T(8,128)} %steps_ref.3) | copy-start | bytes 73732
  3.7 2.1 %copy-start.15 = (f32[12,512]{1,0:T(8,128)S(1)}, f32[12,512]{1,0:T(8,128)}, u32[]{:S(2)}) copy-start(f32[12,512]{1,0:T(8,128)} %rates_ref.3) | copy-start | bytes 73732
  3.7 31.1 %copy-start.6 = (bf16[512,768]{1,0:T(8,128)(2,1)S(1)}, bf16[512,768]{1,0:T(8,128)(2,1)}, u32[]{:S(2)}) copy-start(bf16[512,768]{1,0:T(8,128)(2,1)} %gate_ref.1) | copy-start | bytes 2359300
  3.7 31.1 %copy-start.9 = (bf16[512,128]{1,0:T(8,128)(2,1)S(1)}, bf16[512,128]{1,0:T(8,128)(2,1)}, u32[]{:S(2)}) copy-start(bf16[512,128]{1,0:T(8,128)(2,1)} %read_ref.3) | copy-start | bytes 393220
  3.7 31.1 %copy-start.22 = (f32[12]{0:T(128)S(1)}, f32[12]{0:T(128)}, u32[]{:S(2)}) copy-start(f32[12]{0:T(128)} %skip_ref.1) | copy-start | bytes 148
  5.8 72.7 %copy-start.3 = (bf16[512,768]{1,0:T(8,128)(2,1)S(1)}, bf16[512,768]{1,0:T(8,128)(2,1)}, u32[]{:S(2)}) copy-start(bf16[512,768]{1,0:T(8,128)(2,1)} %k_ref.3) | copy-start | bytes 2359300
  5.8 72.7 %copy-start.19 = (s32[512]{0:T(512)S(1)}, s32[512]{0:T(512)}, u32[]{:S(2)}) copy-start(s32[512]{0:T(512)} %param.16) | copy-start | bytes 6148
  5.8 72.7 %copy-start.20 = (s32[4,3]{1,0:T(4,128)S(1)}, s32[4,3]{1,0:T(4,128)}, u32[]{:S(2)}) copy-start(s32[4,3]{1,0:T(4,128)} %seg_ref.1) | copy-start | bytes 148
  5.8 72.7 %copy-start.21 = (s32[4,3]{1,0:T(4,128)S(1)}, s32[4,3]{1,0:T(4,128)}, u32[]{:S(2)}) copy-start(s32[4,3]{1,0:T(4,128)} %dil_ref.1) | copy-start | bytes 148
  7.3 5.7 %collective-permute-start = (bf16[208,128]{1,0:T(8,128)(2,1)S(1)}, bf16[208,128]{1,0:T(8,128)(2,1)S(1)}, u32[]{:S(2)}, u32[]{:S(2)}) collective-permute-start(bf16[208,128]{1,0:T(8,128)(2,1)S(1)} %get-tuple-element.53), channel_id=1, source_target_pairs={{0,4},{4,0},{8,12},{12,8},{16,20},{20,16},{24,28},{28,24},{32,36},... | collective-permute-start | bytes 159752 | tf_op jit(solution)/shard_map/ppermute | solution.py:589
  10.4 4.1 %collective-permute-start.1 = (bf16[208,128]{1,0:T(8,128)(2,1)S(1)}, bf16[208,128]{1,0:T(8,128)(2,1)S(1)}, u32[]{:S(2)}, u32[]{:S(2)}) collective-permute-start(bf16[208,128]{1,0:T(8,128)(2,1)S(1)} %get-tuple-element.54), channel_id=1, source_target_pairs={{0,8},{4,12},{8,0},{12,4},{16,24},{20,28},{24,16},{28,20},{32,40},... | collective-permute-start | bytes 159752 | tf_op jit(solution)/shard_map/ppermute | solution.py:589
  10.5 6.5 %collective-permute-start.2 = (bf16[208,128]{1,0:T(8,128)(2,1)S(1)}, bf16[208,128]{1,0:T(8,128)(2,1)S(1)}, u32[]{:S(2)}, u32[]{:S(2)}) collective-permute-start(bf16[208,128]{1,0:T(8,128)(2,1)S(1)} %get-tuple-element.55), channel_id=1, source_target_pairs={{0,12},{4,8},{8,4},{12,0},{16,28},{20,24},{24,20},{28,16},{32,44},... | collective-permute-start | bytes 159752 | tf_op jit(solution)/shard_map/ppermute | solution.py:589
  17.7 0.7 copy-start.12
  18.4 20.9 %copy-start.10 = (f32[4,192,128]{2,1,0:T(8,128)}, f32[4,192,128]{2,1,0:T(8,128)S(1)}, u32[]{:S(2)}) copy-start(f32[4,192,128]{2,1,0:T(8,128)S(1)} %get-tuple-element.86.block_before) | copy-start | bytes 1179652
  18.4 9.0 %collective-permute-start.3 = (bf16[208,128]{1,0:T(8,128)(2,1)S(1)}, bf16[208,128]{1,0:T(8,128)(2,1)S(1)}, u32[]{:S(2)}, u32[]{:S(2)}) collective-permute-start(bf16[208,128]{1,0:T(8,128)(2,1)S(1)} %get-tuple-element.61.a0), channel_id=1, source_target_pairs={{0,16},{4,20},{8,24},{12,28},{16,32},{20,36},{24,40},{28,44},{32,4... | collective-permute-start | bytes 159752 | tf_op jit(solution)/shard_map/ppermute | solution.py:594
  21.7 82.8 %collective-permute-start.9 = (bf16[528,768]{1,0:T(8,128)(2,1)}, bf16[528,768]{1,0:T(8,128)(2,1)}, u32[]{:S(2)}, u32[]{:S(2)}) collective-permute-start(bf16[528,768]{1,0:T(8,128)(2,1)} %pack.1), channel_id=1, source_target_pairs={{0,4},{4,0},{8,12},{12,8},{16,20},{20,16},{24,28},{28,24},{32,36},... | collective-permute-start | bytes 2433032 | tf_op jit(solution)/shard_map/ppermute | solution.py:589
  27.4 77.1 %collective-permute-start.10 = (bf16[528,768]{1,0:T(8,128)(2,1)}, bf16[528,768]{1,0:T(8,128)(2,1)}, u32[]{:S(2)}, u32[]{:S(2)}) collective-permute-start(bf16[528,768]{1,0:T(8,128)(2,1)} %pack.1), channel_id=1, source_target_pairs={{0,8},{4,12},{8,0},{12,4},{16,24},{20,28},{24,16},{28,20},{32,40},... | collective-permute-start | bytes 2433032 | tf_op jit(solution)/shard_map/ppermute | solution.py:589
  28.0 76.5 %collective-permute-start.11 = (bf16[528,768]{1,0:T(8,128)(2,1)}, bf16[528,768]{1,0:T(8,128)(2,1)}, u32[]{:S(2)}, u32[]{:S(2)}) collective-permute-start(bf16[528,768]{1,0:T(8,128)(2,1)} %pack.1), channel_id=1, source_target_pairs={{0,12},{4,8},{8,4},{12,0},{16,28},{20,24},{24,20},{28,16},{32,44},... | collective-permute-start | bytes 2433032 | tf_op jit(solution)/shard_map/ppermute | solution.py:589
  29.4 40.6 %collective-permute-start.4 = (bf16[208,128]{1,0:T(8,128)(2,1)S(1)}, bf16[208,128]{1,0:T(8,128)(2,1)S(1)}, u32[]{:S(2)}, u32[]{:S(2)}) collective-permute-start(bf16[208,128]{1,0:T(8,128)(2,1)S(1)} %get-tuple-element.61.a0), channel_id=1, source_target_pairs={{0,32},{4,36},{8,40},{12,44},{16,48},{20,52},{24,56},{28,60},{32,0... | collective-permute-start | bytes 159752 | tf_op jit(solution)/shard_map/ppermute | solution.py:594
  34.4 35.6 %collective-permute-start.5 = (bf16[208,128]{1,0:T(8,128)(2,1)S(1)}, bf16[208,128]{1,0:T(8,128)(2,1)S(1)}, u32[]{:S(2)}, u32[]{:S(2)}) collective-permute-start(bf16[208,128]{1,0:T(8,128)(2,1)S(1)} %get-tuple-element.61.a0), channel_id=1, source_target_pairs={{0,48},{4,52},{8,56},{12,60},{16,0},{20,4},{24,8},{28,12},{32,16},... | collective-permute-start | bytes 159752 | tf_op jit(solution)/shard_map/ppermute | solution.py:594
  39.4 1.2 %copy-start.4 = (f32[512,768]{1,0:T(8,128)}, f32[512,768]{1,0:T(8,128)S(1)}, u32[]{:S(2)}) copy-start(f32[512,768]{1,0:T(8,128)S(1)} %get-tuple-element.93.lift_ref) | copy-start | bytes 4718596
  70.6 5.4 %collective-permute-start.6 = (bf16[208,128]{1,0:T(8,128)(2,1)S(1)}, bf16[208,128]{1,0:T(8,128)(2,1)S(1)}, u32[]{:S(2)}, u32[]{:S(2)}) collective-permute-start(bf16[208,128]{1,0:T(8,128)(2,1)S(1)} %get-tuple-element.80.a0), channel_id=1, source_target_pairs={{0,64},{4,68},{8,72},{12,76},{16,80},{20,84},{24,88},{28,92},{32,9... | collective-permute-start | bytes 159752 | tf_op jit(solution)/shard_map/ppermute | solution.py:594
  72.3 15.2 %collective-permute-start.7 = (bf16[208,128]{1,0:T(8,128)(2,1)S(1)}, bf16[208,128]{1,0:T(8,128)(2,1)}, u32[]{:S(2)}, u32[]{:S(2)}) collective-permute-start(bf16[208,128]{1,0:T(8,128)(2,1)S(1)} %get-tuple-element.80.a0), channel_id=1, source_target_pairs={{0,128},{4,132},{8,136},{12,140},{16,144},{20,148},{24,152},{28,15... | collective-permute-start | bytes 159752 | tf_op jit(solution)/shard_map/ppermute | solution.py:594
  76.0 0.6 copy-start.16
  76.6 10.8 %collective-permute-start.8 = (bf16[208,128]{1,0:T(8,128)(2,1)S(1)}, bf16[208,128]{1,0:T(8,128)(2,1)}, u32[]{:S(2)}, u32[]{:S(2)}) collective-permute-start(bf16[208,128]{1,0:T(8,128)(2,1)S(1)} %get-tuple-element.80.a0), channel_id=1, source_target_pairs={{0,192},{4,196},{8,200},{12,204},{16,208},{20,212},{24,216},{28,22... | collective-permute-start | bytes 159752 | tf_op jit(solution)/shard_map/ppermute | solution.py:594
  78.5 1.1 copy-start.7
  79.6 7.8 %copy-start.11 = (f32[4,192,128]{2,1,0:T(8,128)S(1)}, f32[4,192,128]{2,1,0:T(8,128)}, u32[]{:S(2)}) copy-start(f32[4,192,128]{2,1,0:T(8,128)} %copy-done.10) | copy-start | bytes 1179652
  79.6 7.8 %copy-start.13 = (f32[4,192,128]{2,1,0:T(8,128)S(1)}, f32[4,192,128]{2,1,0:T(8,128)}, u32[]{:S(2)}) copy-start(f32[4,192,128]{2,1,0:T(8,128)} %copy-done.12) | copy-start | bytes 1179652
  79.6 15.3 %copy-start.23 = (f32[768]{0:T(1024)S(1)}, f32[768]{0:T(1024)}, u32[]{:S(2)}) copy-start(f32[768]{0:T(1024)} %param.25) | copy-start | bytes 9220
  79.6 21.8 %copy-start.5 = (f32[512,768]{1,0:T(8,128)S(1)}, f32[512,768]{1,0:T(8,128)}, u32[]{:S(2)}) copy-start(f32[512,768]{1,0:T(8,128)} %copy-done.4) | copy-start | bytes 4718596
  87.4 0.8 copy-start.17
  89.2 5.7 %collective-permute-start.12 = (bf16[192,128]{1,0:T(8,128)(2,1)S(1)}, bf16[192,128]{1,0:T(8,128)(2,1)S(1)}, u32[]{:S(2)}, u32[]{:S(2)}) collective-permute-start(bf16[192,128]{1,0:T(8,128)(2,1)S(1)} %get-tuple-element.89), channel_id=1, source_target_pairs={{0,4},{4,0},{8,12},{12,8},{16,20},{20,16},{24,28},{28,24},{32,36},... | collective-permute-start | bytes 147464 | tf_op jit(solution)/shard_map/ppermute | solution.py:589
  89.4 5.6 %collective-permute-start.13 = (bf16[192,128]{1,0:T(8,128)(2,1)S(1)}, bf16[192,128]{1,0:T(8,128)(2,1)S(1)}, u32[]{:S(2)}, u32[]{:S(2)}) collective-permute-start(bf16[192,128]{1,0:T(8,128)(2,1)S(1)} %get-tuple-element.90), channel_id=1, source_target_pairs={{0,8},{4,12},{8,0},{12,4},{16,24},{20,28},{24,16},{28,20},{32,40},... | collective-permute-start | bytes 147464 | tf_op jit(solution)/shard_map/ppermute | solution.py:589
  94.9 6.5 %collective-permute-start.14 = (bf16[192,128]{1,0:T(8,128)(2,1)S(1)}, bf16[192,128]{1,0:T(8,128)(2,1)S(1)}, u32[]{:S(2)}, u32[]{:S(2)}) collective-permute-start(bf16[192,128]{1,0:T(8,128)(2,1)S(1)} %get-tuple-element.91), channel_id=1, source_target_pairs={{0,12},{4,8},{8,4},{12,0},{16,28},{20,24},{24,20},{28,16},{32,44},... | collective-permute-start | bytes 147464 | tf_op jit(solution)/shard_map/ppermute | solution.py:589

commit v3 on v2

--- a/solution.py
+++ b/solution.py
@@ -78,7 +78,10 @@
     return out
 
 
-def params(mib=14):
+FREE = pl.CostEstimate(flops=1, bytes_accessed=1, transcendentals=0)
+
+
+def params(mib=8):
     return pltpu.CompilerParams(vmem_limit_bytes=mib * 1024 * 1024)
 
 
@@ -215,22 +218,18 @@
         stat_ref[pair * 8 : pair * 8 + 8, :] = jnp.concatenate(stats + [jnp.zeros((4, HALF), F32)], axis=0)
 
 
-def remote_kernel(
-    qe_ref, plan_ref, oe_ref, stat_ref, oo_ref, ve_ref, kv1_ref, kv2_ref, kv3_ref,
-    out_ref, rows_ref,
-):
-    blocks = (kv1_ref, kv2_ref, kv3_ref)
+def remote_kernel(near, qe_ref, plan_ref, oe_ref, stat_ref, oo_ref, ve_ref, *rest):
+    blocks, outs = (rest[:1], rest[1:]) if near else (rest[:2], rest[2:])
     spread = one((iota((16, 128), 0) == 0) & (iota((16, 128), 1) == 16), BF16)
     row, lane = iota((HALF, 128), 0), iota((HALF, 128), 1)
+    wanted = ((lane & 3) == (row >> 6)) & (lane < 16)
+    wanted = one(wanted & (lane < 8) if near else wanted & (lane >= 8))
     sides = []
     for parity in range(2):
         pieces = []
-        for at, ref in enumerate(blocks):
+        for ref in blocks:
             flags = ref[ROWS : ROWS + 16, parity * HALF : (parity + 1) * HALF].astype(F32)
-            line = ((1.0 - flags) * NEG).astype(BF16)
-            wanted = (lane & 3) == (row >> 6)
-            wanted = wanted & (lane < 8) if at == 0 else wanted & (lane >= 8) & (lane < 16)
-            pieces.append(t_dot(line, spread) + one(wanted))
+            pieces.append(t_dot(((1.0 - flags) * NEG).astype(BF16), spread) + wanted)
         sides.append(jnp.concatenate(pieces, axis=0).astype(BF16))
     for pair in range(PAIRS):
         both = slice(pair * 128, (pair + 1) * 128)
@@ -238,6 +237,7 @@
         chunk = slice((pair >> 1) * HALF, (pair >> 1) * HALF + HALF)
         key = jnp.concatenate([ref[:HALF, both] for ref in blocks], axis=0)
         value = jnp.concatenate([ref[place, chunk] for ref in blocks], axis=1)
+        stats = []
         for part in range(2):
             start = pair * 128 + part * HEAD_DIM
             now = slice(start, start + HEAD_DIM)
@@ -252,14 +252,40 @@
             rescale = jnp.exp(before - top)
             out = out + oe_ref[now, :] * rescale
             total = total + stat_ref[stat + 1 : stat + 2, :] * rescale
+            if near:
+                outs[0][now, :] = out
+                stats += [top, total]
+                continue
             done = out / total * ve_ref[:1, part * HALF : (part + 1) * HALF]
-            rows_ref[now, part * HALF : (part + 1) * HALF] = done.astype(BF16)
-            rows_ref[now, (1 - part) * HALF : (2 - part) * HALF] = oo_ref[now, :]
-    out_ref[...] = dot_t(unsorting(), rows_ref[...]).astype(BF16)
-
-
-def state_kernel(v_ref, steps_ref, rates_ref, valid_ref, into_ref, place_ref, *out_refs):
-    full_ref = out_refs[4]
+            outs[1][now, part * HALF : (part + 1) * HALF] = done.astype(BF16)
+            outs[1][now, (1 - part) * HALF : (2 - part) * HALF] = oo_ref[now, :]
+        if near:
+            outs[1][pair * 8 : pair * 8 + 8, :] = jnp.concatenate(
+                stats + [jnp.zeros((4, HALF), F32)], axis=0
+            )
+    if not near:
+        outs[0][...] = dot_t(unsorting(), outs[1][...]).astype(BF16)
+
+
+def state_kernel(v_hbm, steps_hbm, rates_hbm, valid_hbm, into_hbm, place_ref, *rest):
+    out_refs = rest[:4]
+    full_ref, v_ref, steps_ref, rates_ref, valid_ref, into_ref, arrived = rest[4:]
+    copies = [
+        pltpu.make_async_copy(source, target, arrived.at[at])
+        for at, (source, target) in enumerate(
+            (
+                (rates_hbm, rates_ref),
+                (steps_hbm, steps_ref),
+                (valid_hbm, valid_ref),
+                (into_hbm, into_ref),
+                (v_hbm, v_ref),
+            )
+        )
+    ]
+    for copy in copies:
+        copy.start()
+    for copy in copies[:3]:
+        copy.wait()
     later = one(iota((ROWS, ROWS), 0) > iota((ROWS, ROWS), 1), BF16)
     rates = jnp.concatenate([rates_ref[...], jnp.zeros((4, ROWS), F32)], axis=0)
     sums = dot(jnp.concatenate(split(rates, 3), axis=0), later)
@@ -269,6 +295,8 @@
     width = HEADS_HERE * HEAD_DIM
     spread = one((iota((32, width), 0) & 15) == (iota((32, width), 1) >> 6), BF16)
     scale = t_dot(jnp.concatenate(split(weight, 2), axis=0), spread)
+    for copy in copies[3:]:
+        copy.wait()
     driven = (v_ref[...].astype(F32) * scale).astype(BF16)
     full_ref[...] = t_dot(driven, into_ref[...])
     decay = jnp.exp(-jnp.sum(rates, axis=1, keepdims=True))
@@ -287,6 +315,10 @@
     return [tail[k : k + 1] + tail[k + 3 : k + 4] for k in range(3)]
 
 
+def tall(decays):
+    return jnp.concatenate(decays + [jnp.zeros((5, STATE), F32)], axis=0)
+
+
 def spread_rows(decays):
     return jnp.concatenate([jnp.broadcast_to(d, (HEAD_DIM, STATE)) for d in decays], axis=0)
 
@@ -306,7 +338,7 @@
     decays = [jnp.ones((1, STATE), F32)] * 3
     for at in range(4):
         before_ref[at] = state
-        fade_ref[at] = spread_rows(decays)
+        fade_ref[at] = tall(decays)
         now = decay_rows(held[at])
         state = state * spread_rows(now) + held[at, :QUARTER, :]
         decays = [a * b for a, b in zip(decays, now)]
@@ -332,7 +364,7 @@
         held[(place_ref[1] - step) & 3] = ref[...].astype(F32)
     before, before_decays, state, decays = chain(place_ref[1], held)
     before_ref[...] = before
-    fade_ref[...] = spread_rows(before_decays)
+    fade_ref[...] = tall(before_decays)
     total_ref[...] = pack_piece(state, decays)
 
 
@@ -341,19 +373,22 @@
     for step, ref in enumerate((a0, a1, a2, a3)):
         held[(place_ref[2] - step) & 3] = ref[...].astype(F32)
     before = chain(place_ref[2], held)[0]
-    start = line_fade[...] * before + line_before[...]
+    start = spread_rows([line_fade[k : k + 1, :] for k in range(3)]) * before + line_before[...]
     for step in range(4):
         part = place_ref[0] ^ step
-        outs[step][...] = (block_fade[part] * start + block_before[part]).astype(BF16)
+        fade = block_fade[part]
+        fade = spread_rows([fade[k : k + 1] for k in range(3)])
+        outs[step][...] = (fade * start + block_before[part]).astype(BF16)
 
 
 def within_kernel(
+    first,
     v_ref, gate_ref, steps_ref, rates_ref, valid_ref, into_ref, read_ref, skip_ref,
     base_ref, lift_ref, couple_ref, col_ref, row_ref,
 ):
-    pair = pl.program_id(0)
-
-    @pl.when(pair == 0)
+    pair = pl.program_id(0) + first
+
+    @pl.when(pl.program_id(0) == 0)
     def _():
         couple_ref[...] = dot_t(read_ref[...], into_ref[...])
         upto = one(iota((ROWS, ROWS), 0) <= iota((ROWS, ROWS), 1), BF16)
@@ -396,11 +431,13 @@
     gate = gate / (1.0 + jnp.exp(-gate))
     skip = jnp.where(low, skip_ref[2 * pair], skip_ref[2 * pair + 1])
     within = jnp.where(low, results[0], results[1])
-    base_ref[...] = (within + skip * value.astype(F32)) * gate
-    lift_ref[...] = jnp.exp(jnp.where(low, falls[0], falls[1])) * gate
-
-
-def finish_kernel(place_ref, f0, f1, f2, f3, read_ref, base_ref, lift_ref, gain_ref, out_ref, held):
+    base_ref[...] = ((within + skip * value.astype(F32)) * gate).astype(BF16)
+    lift_ref[...] = (jnp.exp(jnp.where(low, falls[0], falls[1])) * gate).astype(BF16)
+
+
+def finish_kernel(place_ref, f0, f1, f2, f3, read_ref, *rest):
+    gain_ref, out_ref, held = rest[4:]
+
     @pl.when(pl.program_id(0) == 0)
     def _():
         for step, ref in enumerate((f0, f1, f2, f3)):
@@ -410,8 +447,10 @@
     together = one((iota((128, 128), 0) >> 6) == (iota((128, 128), 1) >> 6), BF16)
     for pair in range(PAIRS):
         now = slice(pair * 128, (pair + 1) * 128)
+        half = slice(pair % 3 * 128, (pair % 3 + 1) * 128)
+        base_ref, lift_ref = rest[pair // 3 * 2 : pair // 3 * 2 + 2]
         carried = dot_t(read_ref[...], held[now, :])
-        gated = base_ref[:, now] + lift_ref[:, now] * carried
+        gated = base_ref[:, half].astype(F32) + lift_ref[:, half].astype(F32) * carried
         high, low = split(gated * gated, 2)
         mean = (dot(high, together) + dot(low, together)) * (1.0 / HEAD_DIM)
         out_ref[:, now] = (gated * lax.rsqrt(mean + 1e-05) * gain_ref[:, now]).astype(BF16)
@@ -435,18 +474,29 @@
         out_shape=shape(ROWS + 16, WIDTH),
         in_specs=[VMEM] * 3,
         out_specs=VMEM,
+        cost_estimate=FREE,
         compiler_params=params(),
         name="pack",
     )(key_rows, value_rows, valid)
 
 
 def call_state(*args):
+    far = pl.BlockSpec(memory_space=pltpu.HBM)
     return pl.pallas_call(
         state_kernel,
         out_shape=[shape(PIECE, STATE)] * 4,
-        in_specs=[VMEM] * 5 + [SMEM],
+        in_specs=[far] * 5 + [SMEM],
         out_specs=[VMEM] * 4,
-        scratch_shapes=[pltpu.VMEM((WIDTH, STATE), F32)],
+        scratch_shapes=[
+            pltpu.VMEM((WIDTH, STATE), F32),
+            pltpu.VMEM((ROWS, WIDTH), BF16),
+            pltpu.VMEM((HEADS_HERE, ROWS), F32),
+            pltpu.VMEM((HEADS_HERE, ROWS), F32),
+            pltpu.VMEM((1, ROWS), jnp.int32),
+            pltpu.VMEM((ROWS, STATE), BF16),
+            pltpu.SemaphoreType.DMA((5,)),
+        ],
+        cost_estimate=FREE,
         compiler_params=params(),
         name="state",
     )(*args)
@@ -458,10 +508,11 @@
 def call_block(place, *pieces):
     return pl.pallas_call(
         block_kernel,
-        out_shape=[shape(PIECE, STATE), shape(4, QUARTER, STATE, kind=F32), shape(4, QUARTER, STATE, kind=F32)],
+        out_shape=[shape(PIECE, STATE), shape(4, QUARTER, STATE, kind=F32), shape(4, 8, STATE, kind=F32)],
         in_specs=[SMEM] + [VMEM] * 4,
         out_specs=[VMEM] * 3,
         scratch_shapes=HOLD,
+        cost_estimate=FREE,
         compiler_params=params(),
         name="block",
     )(place, *pieces)
@@ -470,10 +521,11 @@
 def call_line(place, *totals):
     return pl.pallas_call(
         line_kernel,
-        out_shape=[shape(PIECE, STATE), shape(QUARTER, STATE, kind=F32), shape(QUARTER, STATE, kind=F32)],
+        out_shape=[shape(PIECE, STATE), shape(QUARTER, STATE, kind=F32), shape(8, STATE, kind=F32)],
         in_specs=[SMEM] + [VMEM] * 4,
         out_specs=[VMEM] * 3,
         scratch_shapes=HOLD,
+        cost_estimate=FREE,
         compiler_params=params(),
         name="line",
     )(place, *totals)
@@ -486,6 +538,7 @@
         in_specs=[SMEM] + [VMEM] * 8,
         out_specs=[VMEM] * 4,
         scratch_shapes=HOLD,
+        cost_estimate=FREE,
         compiler_params=params(),
         name="plane",
     )(place, *args)
@@ -513,22 +566,27 @@
             pltpu.VMEM((WIDTH, ROWS), F32),
             pltpu.VMEM((WIDTH, ROWS), BF16),
         ],
-        compiler_params=params(24),
+        cost_estimate=FREE,
+        compiler_params=params(14),
         name="local",
     )(*args)
 
 
-def call_within(*args):
-    return pl.pallas_call(
-        within_kernel,
-        grid=(PAIRS,),
-        out_shape=[shape(ROWS, WIDTH, kind=F32)] * 2,
-        in_specs=[lanes(ROWS)] * 2
+def call_within(first, *args):
+    def columns(rows):
+        return pl.BlockSpec((rows, 128), lambda pair: (0, first + pair))
+
+    return pl.pallas_call(
+        functools.partial(within_kernel, first),
+        grid=(PAIRS // 2,),
+        out_shape=[shape(ROWS, WIDTH // 2)] * 2,
+        in_specs=[columns(ROWS)] * 2
         + [whole(HEADS_HERE, ROWS)] * 2
         + [whole(1, ROWS), whole(ROWS, STATE), whole(ROWS, STATE), SMEM],
         out_specs=[lanes(ROWS)] * 2,
         scratch_shapes=[pltpu.VMEM((ROWS, ROWS), F32), pltpu.VMEM((16, ROWS), F32), pltpu.VMEM((16, ROWS), F32)],
-        compiler_params=params(),
+        cost_estimate=FREE,
+        compiler_params=params(8),
         name="within",
     )(*args)
 
@@ -543,22 +601,39 @@
         out_shape=shape(ROWS, WIDTH),
         in_specs=[SMEM]
         + [whole(QUARTER, STATE)] * 4
-        + [rows(STATE), rows(WIDTH), rows(WIDTH), whole(1, WIDTH)],
+        + [rows(STATE)]
+        + [rows(WIDTH // 2)] * 4
+        + [whole(1, WIDTH)],
         out_specs=rows(WIDTH),
         scratch_shapes=[pltpu.VMEM((WIDTH, STATE), BF16)],
+        cost_estimate=FREE,
         compiler_params=params(),
         name="finish",
     )(*args)
 
 
+def call_near(kept, arrived):
+    out, stat = pl.pallas_call(
+        functools.partial(remote_kernel, True),
+        out_shape=[KEPT[2], KEPT[3]],
+        in_specs=[VMEM] * 7,
+        out_specs=[VMEM] * 2,
+        cost_estimate=FREE,
+        compiler_params=params(14),
+        name="near",
+    )(*kept, arrived)
+    return [kept[0], kept[1], out, stat, kept[4], kept[5]]
+
+
 def call_remote(kept, arrived):
     return pl.pallas_call(
-        remote_kernel,
+        functools.partial(remote_kernel, False),
         out_shape=shape(ROWS, WIDTH),
-        in_specs=[VMEM] * 9,
+        in_specs=[VMEM] * 8,
         out_specs=VMEM,
         scratch_shapes=[pltpu.VMEM((WIDTH, ROWS), BF16)],
-        compiler_params=params(24),
+        cost_estimate=FREE,
+        compiler_params=params(14),
         name="remote",
     )(*kept, *arrived)
 
@@ -594,28 +669,34 @@
         return lax.ppermute(block, "seq", route)
 
     after = lax.optimization_barrier
-
-    pieces = call_state(value_rows, step_sizes, decay_rates, valid, state_in, place)
-    packed, pieces = after((call_pack(key_rows, value_rows, valid), pieces))
+    scan_inputs = (step_sizes, decay_rates, valid, state_in)
+
+    pieces = call_state(value_rows, *scan_inputs, place)
+    packed = call_pack(key_rows, value_rows, after((valid, pieces))[0])
     pieces = [pieces[0]] + [cross(pieces[mask], mask) for mask in range(1, SPAN_DEV)]
     near = cross(packed, 1)
+    pieces = after((pieces, packed))[0]
     total, block_before, block_fade = call_block(place, *pieces)
     totals = [total] + [turn(total, step, 16) for step in range(1, 4)]
-    packed, totals[1] = after((packed, totals[1]))
-    arrived = [near] + [cross(packed, mask) for mask in range(2, SPAN_DEV)]
-    base, lift = call_within(
-        value_rows, gate_in, step_sizes, decay_rates, after((valid, total))[0], state_in, state_out, skip_weight
-    )
-    totals, base = after((totals, base))
+    halves = list(scan_inputs)
+    halves[2] = after((valid, total))[0]
+    first = call_within(0, value_rows, gate_in, *halves, state_out, skip_weight)
+    totals = after((totals, first))[0]
+    packed, totals = after((packed, totals))
+    arrived = [cross(packed, mask) for mask in range(2, SPAN_DEV)]
     total, line_before, line_fade = call_line(place, *totals)
     kept = call_local(
         query_rows, key_rows, value_rows, after((valid, total))[0], segment_lengths, dilation, rank
     )
     totals = [total] + [turn(total, step, 64) for step in range(1, 4)]
-    totals, kept = after((totals, kept))
+    totals = after((totals, kept))[0]
     carried = call_plane(place, *totals, line_before, line_fade, block_before, block_fade)
+    halves[2] = after((valid, carried))[0]
+    second = call_within(3, value_rows, gate_in, *halves, state_out, skip_weight)
     carried = [carried[0]] + [cross(carried[mask], mask) for mask in range(1, SPAN_DEV)]
-    scanned = call_finish(place, *carried, state_out, base, lift, gain)
+    kept = call_near(after((kept, second))[0], near)
+    carried = after((carried, kept))[0]
+    scanned = call_finish(place, *carried, state_out, *first, *second, gain)
     attended = call_remote(kept, arrived)
     return (attended, scanned)
 

time: 114 us -> 85.4 us (0.75)
  the two profiles are of different devices: /device:TPU:32 before, /device:TPU:16 now
where the time goes in v3:
time: 85.4 us; the launch traced here: 84.9 us
  Pallas kernels  34.2 us (40%)
  starting transfers between devices  28.1 us (33%)
  waiting for transfers between devices  12.3 us (14%)
  local copies, waits for them, and re-layouts  9.4 us (11%)
  between operations  0.86 us (1%)
    ppermute x9, starting transfers between devices, cross(): return lax.ppermute(block, 'seq', [(i, i ^ mask) for i in range(count)])  15.2 us
    ppermute x6, starting transfers between devices, turn(): return lax.ppermute(block, 'seq', route)  12.9 us
    ppermute x9, waiting for transfers between devices, cross(): return lax.ppermute(block, 'seq', [(i, i ^ mask) for i in range(count)])  10 us
    unnamed x48, local copies, waits for them, and re-layouts  9.4 us
    pallas_call x1, Pallas kernels, call_local(): pl.pallas_call(local_kernel, out_shape=KEPT, in_specs=[VMEM] * 4 + [SMEM]...  7.78 us
    pallas_call x1, Pallas kernels, call_remote(): pl.pallas_call(functools.partial(remote_kernel, False), out_shape=shape(R...  7.64 us
    pallas_call x2, Pallas kernels, call_within(): pl.pallas_call(functools.partial(within_kernel, first), grid=(PAIRS // 2,...  5.55 us
    pallas_call x1, Pallas kernels, call_near(): pl.pallas_call(functools.partial(remote_kernel, True), out_shape=[KEPT[2]...  4.69 us
  transfers between devices with their start and end apart: 15, of which 6 were waited for; matrix products, arithmetic and copies ran while one was open for 0% of the time, Pallas kernels for 28%

profile of v3, /device:TPU:16, one launch (start us, length us, event | category | flops | bytes accessed | tf_op | source)
XLA Modules:
  0.0 84.9 jit_solution(12834431473849755708)
XLA Ops:
  0.6 0.1 pad_add_fusion.place_ref
  0.7 0.6 copy-done.19
  1.3 1.1 %copy-done = bf16[512,768]{1,0:T(8,128)(2,1)S(1)} copy-done((bf16[512,768]{1,0:T(8,128)(2,1)S(1)}, bf16[512,768]{1,0:T(8,128)(2,1)}, u32[]{:S(2)}) %copy-start) | copy-done | bytes 786456
  2.5 0.9 %copy-done.5 = bf16[512,128]{1,0:T(8,128)(2,1)S(1)} copy-done((bf16[512,128]{1,0:T(8,128)(2,1)S(1)}, bf16[512,128]{1,0:T(8,128)(2,1)}, u32[]{:S(2)}) %copy-start.5) | copy-done | bytes 131096
  3.4 0.8 copy-done.15
  4.1 0.8 copy-done.17
  4.9 2.0 %state.1 = (bf16[208,128]{1,0:T(8,128)(2,1)S(1)}, bf16[208,128]{1,0:T(8,128)(2,1)S(1)}, bf16[208,128]{1,0:T(8,128)(2,1)S(1)}, bf16[208,128]{1,0:T(8,128)(2,1)S(1)}) custom-call(bf16[512,768]{1,0:T(8,128)(2,1)S(1)} %copy-done, f32[12,512]{1,0:T(8,128)S(1)} %copy-done.15, f32[12,512]{1,0:T(8,128)S(1)} %copy-done.17, s32[1,512]{1,0:T(1,128)S(1)} %bitcast.5, ...), custom_call_target="tpu_custom_call" | custom-call | flops 1 | bytes 1 | tf_op jit(solution)/shard_map/state/pallas_call | solution.py:485
  6.9 3.1 %collective-permute-start = (bf16[208,128]{1,0:T(8,128)(2,1)S(1)}, bf16[208,128]{1,0:T(8,128)(2,1)S(1)}, u32[]{:S(2)}, u32[]{:S(2)}) collective-permute-start(bf16[208,128]{1,0:T(8,128)(2,1)S(1)} %get-tuple-element.60), channel_id=1, source_target_pairs={{0,4},{4,0},{8,12},{12,8},{16,20},{20,16},{24,28},{28,24},{32,36},... | collective-permute-start | bytes 159752 | tf_op jit(solution)/shard_map/ppermute | solution.py:664
  10.0 1.9 %collective-permute-start.1 = (bf16[208,128]{1,0:T(8,128)(2,1)S(1)}, bf16[208,128]{1,0:T(8,128)(2,1)S(1)}, u32[]{:S(2)}, u32[]{:S(2)}) collective-permute-start(bf16[208,128]{1,0:T(8,128)(2,1)S(1)} %get-tuple-element.61), channel_id=1, source_target_pairs={{0,8},{4,12},{8,0},{12,4},{16,24},{20,28},{24,16},{28,20},{32,40},... | collective-permute-start | bytes 159752 | tf_op jit(solution)/shard_map/ppermute | solution.py:664
  11.9 0.1 collective-permute-start.2
  12.0 1.1 %copy-done.3 = bf16[512,768]{1,0:T(8,128)(2,1)S(1)} copy-done((bf16[512,768]{1,0:T(8,128)(2,1)S(1)}, bf16[512,768]{1,0:T(8,128)(2,1)}, u32[]{:S(2)}) %copy-start.3) | copy-done | bytes 786456
  13.1 1.1 %pack.1 = bf16[528,768]{1,0:T(8,128)(2,1)S(1)} custom-call(bf16[512,768]{1,0:T(8,128)(2,1)S(1)} %copy-done.3, bf16[512,768]{1,0:T(8,128)(2,1)S(1)} %copy-done.1, s32[1,512]{1,0:T(1,128)S(1)} %bitcast.6), custom_call_target="tpu_custom_call" | custom-call | flops 1 | bytes 1 | tf_op jit(solution)/shard_map/pack/pallas_call | solution.py:472
  14.3 0.0 copy-start.7
  14.3 0.3 collective-permute-done.1.a2
  14.6 3.9 %collective-permute-done.2.a3 = bf16[208,128]{1,0:T(8,128)(2,1)S(1)} collective-permute-done((bf16[208,128]{1,0:T(8,128)(2,1)S(1)}, bf16[208,128]{1,0:T(8,128)(2,1)S(1)}, u32[]{:S(2)}, u32[]{:S(2)}) %collective-permute-start.2) | collective-permute-done | bytes 53280 | tf_op jit(solution)/shard_map/ppermute | solution.py:664
  18.5 0.6 block.1
  19.1 0.7 copy-done.13
  19.9 3.3 %collective-permute-start.3 = (bf16[208,128]{1,0:T(8,128)(2,1)S(1)}, bf16[208,128]{1,0:T(8,128)(2,1)S(1)}, u32[]{:S(2)}, u32[]{:S(2)}) collective-permute-start(bf16[208,128]{1,0:T(8,128)(2,1)S(1)} %get-tuple-element.76.a0), channel_id=1, source_target_pairs={{0,16},{4,20},{8,24},{12,28},{16,32},{20,36},{24,40},{28,44},{32,4... | collective-permute-start | bytes 159752 | tf_op jit(solution)/shard_map/ppermute | solution.py:669
  23.1 4.5 %collective-permute-start.4 = (bf16[208,128]{1,0:T(8,128)(2,1)S(1)}, bf16[208,128]{1,0:T(8,128)(2,1)S(1)}, u32[]{:S(2)}, u32[]{:S(2)}) collective-permute-start(bf16[208,128]{1,0:T(8,128)(2,1)S(1)} %get-tuple-element.76.a0), channel_id=1, source_target_pairs={{0,32},{4,36},{8,40},{12,44},{16,48},{20,52},{24,56},{28,60},{32,0... | collective-permute-start | bytes 159752 | tf_op jit(solution)/shard_map/ppermute | solution.py:669
  27.6 2.7 %collective-permute-start.5 = (bf16[208,128]{1,0:T(8,128)(2,1)S(1)}, bf16[208,128]{1,0:T(8,128)(2,1)S(1)}, u32[]{:S(2)}, u32[]{:S(2)}) collective-permute-start(bf16[208,128]{1,0:T(8,128)(2,1)S(1)} %get-tuple-element.76.a0), channel_id=1, source_target_pairs={{0,48},{4,52},{8,56},{12,60},{16,0},{20,4},{24,8},{28,12},{32,16},... | collective-permute-start | bytes 159752 | tf_op jit(solution)/shard_map/ppermute | solution.py:669
  30.3 0.5 collective-permute-start.9
  30.8 2.8 %within.2 = (bf16[512,384]{1,0:T(8,128)(2,1)S(1)}, bf16[512,384]{1,0:T(8,128)(2,1)S(1)}) custom-call(bf16[512,768]{1,0:T(8,128)(2,1)S(1)} %copy-done.1, bf16[512,768]{1,0:T(8,128)(2,1)S(1)} %copy-done.2, f32[12,512]{1,0:T(8,128)S(1)} %copy-done.15, f32[12,512]{1,0:T(8,128)S(1)} %copy-done.17, s32[1,512]{1,0:T(1,128)S(1)} %bitcast.7, ...), custom_call_target="tpu_custom_call" | custom-call | flops 1 | bytes 1 | tf_op jit(solution)/shard_map/within/pallas_call | solution.py:579
  33.6 0.7 copy-done.9
  34.3 0.7 copy-done.11
  35.1 1.1 %collective-permute-start.10 = (bf16[528,768]{1,0:T(8,128)(2,1)S(1)}, bf16[528,768]{1,0:T(8,128)(2,1)}, u32[]{:S(2)}, u32[]{:S(2)}) collective-permute-start(bf16[528,768]{1,0:T(8,128)(2,1)S(1)} %pack.1), channel_id=1, source_target_pairs={{0,8},{4,12},{8,0},{12,4},{16,24},{20,28},{24,16},{28,20},{32,40},... | collective-permute-start | bytes 2433032 | tf_op jit(solution)/shard_map/ppermute | solution.py:664
  36.2 3.5 %collective-permute-start.11 = (bf16[528,768]{1,0:T(8,128)(2,1)S(1)}, bf16[528,768]{1,0:T(8,128)(2,1)}, u32[]{:S(2)}, u32[]{:S(2)}) collective-permute-start(bf16[528,768]{1,0:T(8,128)(2,1)S(1)} %pack.1), channel_id=1, source_target_pairs={{0,12},{4,8},{8,4},{12,0},{16,28},{20,24},{24,20},{28,16},{32,44},... | collective-permute-start | bytes 2433032 | tf_op jit(solution)/shard_map/ppermute | solution.py:664
  39.7 0.6 line.1
  40.3 1.4 %collective-permute-start.6 = (bf16[208,128]{1,0:T(8,128)(2,1)S(1)}, bf16[208,128]{1,0:T(8,128)(2,1)S(1)}, u32[]{:S(2)}, u32[]{:S(2)}) collective-permute-start(bf16[208,128]{1,0:T(8,128)(2,1)S(1)} %get-tuple-element.88.a0), channel_id=1, source_target_pairs={{0,64},{4,68},{8,72},{12,76},{16,80},{20,84},{24,88},{28,92},{32,9... | collective-permute-start | bytes 159752 | tf_op jit(solution)/shard_map/ppermute | solution.py:669
  41.6 0.6 collective-permute-start.7
  42.3 2.2 %collective-permute-done.6.a1 = bf16[208,128]{1,0:T(8,128)(2,1)S(1)} collective-permute-done((bf16[208,128]{1,0:T(8,128)(2,1)S(1)}, bf16[208,128]{1,0:T(8,128)(2,1)S(1)}, u32[]{:S(2)}, u32[]{:S(2)}) %collective-permute-start.6) | collective-permute-done | bytes 53280 | tf_op jit(solution)/shard_map/ppermute | solution.py:669
  44.5 0.4 collective-permute-start.8
  45.0 0.7 copy-done.21
  45.6 0.0 copy-done.20
  45.6 1.1 %copy-done.8 = bf16[512,768]{1,0:T(8,128)(2,1)S(1)} copy-done((bf16[512,768]{1,0:T(8,128)(2,1)S(1)}, bf16[512,768]{1,0:T(8,128)(2,1)}, u32[]{:S(2)}) %copy-start.8) | copy-done | bytes 786456
  46.8 7.8 %local.1 = (bf16[768,256]{1,0:T(8,128)(2,1)S(1)}, bf16[384,256]{1,0:T(8,128)(2,1)S(1)}, f32[768,256]{1,0:T(8,128)S(1)}, f32[48,256]{1,0:T(8,128)S(1)}, bf16[768,...) custom-call(bf16[512,768]{1,0:T(8,128)(2,1)S(1)} %copy-done.8, bf16[512,768]{1,0:T(8,128)(2,1)S(1)} %copy-done.4, ...), custom_call_target="tpu_custom_call" | custom-call | flops 1 | bytes 1 | tf_op jit(solution)/shard_map/local/pallas_call | solution.py:558
  54.6 0.0 copy-start.16
  54.6 0.0 copy-start.18
  54.6 1.0 %plane.1 = (bf16[192,128]{1,0:T(8,128)(2,1)S(1)}, bf16[192,128]{1,0:T(8,128)(2,1)S(1)}, bf16[192,128]{1,0:T(8,128)(2,1)S(1)}, bf16[192,128]{1,0:T(8,128)(2,1)S(1)}) custom-call(s32[3]{0:T(128)S(1)} %pad_add_fusion.place_ref, bf16[208,128]{1,0:T(8,128)(2,1)S(1)} %get-tuple-element.88.a0, bf16[208,128]{1,0:T(8,128)(2,1)S(1)} %collective-permute-done.6.a1, ...), custom_call_target="tpu_custom_call" | custom-call | flops 1 | bytes 1 | tf_op jit(solution)/shard_map/plane/pallas_call | solution.py:535
  55.7 0.6 collective-permute-start.12
  56.3 1.0 %collective-permute-start.13 = (bf16[192,128]{1,0:T(8,128)(2,1)S(1)}, bf16[192,128]{1,0:T(8,128)(2,1)S(1)}, u32[]{:S(2)}, u32[]{:S(2)}) collective-permute-start(bf16[192,128]{1,0:T(8,128)(2,1)S(1)} %get-tuple-element.98), channel_id=1, source_target_pairs={{0,8},{4,12},{8,0},{12,4},{16,24},{20,28},{24,16},{28,20},{32,40},... | collective-permute-start | bytes 147464 | tf_op jit(solution)/shard_map/ppermute | solution.py:664
  57.3 3.5 %collective-permute-start.14 = (bf16[192,128]{1,0:T(8,128)(2,1)S(1)}, bf16[192,128]{1,0:T(8,128)(2,1)S(1)}, u32[]{:S(2)}, u32[]{:S(2)}) collective-permute-start(bf16[192,128]{1,0:T(8,128)(2,1)S(1)} %get-tuple-element.99), channel_id=1, source_target_pairs={{0,12},{4,8},{8,4},{12,0},{16,28},{20,24},{24,20},{28,16},{32,44},... | collective-permute-start | bytes 147464 | tf_op jit(solution)/shard_map/ppermute | solution.py:664
  60.8 2.8 %within.3 = (bf16[512,384]{1,0:T(8,128)(2,1)S(1)}, bf16[512,384]{1,0:T(8,128)(2,1)S(1)}) custom-call(bf16[512,768]{1,0:T(8,128)(2,1)S(1)} %copy-done.1, bf16[512,768]{1,0:T(8,128)(2,1)S(1)} %copy-done.2, f32[12,512]{1,0:T(8,128)S(1)} %copy-done.16, f32[12,512]{1,0:T(8,128)S(1)} %copy-done.18, s32[1,512]{1,0:T(1,128)S(1)} %bitcast.9, ...), custom_call_target="tpu_custom_call" | custom-call | flops 1 | bytes 1 | tf_op jit(solution)/shard_map/within/pallas_call | solution.py:579
  63.6 4.7 %near.1 = (f32[768,256]{1,0:T(8,128)S(1)}, f32[48,256]{1,0:T(8,128)S(1)}) custom-call(bf16[768,256]{1,0:T(8,128)(2,1)S(1)} %get-tuple-element.103.qe_ref, bf16[384,256]{1,0:T(8,128)(2,1)S(1)} %get-tuple-element.104.plan_ref, f32[768,256]{1,0:T(8,128)S(1)} %get-tuple-element.105.oe_ref, f32[48,256]{1,0:T(8,128)S(1)} %get-tuple-element.106.stat_ref, ...), custom_call_target="tpu_custom_call" | custom-call | flops 1 | bytes 1 | tf_op jit(solution)/shard_map/near/pallas_call | solution.py:616
  68.3 0.7 collective-permute-done.12.f1
  69.0 2.3 %collective-permute-done.13.f2 = bf16[192,128]{1,0:T(8,128)(2,1)S(1)} collective-permute-done((bf16[192,128]{1,0:T(8,128)(2,1)S(1)}, bf16[192,128]{1,0:T(8,128)(2,1)S(1)}, u32[]{:S(2)}, u32[]{:S(2)}) %collective-permute-start.13) | collective-permute-done | bytes 49184 | tf_op jit(solution)/shard_map/ppermute | solution.py:664
  71.3 2.9 %collective-permute-done.14.f3 = bf16[192,128]{1,0:T(8,128)(2,1)S(1)} collective-permute-done((bf16[192,128]{1,0:T(8,128)(2,1)S(1)}, bf16[192,128]{1,0:T(8,128)(2,1)S(1)}, u32[]{:S(2)}, u32[]{:S(2)}) %collective-permute-start.14) | collective-permute-done | bytes 49184 | tf_op jit(solution)/shard_map/ppermute | solution.py:664
  74.1 3.1 %finish.1 = bf16[512,768]{1,0:T(8,128)(2,1)} custom-call(s32[3]{0:T(128)S(1)} %pad_add_fusion.place_ref, bf16[192,128]{1,0:T(8,128)(2,1)S(1)} %get-tuple-element.112.f0, bf16[192,128]{1,0:T(8,128)(2,1)S(1)} %collective-permute-done.12.f1, bf16[192,128]{1,0:T(8,128)(2,1)S(1)} %collective-permute-done.13.f2, bf16[192,128]{1,0:T(8,128)(2,1)S(1)} %collective-permute-done.14.f3, ...), custom_call_target="tpu_custom_call" | custom-call | flops 1 | bytes 1 | tf_op jit(solution)/shard_map/finish/pallas_call | solution.py:598
  77.3 7.6 %remote.1 = bf16[512,768]{1,0:T(8,128)(2,1)} custom-call(bf16[768,256]{1,0:T(8,128)(2,1)S(1)} %get-tuple-element.103.qe_ref, bf16[384,256]{1,0:T(8,128)(2,1)S(1)} %get-tuple-element.104.plan_ref, f32[768,256]{1,0:T(8,128)S(1)} %get-tuple-element.109.oe_ref, f32[48,256]{1,0:T(8,128)S(1)} %get-tuple-element.110.stat_ref, ...), custom_call_target="tpu_custom_call" | custom-call | flops 1 | bytes 1 | tf_op jit(solution)/shard_map/remote/pallas_call | solution.py:629
  (43 shorter events, 0.1 us)
Async XLA Ops:
  0.6 0.7 copy-start.19
  1.3 1.1 %copy-start = (bf16[512,768]{1,0:T(8,128)(2,1)S(1)}, bf16[512,768]{1,0:T(8,128)(2,1)}, u32[]{:S(2)}) copy-start(bf16[512,768]{1,0:T(8,128)(2,1)} %v_ref.7) | copy-start | bytes 2359300
  2.5 0.9 %copy-start.5 = (bf16[512,128]{1,0:T(8,128)(2,1)S(1)}, bf16[512,128]{1,0:T(8,128)(2,1)}, u32[]{:S(2)}) copy-start(bf16[512,128]{1,0:T(8,128)(2,1)} %into_ref.3) | copy-start | bytes 393220
  3.4 0.8 copy-start.15
  4.1 0.8 copy-start.17
  4.9 7.1 %copy-start.1 = (bf16[512,768]{1,0:T(8,128)(2,1)S(1)}, bf16[512,768]{1,0:T(8,128)(2,1)}, u32[]{:S(2)}) copy-start(bf16[512,768]{1,0:T(8,128)(2,1)} %v_ref.7) | copy-start | bytes 2359300
  6.9 7.4 %collective-permute-start = (bf16[208,128]{1,0:T(8,128)(2,1)S(1)}, bf16[208,128]{1,0:T(8,128)(2,1)S(1)}, u32[]{:S(2)}, u32[]{:S(2)}) collective-permute-start(bf16[208,128]{1,0:T(8,128)(2,1)S(1)} %get-tuple-element.60), channel_id=1, source_target_pairs={{0,4},{4,0},{8,12},{12,8},{16,20},{20,16},{24,28},{28,24},{32,36},... | collective-permute-start | bytes 159752 | tf_op jit(solution)/shard_map/ppermute | solution.py:664
  10.0 4.5 %collective-permute-start.1 = (bf16[208,128]{1,0:T(8,128)(2,1)S(1)}, bf16[208,128]{1,0:T(8,128)(2,1)S(1)}, u32[]{:S(2)}, u32[]{:S(2)}) collective-permute-start(bf16[208,128]{1,0:T(8,128)(2,1)S(1)} %get-tuple-element.61), channel_id=1, source_target_pairs={{0,8},{4,12},{8,0},{12,4},{16,24},{20,28},{24,16},{28,20},{32,40},... | collective-permute-start | bytes 159752 | tf_op jit(solution)/shard_map/ppermute | solution.py:664
  11.9 6.5 %collective-permute-start.2 = (bf16[208,128]{1,0:T(8,128)(2,1)S(1)}, bf16[208,128]{1,0:T(8,128)(2,1)S(1)}, u32[]{:S(2)}, u32[]{:S(2)}) collective-permute-start(bf16[208,128]{1,0:T(8,128)(2,1)S(1)} %get-tuple-element.62), channel_id=1, source_target_pairs={{0,12},{4,8},{8,4},{12,0},{16,28},{20,24},{24,20},{28,16},{32,44},... | collective-permute-start | bytes 159752 | tf_op jit(solution)/shard_map/ppermute | solution.py:664
  12.0 1.1 %copy-start.3 = (bf16[512,768]{1,0:T(8,128)(2,1)S(1)}, bf16[512,768]{1,0:T(8,128)(2,1)}, u32[]{:S(2)}) copy-start(bf16[512,768]{1,0:T(8,128)(2,1)} %k_ref.3) | copy-start | bytes 2359300
  13.1 17.7 %copy-start.2 = (bf16[512,768]{1,0:T(8,128)(2,1)S(1)}, bf16[512,768]{1,0:T(8,128)(2,1)}, u32[]{:S(2)}) copy-start(bf16[512,768]{1,0:T(8,128)(2,1)} %gate_ref.3) | copy-start | bytes 2359300
  14.3 16.5 %copy-start.7 = (bf16[512,128]{1,0:T(8,128)(2,1)S(1)}, bf16[512,128]{1,0:T(8,128)(2,1)}, u32[]{:S(2)}) copy-start(bf16[512,128]{1,0:T(8,128)(2,1)} %read_ref.5) | copy-start | bytes 393220
  19.1 0.7 copy-start.13
  19.9 10.9 %copy-start.22 = (f32[12]{0:T(128)S(1)}, f32[12]{0:T(128)}, u32[]{:S(2)}) copy-start(f32[12]{0:T(128)} %skip_ref.3) | copy-start | bytes 148
  19.9 25.1 %copy-start.4 = (bf16[512,768]{1,0:T(8,128)(2,1)S(1)}, bf16[512,768]{1,0:T(8,128)(2,1)}, u32[]{:S(2)}) copy-start(bf16[512,768]{1,0:T(8,128)(2,1)} %k_ref.3) | copy-start | bytes 2359300
  19.9 15.2 %collective-permute-start.3 = (bf16[208,128]{1,0:T(8,128)(2,1)S(1)}, bf16[208,128]{1,0:T(8,128)(2,1)S(1)}, u32[]{:S(2)}, u32[]{:S(2)}) collective-permute-start(bf16[208,128]{1,0:T(8,128)(2,1)S(1)} %get-tuple-element.76.a0), channel_id=1, source_target_pairs={{0,16},{4,20},{8,24},{12,28},{16,32},{20,36},{24,40},{28,44},{32,4... | collective-permute-start | bytes 159752 | tf_op jit(solution)/shard_map/ppermute | solution.py:669
  23.1 11.9 %collective-permute-start.4 = (bf16[208,128]{1,0:T(8,128)(2,1)S(1)}, bf16[208,128]{1,0:T(8,128)(2,1)S(1)}, u32[]{:S(2)}, u32[]{:S(2)}) collective-permute-start(bf16[208,128]{1,0:T(8,128)(2,1)S(1)} %get-tuple-element.76.a0), channel_id=1, source_target_pairs={{0,32},{4,36},{8,40},{12,44},{16,48},{20,52},{24,56},{28,60},{32,0... | collective-permute-start | bytes 159752 | tf_op jit(solution)/shard_map/ppermute | solution.py:669
  27.6 7.5 %collective-permute-start.5 = (bf16[208,128]{1,0:T(8,128)(2,1)S(1)}, bf16[208,128]{1,0:T(8,128)(2,1)S(1)}, u32[]{:S(2)}, u32[]{:S(2)}) collective-permute-start(bf16[208,128]{1,0:T(8,128)(2,1)S(1)} %get-tuple-element.76.a0), channel_id=1, source_target_pairs={{0,48},{4,52},{8,56},{12,60},{16,0},{20,4},{24,8},{28,12},{32,16},... | collective-permute-start | bytes 159752 | tf_op jit(solution)/shard_map/ppermute | solution.py:669
  30.3 27.0 %collective-permute-start.9 = (bf16[528,768]{1,0:T(8,128)(2,1)S(1)}, bf16[528,768]{1,0:T(8,128)(2,1)}, u32[]{:S(2)}, u32[]{:S(2)}) collective-permute-start(bf16[528,768]{1,0:T(8,128)(2,1)S(1)} %pack.1), channel_id=1, source_target_pairs={{0,4},{4,0},{8,12},{12,8},{16,20},{20,16},{24,28},{28,24},{32,36},... | collective-permute-start | bytes 2433032 | tf_op jit(solution)/shard_map/ppermute | solution.py:664
  33.6 0.7 copy-start.9
  34.3 0.7 copy-start.11
  35.1 42.2 %collective-permute-start.10 = (bf16[528,768]{1,0:T(8,128)(2,1)S(1)}, bf16[528,768]{1,0:T(8,128)(2,1)}, u32[]{:S(2)}, u32[]{:S(2)}) collective-permute-start(bf16[528,768]{1,0:T(8,128)(2,1)S(1)} %pack.1), channel_id=1, source_target_pairs={{0,8},{4,12},{8,0},{12,4},{16,24},{20,28},{24,16},{28,20},{32,40},... | collective-permute-start | bytes 2433032 | tf_op jit(solution)/shard_map/ppermute | solution.py:664
  36.2 41.1 %collective-permute-start.11 = (bf16[528,768]{1,0:T(8,128)(2,1)S(1)}, bf16[528,768]{1,0:T(8,128)(2,1)}, u32[]{:S(2)}, u32[]{:S(2)}) collective-permute-start(bf16[528,768]{1,0:T(8,128)(2,1)S(1)} %pack.1), channel_id=1, source_target_pairs={{0,12},{4,8},{8,4},{12,0},{16,28},{20,24},{24,20},{28,16},{32,44},... | collective-permute-start | bytes 2433032 | tf_op jit(solution)/shard_map/ppermute | solution.py:664
  40.3 4.2 %collective-permute-start.6 = (bf16[208,128]{1,0:T(8,128)(2,1)S(1)}, bf16[208,128]{1,0:T(8,128)(2,1)S(1)}, u32[]{:S(2)}, u32[]{:S(2)}) collective-permute-start(bf16[208,128]{1,0:T(8,128)(2,1)S(1)} %get-tuple-element.88.a0), channel_id=1, source_target_pairs={{0,64},{4,68},{8,72},{12,76},{16,80},{20,84},{24,88},{28,92},{32,9... | collective-permute-start | bytes 159752 | tf_op jit(solution)/shard_map/ppermute | solution.py:669
  41.6 12.9 %collective-permute-start.7 = (bf16[208,128]{1,0:T(8,128)(2,1)S(1)}, bf16[208,128]{1,0:T(8,128)(2,1)}, u32[]{:S(2)}, u32[]{:S(2)}) collective-permute-start(bf16[208,128]{1,0:T(8,128)(2,1)S(1)} %get-tuple-element.88.a0), channel_id=1, source_target_pairs={{0,128},{4,132},{8,136},{12,140},{16,144},{20,148},{24,152},{28,15... | collective-permute-start | bytes 159752 | tf_op jit(solution)/shard_map/ppermute | solution.py:669
  44.5 10.1 %collective-permute-start.8 = (bf16[208,128]{1,0:T(8,128)(2,1)S(1)}, bf16[208,128]{1,0:T(8,128)(2,1)}, u32[]{:S(2)}, u32[]{:S(2)}) collective-permute-start(bf16[208,128]{1,0:T(8,128)(2,1)S(1)} %get-tuple-element.88.a0), channel_id=1, source_target_pairs={{0,192},{4,196},{8,200},{12,204},{16,208},{20,212},{24,216},{28,22... | collective-permute-start | bytes 159752 | tf_op jit(solution)/shard_map/ppermute | solution.py:669
  44.9 0.7 copy-start.21
  44.9 0.7 copy-start.20
  45.6 1.1 %copy-start.8 = (bf16[512,768]{1,0:T(8,128)(2,1)S(1)}, bf16[512,768]{1,0:T(8,128)(2,1)}, u32[]{:S(2)}) copy-start(bf16[512,768]{1,0:T(8,128)(2,1)} %q_ref.1) | copy-start | bytes 2359300
  46.8 7.8 %copy-start.14 = (f32[4,192,128]{2,1,0:T(8,128)S(1)}, f32[4,192,128]{2,1,0:T(8,128)}, u32[]{:S(2)}) copy-start(f32[4,192,128]{2,1,0:T(8,128)} %copy-done.13) | copy-start | bytes 1179652
  54.6 6.2 %copy-start.6 = (bf16[512,128]{1,0:T(8,128)(2,1)S(1)}, bf16[512,128]{1,0:T(8,128)(2,1)}, u32[]{:S(2)}) copy-start(bf16[512,128]{1,0:T(8,128)(2,1)} %into_ref.3) | copy-start | bytes 393220
  54.6 6.2 %copy-start.16 = (f32[12,512]{1,0:T(8,128)S(1)}, f32[12,512]{1,0:T(8,128)}, u32[]{:S(2)}) copy-start(f32[12,512]{1,0:T(8,128)} %steps_ref.3) | copy-start | bytes 73732
  54.6 6.2 %copy-start.18 = (f32[12,512]{1,0:T(8,128)S(1)}, f32[12,512]{1,0:T(8,128)}, u32[]{:S(2)}) copy-start(f32[12,512]{1,0:T(8,128)} %rates_ref.3) | copy-start | bytes 73732
  55.7 5.1 %copy-start.23 = (f32[768]{0:T(1024)S(1)}, f32[768]{0:T(1024)}, u32[]{:S(2)}) copy-start(f32[768]{0:T(1024)} %param.25) | copy-start | bytes 9220
  55.7 13.3 %collective-permute-start.12 = (bf16[192,128]{1,0:T(8,128)(2,1)S(1)}, bf16[192,128]{1,0:T(8,128)(2,1)S(1)}, u32[]{:S(2)}, u32[]{:S(2)}) collective-permute-start(bf16[192,128]{1,0:T(8,128)(2,1)S(1)} %get-tuple-element.97), channel_id=1, source_target_pairs={{0,4},{4,0},{8,12},{12,8},{16,20},{20,16},{24,28},{28,24},{32,36},... | collective-permute-start | bytes 147464 | tf_op jit(solution)/shard_map/ppermute | solution.py:664
  56.3 15.0 %collective-permute-start.13 = (bf16[192,128]{1,0:T(8,128)(2,1)S(1)}, bf16[192,128]{1,0:T(8,128)(2,1)S(1)}, u32[]{:S(2)}, u32[]{:S(2)}) collective-permute-start(bf16[192,128]{1,0:T(8,128)(2,1)S(1)} %get-tuple-element.98), channel_id=1, source_target_pairs={{0,8},{4,12},{8,0},{12,4},{16,24},{20,28},{24,16},{28,20},{32,40},... | collective-permute-start | bytes 147464 | tf_op jit(solution)/shard_map/ppermute | solution.py:664
  57.3 16.9 %collective-permute-start.14 = (bf16[192,128]{1,0:T(8,128)(2,1)S(1)}, bf16[192,128]{1,0:T(8,128)(2,1)S(1)}, u32[]{:S(2)}, u32[]{:S(2)}) collective-permute-start(bf16[192,128]{1,0:T(8,128)(2,1)S(1)} %get-tuple-element.99), channel_id=1, source_target_pairs={{0,12},{4,8},{8,4},{12,0},{16,28},{20,24},{24,20},{28,16},{32,44},... | collective-permute-start | bytes 147464 | tf_op jit(solution)/shard_map/ppermute | solution.py:664
  63.6 10.6 %copy-start.10 = (bf16[512,384]{1,0:T(8,128)(2,1)S(1)}, bf16[512,384]{1,0:T(8,128)(2,1)}, u32[]{:S(2)}) copy-start(bf16[512,384]{1,0:T(8,128)(2,1)} %copy-done.9) | copy-start | bytes 1179652
  63.6 10.6 %copy-start.12 = (bf16[512,384]{1,0:T(8,128)(2,1)S(1)}, bf16[512,384]{1,0:T(8,128)(2,1)}, u32[]{:S(2)}) copy-start(bf16[512,384]{1,0:T(8,128)(2,1)} %copy-done.11) | copy-start | bytes 1179652

commit v4 on v3

--- a/solution.py
+++ b/solution.py
@@ -219,17 +219,17 @@
 
 
 def remote_kernel(near, qe_ref, plan_ref, oe_ref, stat_ref, oo_ref, ve_ref, *rest):
-    blocks, outs = (rest[:1], rest[1:]) if near else (rest[:2], rest[2:])
+    blocks, outs = (rest[:2], rest[2:]) if near else (rest[:1], rest[1:])
     spread = one((iota((16, 128), 0) == 0) & (iota((16, 128), 1) == 16), BF16)
     row, lane = iota((HALF, 128), 0), iota((HALF, 128), 1)
     wanted = ((lane & 3) == (row >> 6)) & (lane < 16)
-    wanted = one(wanted & (lane < 8) if near else wanted & (lane >= 8))
+    close, distant = one(wanted & (lane < 8)), one(wanted & (lane >= 8))
     sides = []
     for parity in range(2):
         pieces = []
-        for ref in blocks:
+        for ref, group in zip(blocks, (close, distant) if near else (distant,)):
             flags = ref[ROWS : ROWS + 16, parity * HALF : (parity + 1) * HALF].astype(F32)
-            pieces.append(t_dot(((1.0 - flags) * NEG).astype(BF16), spread) + wanted)
+            pieces.append(t_dot(((1.0 - flags) * NEG).astype(BF16), spread) + group)
         sides.append(jnp.concatenate(pieces, axis=0).astype(BF16))
     for pair in range(PAIRS):
         both = slice(pair * 128, (pair + 1) * 128)
@@ -382,13 +382,12 @@
 
 
 def within_kernel(
-    first,
     v_ref, gate_ref, steps_ref, rates_ref, valid_ref, into_ref, read_ref, skip_ref,
     base_ref, lift_ref, couple_ref, col_ref, row_ref,
 ):
-    pair = pl.program_id(0) + first
-
-    @pl.when(pl.program_id(0) == 0)
+    pair = pl.program_id(0)
+
+    @pl.when(pair == 0)
     def _():
         couple_ref[...] = dot_t(read_ref[...], into_ref[...])
         upto = one(iota((ROWS, ROWS), 0) <= iota((ROWS, ROWS), 1), BF16)
@@ -435,9 +434,7 @@
     lift_ref[...] = (jnp.exp(jnp.where(low, falls[0], falls[1])) * gate).astype(BF16)
 
 
-def finish_kernel(place_ref, f0, f1, f2, f3, read_ref, *rest):
-    gain_ref, out_ref, held = rest[4:]
-
+def finish_kernel(place_ref, f0, f1, f2, f3, read_ref, base_ref, lift_ref, gain_ref, out_ref, held):
     @pl.when(pl.program_id(0) == 0)
     def _():
         for step, ref in enumerate((f0, f1, f2, f3)):
@@ -447,10 +444,8 @@
     together = one((iota((128, 128), 0) >> 6) == (iota((128, 128), 1) >> 6), BF16)
     for pair in range(PAIRS):
         now = slice(pair * 128, (pair + 1) * 128)
-        half = slice(pair % 3 * 128, (pair % 3 + 1) * 128)
-        base_ref, lift_ref = rest[pair // 3 * 2 : pair // 3 * 2 + 2]
         carried = dot_t(read_ref[...], held[now, :])
-        gated = base_ref[:, half].astype(F32) + lift_ref[:, half].astype(F32) * carried
+        gated = base_ref[:, now].astype(F32) + lift_ref[:, now].astype(F32) * carried
         high, low = split(gated * gated, 2)
         mean = (dot(high, together) + dot(low, together)) * (1.0 / HEAD_DIM)
         out_ref[:, now] = (gated * lax.rsqrt(mean + 1e-05) * gain_ref[:, now]).astype(BF16)
@@ -497,7 +492,7 @@
             pltpu.SemaphoreType.DMA((5,)),
         ],
         cost_estimate=FREE,
-        compiler_params=params(),
+        compiler_params=params(58),
         name="state",
     )(*args)
 
@@ -572,15 +567,12 @@
     )(*args)
 
 
-def call_within(first, *args):
-    def columns(rows):
-        return pl.BlockSpec((rows, 128), lambda pair: (0, first + pair))
-
-    return pl.pallas_call(
-        functools.partial(within_kernel, first),
-        grid=(PAIRS // 2,),
-        out_shape=[shape(ROWS, WIDTH // 2)] * 2,
-        in_specs=[columns(ROWS)] * 2
+def call_within(*args):
+    return pl.pallas_call(
+        within_kernel,
+        grid=(PAIRS,),
+        out_shape=[shape(ROWS, WIDTH)] * 2,
+        in_specs=[lanes(ROWS)] * 2
         + [whole(HEADS_HERE, ROWS)] * 2
         + [whole(1, ROWS), whole(ROWS, STATE), whole(ROWS, STATE), SMEM],
         out_specs=[lanes(ROWS)] * 2,
@@ -602,7 +594,7 @@
         in_specs=[SMEM]
         + [whole(QUARTER, STATE)] * 4
         + [rows(STATE)]
-        + [rows(WIDTH // 2)] * 4
+        + [rows(WIDTH)] * 2
         + [whole(1, WIDTH)],
         out_specs=rows(WIDTH),
         scratch_shapes=[pltpu.VMEM((WIDTH, STATE), BF16)],
@@ -616,12 +608,12 @@
     out, stat = pl.pallas_call(
         functools.partial(remote_kernel, True),
         out_shape=[KEPT[2], KEPT[3]],
-        in_specs=[VMEM] * 7,
+        in_specs=[VMEM] * 8,
         out_specs=[VMEM] * 2,
         cost_estimate=FREE,
         compiler_params=params(14),
         name="near",
-    )(*kept, arrived)
+    )(*kept, *arrived)
     return [kept[0], kept[1], out, stat, kept[4], kept[5]]
 
 
@@ -629,13 +621,13 @@
     return pl.pallas_call(
         functools.partial(remote_kernel, False),
         out_shape=shape(ROWS, WIDTH),
-        in_specs=[VMEM] * 8,
+        in_specs=[VMEM] * 7,
         out_specs=VMEM,
         scratch_shapes=[pltpu.VMEM((WIDTH, ROWS), BF16)],
         cost_estimate=FREE,
         compiler_params=params(14),
         name="remote",
-    )(*kept, *arrived)
+    )(*kept, arrived)
 
 
 def per_device(
@@ -674,16 +666,13 @@
     pieces = call_state(value_rows, *scan_inputs, place)
     packed = call_pack(key_rows, value_rows, after((valid, pieces))[0])
     pieces = [pieces[0]] + [cross(pieces[mask], mask) for mask in range(1, SPAN_DEV)]
-    near = cross(packed, 1)
+    near = [cross(packed, 1)]
     pieces = after((pieces, packed))[0]
     total, block_before, block_fade = call_block(place, *pieces)
     totals = [total] + [turn(total, step, 16) for step in range(1, 4)]
-    halves = list(scan_inputs)
-    halves[2] = after((valid, total))[0]
-    first = call_within(0, value_rows, gate_in, *halves, state_out, skip_weight)
-    totals = after((totals, first))[0]
     packed, totals = after((packed, totals))
-    arrived = [cross(packed, mask) for mask in range(2, SPAN_DEV)]
+    near.append(cross(packed, 2))
+    far = cross(packed, 3)
     total, line_before, line_fade = call_line(place, *totals)
     kept = call_local(
         query_rows, key_rows, value_rows, after((valid, total))[0], segment_lengths, dilation, rank
@@ -691,13 +680,13 @@
     totals = [total] + [turn(total, step, 64) for step in range(1, 4)]
     totals = after((totals, kept))[0]
     carried = call_plane(place, *totals, line_before, line_fade, block_before, block_fade)
-    halves[2] = after((valid, carried))[0]
-    second = call_within(3, value_rows, gate_in, *halves, state_out, skip_weight)
+    scan_inputs = (*scan_inputs[:2], after((valid, carried))[0], state_in)
+    within = call_within(value_rows, gate_in, *scan_inputs, state_out, skip_weight)
     carried = [carried[0]] + [cross(carried[mask], mask) for mask in range(1, SPAN_DEV)]
-    kept = call_near(after((kept, second))[0], near)
+    kept = call_near(after((kept, within))[0], near)
     carried = after((carried, kept))[0]
-    scanned = call_finish(place, *carried, state_out, *first, *second, gain)
-    attended = call_remote(kept, arrived)
+    scanned = call_finish(place, *carried, state_out, *within, gain)
+    attended = call_remote(kept, far)
     return (attended, scanned)
 
 

time: 85.4 us -> 76.7 us (0.90)
  local copies, waits for them, and re-layouts: 9.4 us -> 4.37 us
  starting transfers between devices: 28.1 us -> 25.8 us
  Pallas kernels: 34.2 us -> 32.9 us
    unnamed x48 -> x36, local copies, waits for them, and re-layouts: 9.4 us -> 4.36 us
    pallas_call x1, Pallas kernels: 7.64 us -> 4.87 us  [call_remote(): pl.pallas_call(functools.partial(remote_kernel, False), out_shape=shape(R...]
    ppermute x9, waiting for transfers between devices: 10 us -> 7.34 us  [cross(): return lax.ppermute(block, 'seq', [(i, i ^ mask) for i in range(count)])]
    ppermute x6, waiting for transfers between devices: 2.24 us -> 4.54 us  [turn(): return lax.ppermute(block, 'seq', route)]
    ppermute x9, starting transfers between devices: 15.2 us -> 12.9 us  [cross(): return lax.ppermute(block, 'seq', [(i, i ^ mask) for i in range(count)])]
    pallas_call x1, Pallas kernels: 4.69 us -> 6.21 us  [call_near(): pl.pallas_call(functools.partial(remote_kernel, True), out_shape=[KEPT[2]...]
    pallas_call x1, Pallas kernels: 2.03 us -> 3.28 us  [call_state(): pl.pallas_call(state_kernel, out_shape=[shape(PIECE, STATE)] * 4, in_spec...]
    pallas_call x2 -> x1, Pallas kernels: 5.55 us -> 4.64 us  [call_within(): pl.pallas_call(within_kernel, grid=(PAIRS,), out_shape=[shape(ROWS, WIDTH...]
  transfers between devices with their start and end apart: 15 -> 15, of which waited for: 6 -> 7; matrix products, arithmetic and copies ran while one was open for 0% -> 0% of each run, Pallas kernels for 28% -> 32%
where the time goes in v4:
time: 76.7 us; the launch traced here: 76.5 us
  Pallas kernels  32.9 us (43%)
  starting transfers between devices  25.8 us (34%)
  waiting for transfers between devices  11.9 us (16%)
  local copies, waits for them, and re-layouts  4.37 us (6%)
  between operations  0.86 us (1%)
    ppermute x9, starting transfers between devices, cross(): return lax.ppermute(block, 'seq', [(i, i ^ mask) for i in range(count)])  12.9 us
    ppermute x6, starting transfers between devices, turn(): return lax.ppermute(block, 'seq', route)  12.9 us
    pallas_call x1, Pallas kernels, call_local(): pl.pallas_call(local_kernel, out_shape=KEPT, in_specs=[VMEM] * 4 + [SMEM]...  7.78 us
    ppermute x9, waiting for transfers between devices, cross(): return lax.ppermute(block, 'seq', [(i, i ^ mask) for i in range(count)])  7.34 us
    pallas_call x1, Pallas kernels, call_near(): pl.pallas_call(functools.partial(remote_kernel, True), out_shape=[KEPT[2]...  6.21 us
    pallas_call x1, Pallas kernels, call_remote(): pl.pallas_call(functools.partial(remote_kernel, False), out_shape=shape(R...  4.87 us
    pallas_call x1, Pallas kernels, call_within(): pl.pallas_call(within_kernel, grid=(PAIRS,), out_shape=[shape(ROWS, WIDTH...  4.64 us
    ppermute x6, waiting for transfers between devices, turn(): return lax.ppermute(block, 'seq', route)  4.54 us
  transfers between devices with their start and end apart: 15, of which 7 were waited for; matrix products, arithmetic and copies ran while one was open for 0% of the time, Pallas kernels for 32%

profile of v4, /device:TPU:16, one launch (start us, length us, event | category | flops | bytes accessed | tf_op | source)
XLA Modules:
  0.0 76.5 jit_solution(5734348628512822138)
XLA Ops:
  0.6 0.0 copy-start
  0.6 0.7 pad_add_fusion.place_ref
  1.3 3.3 %state.1 = (bf16[208,128]{1,0:T(8,128)(2,1)}, bf16[208,128]{1,0:T(8,128)(2,1)}, bf16[208,128]{1,0:T(8,128)(2,1)}, bf16[208,128]{1,0:T(8,128)(2,1)}) custom-call(bf16[512,768]{1,0:T(8,128)(2,1)} %v_ref.5, f32[12,512]{1,0:T(8,128)} %steps_ref.1, f32[12,512]{1,0:T(8,128)} %rates_ref.1, s32[1,512]{1,0:T(1,128)} %bitcast.5, bf16[512,128]{1,0:T(8,128)(2,1)} %into_ref.1, ...), custom_call_target="tpu_custom_call" | custom-call | flops 1 | bytes 1 | tf_op jit(solution)/shard_map/state/pallas_call | solution.py:480
  4.6 3.1 %collective-permute-start = (bf16[208,128]{1,0:T(8,128)(2,1)}, bf16[208,128]{1,0:T(8,128)(2,1)S(1)}, u32[]{:S(2)}, u32[]{:S(2)}) collective-permute-start(bf16[208,128]{1,0:T(8,128)(2,1)} %get-tuple-element.53), channel_id=1, source_target_pairs={{0,4},{4,0},{8,12},{12,8},{16,20},{20,16},{24,28},{28,24},{32,36},... | collective-permute-start | bytes 159752 | tf_op jit(solution)/shard_map/ppermute | solution.py:656
  7.7 1.9 %collective-permute-start.1 = (bf16[208,128]{1,0:T(8,128)(2,1)}, bf16[208,128]{1,0:T(8,128)(2,1)S(1)}, u32[]{:S(2)}, u32[]{:S(2)}) collective-permute-start(bf16[208,128]{1,0:T(8,128)(2,1)} %get-tuple-element.54), channel_id=1, source_target_pairs={{0,8},{4,12},{8,0},{12,4},{16,24},{20,28},{24,16},{28,20},{32,40},... | collective-permute-start | bytes 159752 | tf_op jit(solution)/shard_map/ppermute | solution.py:656
  9.6 0.1 collective-permute-start.2
  9.7 1.1 %copy-done.1 = bf16[512,768]{1,0:T(8,128)(2,1)S(1)} copy-done((bf16[512,768]{1,0:T(8,128)(2,1)S(1)}, bf16[512,768]{1,0:T(8,128)(2,1)}, u32[]{:S(2)}) %copy-start.1) | copy-done | bytes 786456
  10.8 1.1 %pack.1 = bf16[528,768]{1,0:T(8,128)(2,1)S(1)} custom-call(bf16[512,768]{1,0:T(8,128)(2,1)S(1)} %copy-done.1, bf16[512,768]{1,0:T(8,128)(2,1)S(1)} %copy-done, s32[1,512]{1,0:T(1,128)S(1)} %bitcast.6), custom_call_target="tpu_custom_call" | custom-call | flops 1 | bytes 1 | tf_op jit(solution)/shard_map/pack/pallas_call | solution.py:467
  12.0 0.5 collective-permute-done.1.a2
  12.4 3.9 %collective-permute-done.2.a3 = bf16[208,128]{1,0:T(8,128)(2,1)S(1)} collective-permute-done((bf16[208,128]{1,0:T(8,128)(2,1)}, bf16[208,128]{1,0:T(8,128)(2,1)S(1)}, u32[]{:S(2)}, u32[]{:S(2)}) %collective-permute-start.2) | collective-permute-done | bytes 53280 | tf_op jit(solution)/shard_map/ppermute | solution.py:656
  16.4 0.6 block.1
  17.0 0.0 copy-start.7
  17.0 0.7 copy-done.7
  17.7 3.3 %collective-permute-start.3 = (bf16[208,128]{1,0:T(8,128)(2,1)S(1)}, bf16[208,128]{1,0:T(8,128)(2,1)S(1)}, u32[]{:S(2)}, u32[]{:S(2)}) collective-permute-start(bf16[208,128]{1,0:T(8,128)(2,1)S(1)} %get-tuple-element.62.a0), channel_id=1, source_target_pairs={{0,16},{4,20},{8,24},{12,28},{16,32},{20,36},{24,40},{28,44},{32,4... | collective-permute-start | bytes 159752 | tf_op jit(solution)/shard_map/ppermute | solution.py:661
  21.0 4.5 %collective-permute-start.4 = (bf16[208,128]{1,0:T(8,128)(2,1)S(1)}, bf16[208,128]{1,0:T(8,128)(2,1)S(1)}, u32[]{:S(2)}, u32[]{:S(2)}) collective-permute-start(bf16[208,128]{1,0:T(8,128)(2,1)S(1)} %get-tuple-element.62.a0), channel_id=1, source_target_pairs={{0,32},{4,36},{8,40},{12,44},{16,48},{20,52},{24,56},{28,60},{32,0... | collective-permute-start | bytes 159752 | tf_op jit(solution)/shard_map/ppermute | solution.py:661
  25.5 2.7 %collective-permute-start.5 = (bf16[208,128]{1,0:T(8,128)(2,1)S(1)}, bf16[208,128]{1,0:T(8,128)(2,1)S(1)}, u32[]{:S(2)}, u32[]{:S(2)}) collective-permute-start(bf16[208,128]{1,0:T(8,128)(2,1)S(1)} %get-tuple-element.62.a0), channel_id=1, source_target_pairs={{0,48},{4,52},{8,56},{12,60},{16,0},{20,4},{24,8},{28,12},{32,16},... | collective-permute-start | bytes 159752 | tf_op jit(solution)/shard_map/ppermute | solution.py:661
  28.2 0.5 collective-permute-start.9
  28.7 0.0 collective-permute-done.3.a1
  28.7 0.9 %collective-permute-done.4.a2 = bf16[208,128]{1,0:T(8,128)(2,1)S(1)} collective-permute-done((bf16[208,128]{1,0:T(8,128)(2,1)S(1)}, bf16[208,128]{1,0:T(8,128)(2,1)S(1)}, u32[]{:S(2)}, u32[]{:S(2)}) %collective-permute-start.4) | collective-permute-done | bytes 53280 | tf_op jit(solution)/shard_map/ppermute | solution.py:661
  29.6 1.4 %collective-permute-done.5.a3 = bf16[208,128]{1,0:T(8,128)(2,1)S(1)} collective-permute-done((bf16[208,128]{1,0:T(8,128)(2,1)S(1)}, bf16[208,128]{1,0:T(8,128)(2,1)S(1)}, u32[]{:S(2)}, u32[]{:S(2)}) %collective-permute-start.5) | collective-permute-done | bytes 53280 | tf_op jit(solution)/shard_map/ppermute | solution.py:661
  31.0 1.0 %collective-permute-start.10 = (bf16[528,768]{1,0:T(8,128)(2,1)S(1)}, bf16[528,768]{1,0:T(8,128)(2,1)}, u32[]{:S(2)}, u32[]{:S(2)}) collective-permute-start(bf16[528,768]{1,0:T(8,128)(2,1)S(1)} %pack.1), channel_id=1, source_target_pairs={{0,8},{4,12},{8,0},{12,4},{16,24},{20,28},{24,16},{28,20},{32,40},... | collective-permute-start | bytes 2433032 | tf_op jit(solution)/shard_map/ppermute | solution.py:656
  32.0 1.3 %collective-permute-start.11 = (bf16[528,768]{1,0:T(8,128)(2,1)S(1)}, bf16[528,768]{1,0:T(8,128)(2,1)S(1)}, u32[]{:S(2)}, u32[]{:S(2)}) collective-permute-start(bf16[528,768]{1,0:T(8,128)(2,1)S(1)} %pack.1), channel_id=1, source_target_pairs={{0,12},{4,8},{8,4},{12,0},{16,28},{20,24},{24,20},{28,16},{32,44},... | collective-permute-start | bytes 2433032 | tf_op jit(solution)/shard_map/ppermute | solution.py:656
  33.3 0.6 line.1
  33.9 1.4 %collective-permute-start.6 = (bf16[208,128]{1,0:T(8,128)(2,1)S(1)}, bf16[208,128]{1,0:T(8,128)(2,1)S(1)}, u32[]{:S(2)}, u32[]{:S(2)}) collective-permute-start(bf16[208,128]{1,0:T(8,128)(2,1)S(1)} %get-tuple-element.74.a0), channel_id=1, source_target_pairs={{0,64},{4,68},{8,72},{12,76},{16,80},{20,84},{24,88},{28,92},{32,9... | collective-permute-start | bytes 159752 | tf_op jit(solution)/shard_map/ppermute | solution.py:661
  35.3 0.6 collective-permute-start.7
  35.9 2.2 %collective-permute-done.6.a1 = bf16[208,128]{1,0:T(8,128)(2,1)S(1)} collective-permute-done((bf16[208,128]{1,0:T(8,128)(2,1)S(1)}, bf16[208,128]{1,0:T(8,128)(2,1)S(1)}, u32[]{:S(2)}, u32[]{:S(2)}) %collective-permute-start.6) | collective-permute-done | bytes 53280 | tf_op jit(solution)/shard_map/ppermute | solution.py:661
  38.1 0.4 collective-permute-start.8
  38.6 0.7 copy-done.15
  39.2 0.0 copy-done.14
  39.3 1.1 %copy-done.4 = bf16[512,768]{1,0:T(8,128)(2,1)S(1)} copy-done((bf16[512,768]{1,0:T(8,128)(2,1)S(1)}, bf16[512,768]{1,0:T(8,128)(2,1)}, u32[]{:S(2)}) %copy-start.4) | copy-done | bytes 786456
  40.4 7.8 %local.1 = (bf16[768,256]{1,0:T(8,128)(2,1)S(1)}, bf16[384,256]{1,0:T(8,128)(2,1)S(1)}, f32[768,256]{1,0:T(8,128)S(1)}, f32[48,256]{1,0:T(8,128)S(1)}, bf16[768,...) custom-call(bf16[512,768]{1,0:T(8,128)(2,1)S(1)} %copy-done.4, bf16[512,768]{1,0:T(8,128)(2,1)S(1)} %copy-done.2, ...), custom_call_target="tpu_custom_call" | custom-call | flops 1 | bytes 1 | tf_op jit(solution)/shard_map/local/pallas_call | solution.py:553
  48.2 0.0 collective-permute-done.8.a3
  48.2 0.0 copy-start.5
  48.2 0.0 copy-start.6
  48.2 0.0 copy-start.9
  48.2 0.0 copy-start.10
  48.3 0.7 plane.1
  48.9 0.0 copy-start.17
  48.9 2.8 %collective-permute-start.12 = (bf16[192,128]{1,0:T(8,128)(2,1)S(1)}, bf16[192,128]{1,0:T(8,128)(2,1)S(1)}, u32[]{:S(2)}, u32[]{:S(2)}) collective-permute-start(bf16[192,128]{1,0:T(8,128)(2,1)S(1)} %get-tuple-element.83), channel_id=1, source_target_pairs={{0,4},{4,0},{8,12},{12,8},{16,20},{20,16},{24,28},{28,24},{32,36},... | collective-permute-start | bytes 147464 | tf_op jit(solution)/shard_map/ppermute | solution.py:656
  51.8 1.0 %collective-permute-start.13 = (bf16[192,128]{1,0:T(8,128)(2,1)S(1)}, bf16[192,128]{1,0:T(8,128)(2,1)S(1)}, u32[]{:S(2)}, u32[]{:S(2)}) collective-permute-start(bf16[192,128]{1,0:T(8,128)(2,1)S(1)} %get-tuple-element.84), channel_id=1, source_target_pairs={{0,8},{4,12},{8,0},{12,4},{16,24},{20,28},{24,16},{28,20},{32,40},... | collective-permute-start | bytes 147464 | tf_op jit(solution)/shard_map/ppermute | solution.py:656
  52.8 1.3 %collective-permute-start.14 = (bf16[192,128]{1,0:T(8,128)(2,1)S(1)}, bf16[192,128]{1,0:T(8,128)(2,1)S(1)}, u32[]{:S(2)}, u32[]{:S(2)}) collective-permute-start(bf16[192,128]{1,0:T(8,128)(2,1)S(1)} %get-tuple-element.85), channel_id=1, source_target_pairs={{0,12},{4,8},{8,4},{12,0},{16,28},{20,24},{24,20},{28,16},{32,44},... | collective-permute-start | bytes 147464 | tf_op jit(solution)/shard_map/ppermute | solution.py:656
  54.1 0.6 copy-done.16
  54.7 4.6 %within.1 = (bf16[512,768]{1,0:T(8,128)(2,1)S(1)}, bf16[512,768]{1,0:T(8,128)(2,1)S(1)}) custom-call(bf16[512,768]{1,0:T(8,128)(2,1)S(1)} %copy-done, bf16[512,768]{1,0:T(8,128)(2,1)S(1)} %copy-done.3, f32[12,512]{1,0:T(8,128)S(1)} %copy-done.9, f32[12,512]{1,0:T(8,128)S(1)} %copy-done.10, s32[1,512]{1,0:T(1,128)S(1)} %bitcast.8, ...), custom_call_target="tpu_custom_call" | custom-call | flops 1 | bytes 1 | tf_op jit(solution)/shard_map/within/pallas_call | solution.py:571
  59.3 6.2 %near.1 = (f32[768,256]{1,0:T(8,128)S(1)}, f32[48,256]{1,0:T(8,128)S(1)}) custom-call(bf16[768,256]{1,0:T(8,128)(2,1)S(1)} %get-tuple-element.89.qe_ref, bf16[384,256]{1,0:T(8,128)(2,1)S(1)} %get-tuple-element.90.plan_ref, f32[768,256]{1,0:T(8,128)S(1)} %get-tuple-element.91.oe_ref, f32[48,256]{1,0:T(8,128)S(1)} %get-tuple-element.92.stat_ref, ...), custom_call_target="tpu_custom_call" | custom-call | flops 1 | bytes 1 | tf_op jit(solution)/shard_map/near/pallas_call | solution.py:608
  65.6 2.0 %collective-permute-done.13.f2 = bf16[192,128]{1,0:T(8,128)(2,1)S(1)} collective-permute-done((bf16[192,128]{1,0:T(8,128)(2,1)S(1)}, bf16[192,128]{1,0:T(8,128)(2,1)S(1)}, u32[]{:S(2)}, u32[]{:S(2)}) %collective-permute-start.13) | collective-permute-done | bytes 49184 | tf_op jit(solution)/shard_map/ppermute | solution.py:656
  67.6 0.9 %collective-permute-done.14.f3 = bf16[192,128]{1,0:T(8,128)(2,1)S(1)} collective-permute-done((bf16[192,128]{1,0:T(8,128)(2,1)S(1)}, bf16[192,128]{1,0:T(8,128)(2,1)S(1)}, u32[]{:S(2)}, u32[]{:S(2)}) %collective-permute-start.14) | collective-permute-done | bytes 49184 | tf_op jit(solution)/shard_map/ppermute | solution.py:656
  68.5 3.1 %finish.1 = bf16[512,768]{1,0:T(8,128)(2,1)} custom-call(s32[3]{0:T(128)S(1)} %copy-done.13, bf16[192,128]{1,0:T(8,128)(2,1)S(1)} %get-tuple-element.98.f0, bf16[192,128]{1,0:T(8,128)(2,1)S(1)} %collective-permute-done.12.f1, bf16[192,128]{1,0:T(8,128)(2,1)S(1)} %collective-permute-done.13.f2, bf16[192,128]{1,0:T(8,128)(2,1)S(1)} %collective-permute-done.14.f3, ...), custom_call_target="tpu_custom_call" | custom-call | flops 1 | bytes 1 | tf_op jit(solution)/shard_map/finish/pallas_call | solution.py:590
  71.6 4.9 %remote.1 = bf16[512,768]{1,0:T(8,128)(2,1)} custom-call(bf16[768,256]{1,0:T(8,128)(2,1)S(1)} %get-tuple-element.89.qe_ref, bf16[384,256]{1,0:T(8,128)(2,1)S(1)} %get-tuple-element.90.plan_ref, f32[768,256]{1,0:T(8,128)S(1)} %get-tuple-element.96.oe_ref, f32[48,256]{1,0:T(8,128)S(1)} %get-tuple-element.97.stat_ref, ...), custom_call_target="tpu_custom_call" | custom-call | flops 1 | bytes 1 | tf_op jit(solution)/shard_map/remote/pallas_call | solution.py:621
  (30 shorter events, 0.1 us)
Async XLA Ops:
  0.6 9.0 %copy-start = (bf16[512,768]{1,0:T(8,128)(2,1)S(1)}, bf16[512,768]{1,0:T(8,128)(2,1)}, u32[]{:S(2)}) copy-start(bf16[512,768]{1,0:T(8,128)(2,1)} %v_ref.5) | copy-start | bytes 2359300
  4.6 7.4 %collective-permute-start = (bf16[208,128]{1,0:T(8,128)(2,1)}, bf16[208,128]{1,0:T(8,128)(2,1)S(1)}, u32[]{:S(2)}, u32[]{:S(2)}) collective-permute-start(bf16[208,128]{1,0:T(8,128)(2,1)} %get-tuple-element.53), channel_id=1, source_target_pairs={{0,4},{4,0},{8,12},{12,8},{16,20},{20,16},{24,28},{28,24},{32,36},... | collective-permute-start | bytes 159752 | tf_op jit(solution)/shard_map/ppermute | solution.py:656
  7.7 2.0 %copy-start.12 = (s32[512]{0:T(512)S(1)}, s32[512]{0:T(512)}, u32[]{:S(2)}) copy-start(s32[512]{0:T(512)} %param.16) | copy-start | bytes 6148
  7.7 4.7 %collective-permute-start.1 = (bf16[208,128]{1,0:T(8,128)(2,1)}, bf16[208,128]{1,0:T(8,128)(2,1)S(1)}, u32[]{:S(2)}, u32[]{:S(2)}) collective-permute-start(bf16[208,128]{1,0:T(8,128)(2,1)} %get-tuple-element.54), channel_id=1, source_target_pairs={{0,8},{4,12},{8,0},{12,4},{16,24},{20,28},{24,16},{28,20},{32,40},... | collective-permute-start | bytes 159752 | tf_op jit(solution)/shard_map/ppermute | solution.py:656
  9.6 6.7 %collective-permute-start.2 = (bf16[208,128]{1,0:T(8,128)(2,1)}, bf16[208,128]{1,0:T(8,128)(2,1)S(1)}, u32[]{:S(2)}, u32[]{:S(2)}) collective-permute-start(bf16[208,128]{1,0:T(8,128)(2,1)} %get-tuple-element.55), channel_id=1, source_target_pairs={{0,12},{4,8},{8,4},{12,0},{16,28},{20,24},{24,20},{28,16},{32,44},... | collective-permute-start | bytes 159752 | tf_op jit(solution)/shard_map/ppermute | solution.py:656
  9.7 1.1 %copy-start.1 = (bf16[512,768]{1,0:T(8,128)(2,1)S(1)}, bf16[512,768]{1,0:T(8,128)(2,1)}, u32[]{:S(2)}) copy-start(bf16[512,768]{1,0:T(8,128)(2,1)} %k_ref.3) | copy-start | bytes 2359300
  10.8 5.6 %copy-start.11 = (bf16[208,128]{1,0:T(8,128)(2,1)S(1)}, bf16[208,128]{1,0:T(8,128)(2,1)}, u32[]{:S(2)}) copy-start(bf16[208,128]{1,0:T(8,128)(2,1)} %get-tuple-element.57.a0) | copy-start | bytes 159748
  10.8 5.6 %copy-start.13 = (s32[3]{0:T(128)S(1)}, s32[3]{0:T(128)}, u32[]{:S(2)}) copy-start(s32[3]{0:T(128)} %pad_add_fusion.place_ref) | copy-start | bytes 40
  10.8 27.7 %copy-start.2 = (bf16[512,768]{1,0:T(8,128)(2,1)S(1)}, bf16[512,768]{1,0:T(8,128)(2,1)}, u32[]{:S(2)}) copy-start(bf16[512,768]{1,0:T(8,128)(2,1)} %k_ref.3) | copy-start | bytes 2359300
  17.0 0.7 copy-start.7
  17.7 10.9 %collective-permute-start.3 = (bf16[208,128]{1,0:T(8,128)(2,1)S(1)}, bf16[208,128]{1,0:T(8,128)(2,1)S(1)}, u32[]{:S(2)}, u32[]{:S(2)}) collective-permute-start(bf16[208,128]{1,0:T(8,128)(2,1)S(1)} %get-tuple-element.62.a0), channel_id=1, source_target_pairs={{0,16},{4,20},{8,24},{12,28},{16,32},{20,36},{24,40},{28,44},{32,4... | collective-permute-start | bytes 159752 | tf_op jit(solution)/shard_map/ppermute | solution.py:661
  21.0 8.6 %collective-permute-start.4 = (bf16[208,128]{1,0:T(8,128)(2,1)S(1)}, bf16[208,128]{1,0:T(8,128)(2,1)S(1)}, u32[]{:S(2)}, u32[]{:S(2)}) collective-permute-start(bf16[208,128]{1,0:T(8,128)(2,1)S(1)} %get-tuple-element.62.a0), channel_id=1, source_target_pairs={{0,32},{4,36},{8,40},{12,44},{16,48},{20,52},{24,56},{28,60},{32,0... | collective-permute-start | bytes 159752 | tf_op jit(solution)/shard_map/ppermute | solution.py:661
  25.5 5.5 %collective-permute-start.5 = (bf16[208,128]{1,0:T(8,128)(2,1)S(1)}, bf16[208,128]{1,0:T(8,128)(2,1)S(1)}, u32[]{:S(2)}, u32[]{:S(2)}) collective-permute-start(bf16[208,128]{1,0:T(8,128)(2,1)S(1)} %get-tuple-element.62.a0), channel_id=1, source_target_pairs={{0,48},{4,52},{8,56},{12,60},{16,0},{20,4},{24,8},{28,12},{32,16},... | collective-permute-start | bytes 159752 | tf_op jit(solution)/shard_map/ppermute | solution.py:661
  28.2 24.6 %collective-permute-start.9 = (bf16[528,768]{1,0:T(8,128)(2,1)S(1)}, bf16[528,768]{1,0:T(8,128)(2,1)}, u32[]{:S(2)}, u32[]{:S(2)}) collective-permute-start(bf16[528,768]{1,0:T(8,128)(2,1)S(1)} %pack.1), channel_id=1, source_target_pairs={{0,4},{4,0},{8,12},{12,8},{16,20},{20,16},{24,28},{28,24},{32,36},... | collective-permute-start | bytes 2433032 | tf_op jit(solution)/shard_map/ppermute | solution.py:656
  31.0 28.3 %collective-permute-start.10 = (bf16[528,768]{1,0:T(8,128)(2,1)S(1)}, bf16[528,768]{1,0:T(8,128)(2,1)}, u32[]{:S(2)}, u32[]{:S(2)}) collective-permute-start(bf16[528,768]{1,0:T(8,128)(2,1)S(1)} %pack.1), channel_id=1, source_target_pairs={{0,8},{4,12},{8,0},{12,4},{16,24},{20,28},{24,16},{28,20},{32,40},... | collective-permute-start | bytes 2433032 | tf_op jit(solution)/shard_map/ppermute | solution.py:656
  32.0 39.6 %collective-permute-start.11 = (bf16[528,768]{1,0:T(8,128)(2,1)S(1)}, bf16[528,768]{1,0:T(8,128)(2,1)S(1)}, u32[]{:S(2)}, u32[]{:S(2)}) collective-permute-start(bf16[528,768]{1,0:T(8,128)(2,1)S(1)} %pack.1), channel_id=1, source_target_pairs={{0,12},{4,8},{8,4},{12,0},{16,28},{20,24},{24,20},{28,16},{32,44},... | collective-permute-start | bytes 2433032 | tf_op jit(solution)/shard_map/ppermute | solution.py:656
  33.9 4.2 %collective-permute-start.6 = (bf16[208,128]{1,0:T(8,128)(2,1)S(1)}, bf16[208,128]{1,0:T(8,128)(2,1)S(1)}, u32[]{:S(2)}, u32[]{:S(2)}) collective-permute-start(bf16[208,128]{1,0:T(8,128)(2,1)S(1)} %get-tuple-element.74.a0), channel_id=1, source_target_pairs={{0,64},{4,68},{8,72},{12,76},{16,80},{20,84},{24,88},{28,92},{32,9... | collective-permute-start | bytes 159752 | tf_op jit(solution)/shard_map/ppermute | solution.py:661
  35.3 12.9 %collective-permute-start.7 = (bf16[208,128]{1,0:T(8,128)(2,1)S(1)}, bf16[208,128]{1,0:T(8,128)(2,1)S(1)}, u32[]{:S(2)}, u32[]{:S(2)}) collective-permute-start(bf16[208,128]{1,0:T(8,128)(2,1)S(1)} %get-tuple-element.74.a0), channel_id=1, source_target_pairs={{0,128},{4,132},{8,136},{12,140},{16,144},{20,148},{24,152},{28,15... | collective-permute-start | bytes 159752 | tf_op jit(solution)/shard_map/ppermute | solution.py:661
  38.1 10.1 %collective-permute-start.8 = (bf16[208,128]{1,0:T(8,128)(2,1)S(1)}, bf16[208,128]{1,0:T(8,128)(2,1)S(1)}, u32[]{:S(2)}, u32[]{:S(2)}) collective-permute-start(bf16[208,128]{1,0:T(8,128)(2,1)S(1)} %get-tuple-element.74.a0), channel_id=1, source_target_pairs={{0,192},{4,196},{8,200},{12,204},{16,208},{20,212},{24,216},{28,22... | collective-permute-start | bytes 159752 | tf_op jit(solution)/shard_map/ppermute | solution.py:661
  38.6 0.7 copy-start.15
  38.6 0.7 copy-start.14
  39.2 1.1 %copy-start.4 = (bf16[512,768]{1,0:T(8,128)(2,1)S(1)}, bf16[512,768]{1,0:T(8,128)(2,1)}, u32[]{:S(2)}) copy-start(bf16[512,768]{1,0:T(8,128)(2,1)} %q_ref.1) | copy-start | bytes 2359300
  40.4 7.8 %copy-start.8 = (f32[4,192,128]{2,1,0:T(8,128)S(1)}, f32[4,192,128]{2,1,0:T(8,128)}, u32[]{:S(2)}) copy-start(f32[4,192,128]{2,1,0:T(8,128)} %copy-done.7) | copy-start | bytes 1179652
  40.4 13.6 %copy-start.3 = (bf16[512,768]{1,0:T(8,128)(2,1)S(1)}, bf16[512,768]{1,0:T(8,128)(2,1)}, u32[]{:S(2)}) copy-start(bf16[512,768]{1,0:T(8,128)(2,1)} %gate_ref.1) | copy-start | bytes 2359300
  48.2 5.8 %copy-start.5 = (bf16[512,128]{1,0:T(8,128)(2,1)S(1)}, bf16[512,128]{1,0:T(8,128)(2,1)}, u32[]{:S(2)}) copy-start(bf16[512,128]{1,0:T(8,128)(2,1)} %into_ref.1) | copy-start | bytes 393220
  48.2 5.8 %copy-start.6 = (bf16[512,128]{1,0:T(8,128)(2,1)S(1)}, bf16[512,128]{1,0:T(8,128)(2,1)}, u32[]{:S(2)}) copy-start(bf16[512,128]{1,0:T(8,128)(2,1)} %read_ref.3) | copy-start | bytes 393220
  48.2 5.8 %copy-start.9 = (f32[12,512]{1,0:T(8,128)S(1)}, f32[12,512]{1,0:T(8,128)}, u32[]{:S(2)}) copy-start(f32[12,512]{1,0:T(8,128)} %steps_ref.1) | copy-start | bytes 73732
  48.2 5.8 %copy-start.10 = (f32[12,512]{1,0:T(8,128)S(1)}, f32[12,512]{1,0:T(8,128)}, u32[]{:S(2)}) copy-start(f32[12,512]{1,0:T(8,128)} %rates_ref.1) | copy-start | bytes 73732
  48.9 5.1 %copy-start.17 = (f32[768]{0:T(1024)S(1)}, f32[768]{0:T(1024)}, u32[]{:S(2)}) copy-start(f32[768]{0:T(1024)} %param.25) | copy-start | bytes 9220
  48.9 16.6 %collective-permute-start.12 = (bf16[192,128]{1,0:T(8,128)(2,1)S(1)}, bf16[192,128]{1,0:T(8,128)(2,1)S(1)}, u32[]{:S(2)}, u32[]{:S(2)}) collective-permute-start(bf16[192,128]{1,0:T(8,128)(2,1)S(1)} %get-tuple-element.83), channel_id=1, source_target_pairs={{0,4},{4,0},{8,12},{12,8},{16,20},{20,16},{24,28},{28,24},{32,36},... | collective-permute-start | bytes 147464 | tf_op jit(solution)/shard_map/ppermute | solution.py:656
  51.8 15.8 %collective-permute-start.13 = (bf16[192,128]{1,0:T(8,128)(2,1)S(1)}, bf16[192,128]{1,0:T(8,128)(2,1)S(1)}, u32[]{:S(2)}, u32[]{:S(2)}) collective-permute-start(bf16[192,128]{1,0:T(8,128)(2,1)S(1)} %get-tuple-element.84), channel_id=1, source_target_pairs={{0,8},{4,12},{8,0},{12,4},{16,24},{20,28},{24,16},{28,20},{32,40},... | collective-permute-start | bytes 147464 | tf_op jit(solution)/shard_map/ppermute | solution.py:656
  52.8 15.7 %collective-permute-start.14 = (bf16[192,128]{1,0:T(8,128)(2,1)S(1)}, bf16[192,128]{1,0:T(8,128)(2,1)S(1)}, u32[]{:S(2)}, u32[]{:S(2)}) collective-permute-start(bf16[192,128]{1,0:T(8,128)(2,1)S(1)} %get-tuple-element.85), channel_id=1, source_target_pairs={{0,12},{4,8},{8,4},{12,0},{16,28},{20,24},{24,20},{28,16},{32,44},... | collective-permute-start | bytes 147464 | tf_op jit(solution)/shard_map/ppermute | solution.py:656
  54.0 0.7 copy-start.16

commit v5 on v4

--- a/solution.py
+++ b/solution.py
@@ -152,8 +152,18 @@
     return jnp.where(count == 1, 0.0, jnp.where(count == 2, LN2_HI + LN2_LO, LN3_HI + LN3_LO))
 
 
-def softmax_columns(keys, queries, values, own, before):
-    scores = dot(keys, queries)
+def staggered(jobs, depth=2):
+    waiting = []
+    for keys, queries, finish in jobs:
+        waiting.append((finish, dot(keys(), queries())))
+        if len(waiting) > depth:
+            finish, scores = waiting.pop(0)
+            finish(scores)
+    for finish, scores in waiting:
+        finish(scores)
+
+
+def softmax_columns(scores, values, own, before):
     if own is not None:
         tile = 128
         diagonal = iota((tile, tile), 0) == iota((tile, tile), 1)
@@ -173,10 +183,18 @@
 
 
 def all_queries(rows, part, plan):
-    blank = jnp.zeros((HEAD_DIM, rows.shape[1]), BF16)
-    pieces = [rows, blank] if part == 0 else [blank, rows]
-    rest = jnp.zeros((128 - plan.shape[0], rows.shape[1]), BF16)
-    return jnp.concatenate(pieces + [plan.astype(BF16), rest], axis=0)
+    rest = jnp.zeros((HEAD_DIM - plan.shape[0], rows.shape[1]), BF16)
+    pieces = [plan.astype(BF16), rest]
+    return jnp.concatenate([rows] + pieces if part == 0 else pieces + [rows], axis=0)
+
+
+def own_lanes(rows, part):
+    lane = iota((rows, 128), 1)
+    return one((lane < HEAD_DIM) == (part == 0), BF16)
+
+
+def plan_lane(rows, part):
+    return iota((rows, 128), 1) - (HEAD_DIM if part == 0 else 0)
 
 
 def local_kernel(
@@ -188,81 +206,100 @@
     valid = jnp.broadcast_to(valid_ref[...].astype(F32), (128, ROWS)).astype(BF16)
     flags = dot(valid, unsort_ref[...])
     ve_ref[...] = flags[:8]
-    row, lane = iota((ROWS, 128), 0), iota((ROWS, 128), 1)
-    key_side = one(((row >> 5) == (lane & 15)) & (lane < 32))
-    key_side = jnp.where(lane == 32, (1.0 - flags.T) * NEG, key_side).astype(BF16)
+    row = iota((ROWS, 128), 0)
+    hidden = (1.0 - flags.T) * NEG
+    sides, masks = [], []
+    for part in range(2):
+        lane = plan_lane(ROWS, part)
+        side = one(((row >> 5) == (lane & 15)) & (lane >= 0) & (lane < 32))
+        sides.append(jnp.where(lane == 32, hidden, side).astype(BF16))
+        masks.append(own_lanes(ROWS, part))
     sq_ref[...] = t_dot(q_ref[...], unsort_ref[...]) * (HEAD_DIM**-0.5)
     sk_ref[...] = t_dot(k_ref[...], unsort_ref[...])
     sv_ref[...] = t_dot(v_ref[...], unsort_ref[...]).astype(BF16)
-    for pair in range(PAIRS):
+    def job(pair, part):
         both = slice(pair * 128, (pair + 1) * 128)
-        key = sk_ref[both, :].T.astype(BF16)
-        keys = jnp.concatenate([key, key_side], axis=1)
-        stats = []
-        for part in range(2):
-            head = rank_ref[0] * HEADS_HERE + 2 * pair + part
-            start = pair * 128 + part * HEAD_DIM
-            now = slice(start, start + HEAD_DIM)
+        head = rank_ref[0] * HEADS_HERE + 2 * pair + part
+        start = pair * 128 + part * HEAD_DIM
+        now = slice(start, start + HEAD_DIM)
+        inside = slice(part * HALF, (part + 1) * HALF)
+        outside = slice((1 - part) * HALF, (2 - part) * HALF)
+
+        def keys():
+            return sk_ref[both, :].T.astype(BF16) * masks[part] + sides[part]
+
+        def queries():
+            return all_queries(sq_ref[now, :].astype(BF16), part, local_plan(head, seg_ref, dil_ref))
+
+        def finish(scores):
             query = sq_ref[now, :]
-            queries = all_queries(query.astype(BF16), part, local_plan(head, seg_ref, dil_ref))
             own = jnp.sum(query * sk_ref[now, :], axis=0, keepdims=True) + own_bias(head, dil_ref)
-            out, total, top = softmax_columns(keys, queries, sv_ref[now, :], own, None)
-            inside = slice(part * HALF, (part + 1) * HALF)
-            outside = slice((1 - part) * HALF, (2 - part) * HALF)
+            out, total, top = softmax_columns(scores, sv_ref[now, :], own, None)
             qe_ref[now, :] = query[:, inside].astype(BF16)
             oe_ref[now, :] = out[:, inside]
             oo_ref[now, :] = (out[:, outside] / total[:, outside] * flags[:1, outside]).astype(BF16)
-            stats += [top[:, inside], total[:, inside]]
             at = (2 * pair + part) * 32
             plan_ref[at : at + 32, :] = remote_plan(head, seg_ref, dil_ref).astype(BF16)
-        stat_ref[pair * 8 : pair * 8 + 8, :] = jnp.concatenate(stats + [jnp.zeros((4, HALF), F32)], axis=0)
+            stat = pair * 8 + 2 * part
+            stat_ref[stat : stat + 1, :] = top[:, inside]
+            stat_ref[stat + 1 : stat + 2, :] = total[:, inside]
+
+        return keys, queries, finish
+
+    staggered([job(pair, part) for pair in range(PAIRS) for part in range(2)])
 
 
 def remote_kernel(near, qe_ref, plan_ref, oe_ref, stat_ref, oo_ref, ve_ref, *rest):
     blocks, outs = (rest[:2], rest[2:]) if near else (rest[:1], rest[1:])
-    spread = one((iota((16, 128), 0) == 0) & (iota((16, 128), 1) == 16), BF16)
-    row, lane = iota((HALF, 128), 0), iota((HALF, 128), 1)
-    wanted = ((lane & 3) == (row >> 6)) & (lane < 16)
-    close, distant = one(wanted & (lane < 8)), one(wanted & (lane >= 8))
-    sides = []
-    for parity in range(2):
+    row = iota((HALF, 128), 0)
+    sides, masks = [], []
+    for part in range(2):
+        lane = plan_lane(HALF, part)
+        first = one((iota((16, 128), 0) == 0) & (plan_lane(16, part) == 16), BF16)
+        same = ((lane & 3) == (row >> 6)) & (lane >= 0)
+        close, distant = one(same & (lane < 8)), one(same & (lane >= 8) & (lane < 16))
         pieces = []
         for ref, group in zip(blocks, (close, distant) if near else (distant,)):
-            flags = ref[ROWS : ROWS + 16, parity * HALF : (parity + 1) * HALF].astype(F32)
-            pieces.append(t_dot(((1.0 - flags) * NEG).astype(BF16), spread) + group)
+            flags = ref[ROWS : ROWS + 16, part * HALF : (part + 1) * HALF].astype(F32)
+            pieces.append(t_dot(((1.0 - flags) * NEG).astype(BF16), first) + group)
         sides.append(jnp.concatenate(pieces, axis=0).astype(BF16))
-    for pair in range(PAIRS):
+        masks.append(own_lanes(HALF * len(blocks), part))
+    def job(pair, part):
         both = slice(pair * 128, (pair + 1) * 128)
-        place = slice(HALF + (pair & 1) * 128, HALF + (pair & 1) * 128 + 128)
+        start = pair * 128 + part * HEAD_DIM
+        now = slice(start, start + HEAD_DIM)
+        place = start % HALF + HALF
+        place = slice(place, place + HEAD_DIM)
         chunk = slice((pair >> 1) * HALF, (pair >> 1) * HALF + HALF)
-        key = jnp.concatenate([ref[:HALF, both] for ref in blocks], axis=0)
-        value = jnp.concatenate([ref[place, chunk] for ref in blocks], axis=1)
-        stats = []
-        for part in range(2):
-            start = pair * 128 + part * HEAD_DIM
-            now = slice(start, start + HEAD_DIM)
-            at = (2 * pair + part) * 32
-            keys = jnp.concatenate([key, sides[part]], axis=1)
-            queries = all_queries(qe_ref[now, :], part, plan_ref[at : at + 32, :])
-            stat = pair * 8 + 2 * part
+        at = (2 * pair + part) * 32
+        stat = pair * 8 + 2 * part
+
+        def keys():
+            key = jnp.concatenate([ref[:HALF, both] for ref in blocks], axis=0)
+            return key * masks[part] + sides[part]
+
+        def queries():
+            return all_queries(qe_ref[now, :], part, plan_ref[at : at + 32, :])
+
+        def finish(scores):
+            value = jnp.concatenate([ref[place, chunk] for ref in blocks], axis=1)
             before = stat_ref[stat : stat + 1, :]
-            out, total, top = softmax_columns(
-                keys, queries, value[part * HEAD_DIM : (part + 1) * HEAD_DIM], None, before
-            )
+            out, total, top = softmax_columns(scores, value, None, before)
             rescale = jnp.exp(before - top)
             out = out + oe_ref[now, :] * rescale
             total = total + stat_ref[stat + 1 : stat + 2, :] * rescale
             if near:
                 outs[0][now, :] = out
-                stats += [top, total]
-                continue
+                outs[1][stat : stat + 1, :] = top
+                outs[1][stat + 1 : stat + 2, :] = total
+                return
             done = out / total * ve_ref[:1, part * HALF : (part + 1) * HALF]
             outs[1][now, part * HALF : (part + 1) * HALF] = done.astype(BF16)
             outs[1][now, (1 - part) * HALF : (2 - part) * HALF] = oo_ref[now, :]
-        if near:
-            outs[1][pair * 8 : pair * 8 + 8, :] = jnp.concatenate(
-                stats + [jnp.zeros((4, HALF), F32)], axis=0
-            )
+
+        return keys, queries, finish
+
+    staggered([job(pair, part) for pair in range(PAIRS) for part in range(2)])
     if not near:
         outs[0][...] = dot_t(unsorting(), outs[1][...]).astype(BF16)
 

time: 76.7 us -> 75 us (0.978)
  Pallas kernels: 32.9 us -> 27.4 us
  waiting for transfers between devices: 11.9 us -> 15.6 us
    ppermute x9, waiting for transfers between devices: 7.34 us -> 11.1 us  [cross(): return lax.ppermute(block, 'seq', [(i, i ^ mask) for i in range(count)])]
    pallas_call x1, Pallas kernels: 6.21 us -> 3.86 us  [call_near(): pl.pallas_call(functools.partial(remote_kernel, True), out_shape=[KEPT[2]...]
    pallas_call x1, Pallas kernels: 4.87 us -> 3.1 us  [call_remote(): pl.pallas_call(functools.partial(remote_kernel, False), out_shape=shape(R...]
    pallas_call x1, Pallas kernels: 7.78 us -> 6.41 us  [call_local(): pl.pallas_call(local_kernel, out_shape=KEPT, in_specs=[VMEM] * 4 + [SMEM]...]
  transfers between devices with their start and end apart: 15 -> 15, of which waited for: 7 -> 8; matrix products, arithmetic and copies ran while one was open for 0% -> 0% of each run, Pallas kernels for 32% -> 27%
where the time goes in v5:
time: 75 us; the launch traced here: 74.7 us
  Pallas kernels  27.4 us (37%)
  starting transfers between devices  25.8 us (34%)
  waiting for transfers between devices  15.6 us (21%)
  local copies, waits for them, and re-layouts  4.37 us (6%)
  between operations  0.85 us (1%)
    ppermute x9, starting transfers between devices, cross(): return lax.ppermute(block, 'seq', [(i, i ^ mask) for i in range(count)])  12.9 us
    ppermute x6, starting transfers between devices, turn(): return lax.ppermute(block, 'seq', route)  12.9 us
    ppermute x9, waiting for transfers between devices, cross(): return lax.ppermute(block, 'seq', [(i, i ^ mask) for i in range(count)])  11.1 us
    pallas_call x1, Pallas kernels, call_local(): pl.pallas_call(local_kernel, out_shape=KEPT, in_specs=[VMEM] * 4 + [SMEM]...  6.41 us
    pallas_call x1, Pallas kernels, call_within(): pl.pallas_call(within_kernel, grid=(PAIRS,), out_shape=[shape(ROWS, WIDTH...  4.64 us
    ppermute x6, waiting for transfers between devices, turn(): return lax.ppermute(block, 'seq', route)  4.54 us
    unnamed x36, local copies, waits for them, and re-layouts  4.36 us
    pallas_call x1, Pallas kernels, call_near(): pl.pallas_call(functools.partial(remote_kernel, True), out_shape=[KEPT[2]...  3.86 us
  transfers between devices with their start and end apart: 15, of which 8 were waited for; matrix products, arithmetic and copies ran while one was open for 0% of the time, Pallas kernels for 27%

profile of v5, /device:TPU:16, one launch (start us, length us, event | category | flops | bytes accessed | tf_op | source)
XLA Modules:
  0.0 74.7 jit_solution(1308630978680732842)
XLA Ops:
  0.6 0.0 copy-start
  0.6 0.7 pad_add_fusion.place_ref
  1.3 3.3 %state.1 = (bf16[208,128]{1,0:T(8,128)(2,1)}, bf16[208,128]{1,0:T(8,128)(2,1)}, bf16[208,128]{1,0:T(8,128)(2,1)}, bf16[208,128]{1,0:T(8,128)(2,1)}) custom-call(bf16[512,768]{1,0:T(8,128)(2,1)} %v_ref.5, f32[12,512]{1,0:T(8,128)} %steps_ref.1, f32[12,512]{1,0:T(8,128)} %rates_ref.1, s32[1,512]{1,0:T(1,128)} %bitcast.5, bf16[512,128]{1,0:T(8,128)(2,1)} %into_ref.1, ...), custom_call_target="tpu_custom_call" | custom-call | flops 1 | bytes 1 | tf_op jit(solution)/shard_map/state/pallas_call | solution.py:517
  4.6 3.1 %collective-permute-start = (bf16[208,128]{1,0:T(8,128)(2,1)}, bf16[208,128]{1,0:T(8,128)(2,1)S(1)}, u32[]{:S(2)}, u32[]{:S(2)}) collective-permute-start(bf16[208,128]{1,0:T(8,128)(2,1)} %get-tuple-element.53), channel_id=1, source_target_pairs={{0,4},{4,0},{8,12},{12,8},{16,20},{20,16},{24,28},{28,24},{32,36},... | collective-permute-start | bytes 159752 | tf_op jit(solution)/shard_map/ppermute | solution.py:693
  7.7 1.9 %collective-permute-start.1 = (bf16[208,128]{1,0:T(8,128)(2,1)}, bf16[208,128]{1,0:T(8,128)(2,1)S(1)}, u32[]{:S(2)}, u32[]{:S(2)}) collective-permute-start(bf16[208,128]{1,0:T(8,128)(2,1)} %get-tuple-element.54), channel_id=1, source_target_pairs={{0,8},{4,12},{8,0},{12,4},{16,24},{20,28},{24,16},{28,20},{32,40},... | collective-permute-start | bytes 159752 | tf_op jit(solution)/shard_map/ppermute | solution.py:693
  9.6 0.1 collective-permute-start.2
  9.7 1.1 %copy-done.1 = bf16[512,768]{1,0:T(8,128)(2,1)S(1)} copy-done((bf16[512,768]{1,0:T(8,128)(2,1)S(1)}, bf16[512,768]{1,0:T(8,128)(2,1)}, u32[]{:S(2)}) %copy-start.1) | copy-done | bytes 786456
  10.8 1.1 %pack.1 = bf16[528,768]{1,0:T(8,128)(2,1)S(1)} custom-call(bf16[512,768]{1,0:T(8,128)(2,1)S(1)} %copy-done.1, bf16[512,768]{1,0:T(8,128)(2,1)S(1)} %copy-done, s32[1,512]{1,0:T(1,128)S(1)} %bitcast.6), custom_call_target="tpu_custom_call" | custom-call | flops 1 | bytes 1 | tf_op jit(solution)/shard_map/pack/pallas_call | solution.py:504
  11.9 0.0 collective-permute-done.a1
  12.0 0.5 collective-permute-done.1.a2
  12.4 3.9 %collective-permute-done.2.a3 = bf16[208,128]{1,0:T(8,128)(2,1)S(1)} collective-permute-done((bf16[208,128]{1,0:T(8,128)(2,1)}, bf16[208,128]{1,0:T(8,128)(2,1)S(1)}, u32[]{:S(2)}, u32[]{:S(2)}) %collective-permute-start.2) | collective-permute-done | bytes 53280 | tf_op jit(solution)/shard_map/ppermute | solution.py:693
  16.4 0.6 block.1
  17.0 0.0 copy-start.7
  17.0 0.7 copy-done.7
  17.7 3.3 %collective-permute-start.3 = (bf16[208,128]{1,0:T(8,128)(2,1)S(1)}, bf16[208,128]{1,0:T(8,128)(2,1)S(1)}, u32[]{:S(2)}, u32[]{:S(2)}) collective-permute-start(bf16[208,128]{1,0:T(8,128)(2,1)S(1)} %get-tuple-element.62.a0), channel_id=1, source_target_pairs={{0,16},{4,20},{8,24},{12,28},{16,32},{20,36},{24,40},{28,44},{32,4... | collective-permute-start | bytes 159752 | tf_op jit(solution)/shard_map/ppermute | solution.py:698
  21.0 4.5 %collective-permute-start.4 = (bf16[208,128]{1,0:T(8,128)(2,1)S(1)}, bf16[208,128]{1,0:T(8,128)(2,1)S(1)}, u32[]{:S(2)}, u32[]{:S(2)}) collective-permute-start(bf16[208,128]{1,0:T(8,128)(2,1)S(1)} %get-tuple-element.62.a0), channel_id=1, source_target_pairs={{0,32},{4,36},{8,40},{12,44},{16,48},{20,52},{24,56},{28,60},{32,0... | collective-permute-start | bytes 159752 | tf_op jit(solution)/shard_map/ppermute | solution.py:698
  25.5 2.7 %collective-permute-start.5 = (bf16[208,128]{1,0:T(8,128)(2,1)S(1)}, bf16[208,128]{1,0:T(8,128)(2,1)S(1)}, u32[]{:S(2)}, u32[]{:S(2)}) collective-permute-start(bf16[208,128]{1,0:T(8,128)(2,1)S(1)} %get-tuple-element.62.a0), channel_id=1, source_target_pairs={{0,48},{4,52},{8,56},{12,60},{16,0},{20,4},{24,8},{28,12},{32,16},... | collective-permute-start | bytes 159752 | tf_op jit(solution)/shard_map/ppermute | solution.py:698
  28.2 0.5 collective-permute-start.9
  28.7 0.9 %collective-permute-done.4.a2 = bf16[208,128]{1,0:T(8,128)(2,1)S(1)} collective-permute-done((bf16[208,128]{1,0:T(8,128)(2,1)S(1)}, bf16[208,128]{1,0:T(8,128)(2,1)S(1)}, u32[]{:S(2)}, u32[]{:S(2)}) %collective-permute-start.4) | collective-permute-done | bytes 53280 | tf_op jit(solution)/shard_map/ppermute | solution.py:698
  29.6 1.4 %collective-permute-done.5.a3 = bf16[208,128]{1,0:T(8,128)(2,1)S(1)} collective-permute-done((bf16[208,128]{1,0:T(8,128)(2,1)S(1)}, bf16[208,128]{1,0:T(8,128)(2,1)S(1)}, u32[]{:S(2)}, u32[]{:S(2)}) %collective-permute-start.5) | collective-permute-done | bytes 53280 | tf_op jit(solution)/shard_map/ppermute | solution.py:698
  31.0 1.0 %collective-permute-start.10 = (bf16[528,768]{1,0:T(8,128)(2,1)S(1)}, bf16[528,768]{1,0:T(8,128)(2,1)}, u32[]{:S(2)}, u32[]{:S(2)}) collective-permute-start(bf16[528,768]{1,0:T(8,128)(2,1)S(1)} %pack.1), channel_id=1, source_target_pairs={{0,8},{4,12},{8,0},{12,4},{16,24},{20,28},{24,16},{28,20},{32,40},... | collective-permute-start | bytes 2433032 | tf_op jit(solution)/shard_map/ppermute | solution.py:693
  32.0 1.3 %collective-permute-start.11 = (bf16[528,768]{1,0:T(8,128)(2,1)S(1)}, bf16[528,768]{1,0:T(8,128)(2,1)S(1)}, u32[]{:S(2)}, u32[]{:S(2)}) collective-permute-start(bf16[528,768]{1,0:T(8,128)(2,1)S(1)} %pack.1), channel_id=1, source_target_pairs={{0,12},{4,8},{8,4},{12,0},{16,28},{20,24},{24,20},{28,16},{32,44},... | collective-permute-start | bytes 2433032 | tf_op jit(solution)/shard_map/ppermute | solution.py:693
  33.3 0.6 line.1
  33.9 1.4 %collective-permute-start.6 = (bf16[208,128]{1,0:T(8,128)(2,1)S(1)}, bf16[208,128]{1,0:T(8,128)(2,1)S(1)}, u32[]{:S(2)}, u32[]{:S(2)}) collective-permute-start(bf16[208,128]{1,0:T(8,128)(2,1)S(1)} %get-tuple-element.74.a0), channel_id=1, source_target_pairs={{0,64},{4,68},{8,72},{12,76},{16,80},{20,84},{24,88},{28,92},{32,9... | collective-permute-start | bytes 159752 | tf_op jit(solution)/shard_map/ppermute | solution.py:698
  35.3 0.6 collective-permute-start.7
  35.9 2.2 %collective-permute-done.6.a1 = bf16[208,128]{1,0:T(8,128)(2,1)S(1)} collective-permute-done((bf16[208,128]{1,0:T(8,128)(2,1)S(1)}, bf16[208,128]{1,0:T(8,128)(2,1)S(1)}, u32[]{:S(2)}, u32[]{:S(2)}) %collective-permute-start.6) | collective-permute-done | bytes 53280 | tf_op jit(solution)/shard_map/ppermute | solution.py:698
  38.1 0.4 collective-permute-start.8
  38.6 0.7 copy-done.15
  39.2 0.0 copy-done.14
  39.3 1.1 %copy-done.4 = bf16[512,768]{1,0:T(8,128)(2,1)S(1)} copy-done((bf16[512,768]{1,0:T(8,128)(2,1)S(1)}, bf16[512,768]{1,0:T(8,128)(2,1)}, u32[]{:S(2)}) %copy-start.4) | copy-done | bytes 786456
  40.4 6.4 %local.1 = (bf16[768,256]{1,0:T(8,128)(2,1)S(1)}, bf16[384,256]{1,0:T(8,128)(2,1)S(1)}, f32[768,256]{1,0:T(8,128)S(1)}, f32[48,256]{1,0:T(8,128)S(1)}, bf16[768,...) custom-call(bf16[512,768]{1,0:T(8,128)(2,1)S(1)} %copy-done.4, bf16[512,768]{1,0:T(8,128)(2,1)S(1)} %copy-done.2, ...), custom_call_target="tpu_custom_call" | custom-call | flops 1 | bytes 1 | tf_op jit(solution)/shard_map/local/pallas_call | solution.py:590
  46.8 0.0 copy-start.5
  46.8 0.0 copy-start.6
  46.9 0.0 copy-start.9
  46.9 0.0 copy-start.10
  46.9 0.7 plane.1
  47.5 0.0 copy-start.17
  47.6 2.8 %collective-permute-start.12 = (bf16[192,128]{1,0:T(8,128)(2,1)S(1)}, bf16[192,128]{1,0:T(8,128)(2,1)S(1)}, u32[]{:S(2)}, u32[]{:S(2)}) collective-permute-start(bf16[192,128]{1,0:T(8,128)(2,1)S(1)} %get-tuple-element.83), channel_id=1, source_target_pairs={{0,4},{4,0},{8,12},{12,8},{16,20},{20,16},{24,28},{28,24},{32,36},... | collective-permute-start | bytes 147464 | tf_op jit(solution)/shard_map/ppermute | solution.py:693
  50.4 1.0 %collective-permute-start.13 = (bf16[192,128]{1,0:T(8,128)(2,1)S(1)}, bf16[192,128]{1,0:T(8,128)(2,1)S(1)}, u32[]{:S(2)}, u32[]{:S(2)}) collective-permute-start(bf16[192,128]{1,0:T(8,128)(2,1)S(1)} %get-tuple-element.84), channel_id=1, source_target_pairs={{0,8},{4,12},{8,0},{12,4},{16,24},{20,28},{24,16},{28,20},{32,40},... | collective-permute-start | bytes 147464 | tf_op jit(solution)/shard_map/ppermute | solution.py:693
  51.4 1.3 %collective-permute-start.14 = (bf16[192,128]{1,0:T(8,128)(2,1)S(1)}, bf16[192,128]{1,0:T(8,128)(2,1)S(1)}, u32[]{:S(2)}, u32[]{:S(2)}) collective-permute-start(bf16[192,128]{1,0:T(8,128)(2,1)S(1)} %get-tuple-element.85), channel_id=1, source_target_pairs={{0,12},{4,8},{8,4},{12,0},{16,28},{20,24},{24,20},{28,16},{32,44},... | collective-permute-start | bytes 147464 | tf_op jit(solution)/shard_map/ppermute | solution.py:693
  52.7 0.6 copy-done.16
  53.3 4.6 %within.1 = (bf16[512,768]{1,0:T(8,128)(2,1)S(1)}, bf16[512,768]{1,0:T(8,128)(2,1)S(1)}) custom-call(bf16[512,768]{1,0:T(8,128)(2,1)S(1)} %copy-done, bf16[512,768]{1,0:T(8,128)(2,1)S(1)} %copy-done.3, f32[12,512]{1,0:T(8,128)S(1)} %copy-done.9, f32[12,512]{1,0:T(8,128)S(1)} %copy-done.10, s32[1,512]{1,0:T(1,128)S(1)} %bitcast.8, ...), custom_call_target="tpu_custom_call" | custom-call | flops 1 | bytes 1 | tf_op jit(solution)/shard_map/within/pallas_call | solution.py:608
  58.0 3.9 %near.1 = (f32[768,256]{1,0:T(8,128)S(1)}, f32[48,256]{1,0:T(8,128)S(1)}) custom-call(bf16[768,256]{1,0:T(8,128)(2,1)S(1)} %get-tuple-element.89.qe_ref, bf16[384,256]{1,0:T(8,128)(2,1)S(1)} %get-tuple-element.90.plan_ref, f32[768,256]{1,0:T(8,128)S(1)} %get-tuple-element.91.oe_ref, f32[48,256]{1,0:T(8,128)S(1)} %get-tuple-element.92.stat_ref, ...), custom_call_target="tpu_custom_call" | custom-call | flops 1 | bytes 1 | tf_op jit(solution)/shard_map/near/pallas_call | solution.py:645
  61.8 2.2 %collective-permute-done.12.f1 = bf16[192,128]{1,0:T(8,128)(2,1)S(1)} collective-permute-done((bf16[192,128]{1,0:T(8,128)(2,1)S(1)}, bf16[192,128]{1,0:T(8,128)(2,1)S(1)}, u32[]{:S(2)}, u32[]{:S(2)}) %collective-permute-start.12) | collective-permute-done | bytes 49184 | tf_op jit(solution)/shard_map/ppermute | solution.py:693
  64.0 3.5 %collective-permute-done.13.f2 = bf16[192,128]{1,0:T(8,128)(2,1)S(1)} collective-permute-done((bf16[192,128]{1,0:T(8,128)(2,1)S(1)}, bf16[192,128]{1,0:T(8,128)(2,1)S(1)}, u32[]{:S(2)}, u32[]{:S(2)}) %collective-permute-start.13) | collective-permute-done | bytes 49184 | tf_op jit(solution)/shard_map/ppermute | solution.py:693
  67.6 0.9 %collective-permute-done.14.f3 = bf16[192,128]{1,0:T(8,128)(2,1)S(1)} collective-permute-done((bf16[192,128]{1,0:T(8,128)(2,1)S(1)}, bf16[192,128]{1,0:T(8,128)(2,1)S(1)}, u32[]{:S(2)}, u32[]{:S(2)}) %collective-permute-start.14) | collective-permute-done | bytes 49184 | tf_op jit(solution)/shard_map/ppermute | solution.py:693
  68.5 3.1 %finish.1 = bf16[512,768]{1,0:T(8,128)(2,1)} custom-call(s32[3]{0:T(128)S(1)} %copy-done.13, bf16[192,128]{1,0:T(8,128)(2,1)S(1)} %get-tuple-element.98.f0, bf16[192,128]{1,0:T(8,128)(2,1)S(1)} %collective-permute-done.12.f1, bf16[192,128]{1,0:T(8,128)(2,1)S(1)} %collective-permute-done.13.f2, bf16[192,128]{1,0:T(8,128)(2,1)S(1)} %collective-permute-done.14.f3, ...), custom_call_target="tpu_custom_call" | custom-call | flops 1 | bytes 1 | tf_op jit(solution)/shard_map/finish/pallas_call | solution.py:627
  71.6 3.1 %remote.1 = bf16[512,768]{1,0:T(8,128)(2,1)} custom-call(bf16[768,256]{1,0:T(8,128)(2,1)S(1)} %get-tuple-element.89.qe_ref, bf16[384,256]{1,0:T(8,128)(2,1)S(1)} %get-tuple-element.90.plan_ref, f32[768,256]{1,0:T(8,128)S(1)} %get-tuple-element.96.oe_ref, f32[48,256]{1,0:T(8,128)S(1)} %get-tuple-element.97.stat_ref, ...), custom_call_target="tpu_custom_call" | custom-call | flops 1 | bytes 1 | tf_op jit(solution)/shard_map/remote/pallas_call | solution.py:658
  (30 shorter events, 0.1 us)
Async XLA Ops:
  0.6 9.0 %copy-start = (bf16[512,768]{1,0:T(8,128)(2,1)S(1)}, bf16[512,768]{1,0:T(8,128)(2,1)}, u32[]{:S(2)}) copy-start(bf16[512,768]{1,0:T(8,128)(2,1)} %v_ref.5) | copy-start | bytes 2359300
  4.6 7.4 %collective-permute-start = (bf16[208,128]{1,0:T(8,128)(2,1)}, bf16[208,128]{1,0:T(8,128)(2,1)S(1)}, u32[]{:S(2)}, u32[]{:S(2)}) collective-permute-start(bf16[208,128]{1,0:T(8,128)(2,1)} %get-tuple-element.53), channel_id=1, source_target_pairs={{0,4},{4,0},{8,12},{12,8},{16,20},{20,16},{24,28},{28,24},{32,36},... | collective-permute-start | bytes 159752 | tf_op jit(solution)/shard_map/ppermute | solution.py:693
  7.7 2.0 %copy-start.12 = (s32[512]{0:T(512)S(1)}, s32[512]{0:T(512)}, u32[]{:S(2)}) copy-start(s32[512]{0:T(512)} %param.16) | copy-start | bytes 6148
  7.7 4.7 %collective-permute-start.1 = (bf16[208,128]{1,0:T(8,128)(2,1)}, bf16[208,128]{1,0:T(8,128)(2,1)S(1)}, u32[]{:S(2)}, u32[]{:S(2)}) collective-permute-start(bf16[208,128]{1,0:T(8,128)(2,1)} %get-tuple-element.54), channel_id=1, source_target_pairs={{0,8},{4,12},{8,0},{12,4},{16,24},{20,28},{24,16},{28,20},{32,40},... | collective-permute-start | bytes 159752 | tf_op jit(solution)/shard_map/ppermute | solution.py:693
  9.6 6.7 %collective-permute-start.2 = (bf16[208,128]{1,0:T(8,128)(2,1)}, bf16[208,128]{1,0:T(8,128)(2,1)S(1)}, u32[]{:S(2)}, u32[]{:S(2)}) collective-permute-start(bf16[208,128]{1,0:T(8,128)(2,1)} %get-tuple-element.55), channel_id=1, source_target_pairs={{0,12},{4,8},{8,4},{12,0},{16,28},{20,24},{24,20},{28,16},{32,44},... | collective-permute-start | bytes 159752 | tf_op jit(solution)/shard_map/ppermute | solution.py:693
  9.7 1.1 %copy-start.1 = (bf16[512,768]{1,0:T(8,128)(2,1)S(1)}, bf16[512,768]{1,0:T(8,128)(2,1)}, u32[]{:S(2)}) copy-start(bf16[512,768]{1,0:T(8,128)(2,1)} %k_ref.3) | copy-start | bytes 2359300
  10.8 5.6 %copy-start.11 = (bf16[208,128]{1,0:T(8,128)(2,1)S(1)}, bf16[208,128]{1,0:T(8,128)(2,1)}, u32[]{:S(2)}) copy-start(bf16[208,128]{1,0:T(8,128)(2,1)} %get-tuple-element.57.a0) | copy-start | bytes 159748
  10.8 5.6 %copy-start.13 = (s32[3]{0:T(128)S(1)}, s32[3]{0:T(128)}, u32[]{:S(2)}) copy-start(s32[3]{0:T(128)} %pad_add_fusion.place_ref) | copy-start | bytes 40
  10.8 27.7 %copy-start.2 = (bf16[512,768]{1,0:T(8,128)(2,1)S(1)}, bf16[512,768]{1,0:T(8,128)(2,1)}, u32[]{:S(2)}) copy-start(bf16[512,768]{1,0:T(8,128)(2,1)} %k_ref.3) | copy-start | bytes 2359300
  17.0 0.7 %copy-start.7 = (f32[4,192,128]{2,1,0:T(8,128)}, f32[4,192,128]{2,1,0:T(8,128)S(1)}, u32[]{:S(2)}) copy-start(f32[4,192,128]{2,1,0:T(8,128)S(1)} %get-tuple-element.80.block_before) | copy-start | bytes 1179652
  17.7 10.9 %collective-permute-start.3 = (bf16[208,128]{1,0:T(8,128)(2,1)S(1)}, bf16[208,128]{1,0:T(8,128)(2,1)S(1)}, u32[]{:S(2)}, u32[]{:S(2)}) collective-permute-start(bf16[208,128]{1,0:T(8,128)(2,1)S(1)} %get-tuple-element.62.a0), channel_id=1, source_target_pairs={{0,16},{4,20},{8,24},{12,28},{16,32},{20,36},{24,40},{28,44},{32,4... | collective-permute-start | bytes 159752 | tf_op jit(solution)/shard_map/ppermute | solution.py:698
  21.0 8.6 %collective-permute-start.4 = (bf16[208,128]{1,0:T(8,128)(2,1)S(1)}, bf16[208,128]{1,0:T(8,128)(2,1)S(1)}, u32[]{:S(2)}, u32[]{:S(2)}) collective-permute-start(bf16[208,128]{1,0:T(8,128)(2,1)S(1)} %get-tuple-element.62.a0), channel_id=1, source_target_pairs={{0,32},{4,36},{8,40},{12,44},{16,48},{20,52},{24,56},{28,60},{32,0... | collective-permute-start | bytes 159752 | tf_op jit(solution)/shard_map/ppermute | solution.py:698
  25.5 5.5 %collective-permute-start.5 = (bf16[208,128]{1,0:T(8,128)(2,1)S(1)}, bf16[208,128]{1,0:T(8,128)(2,1)S(1)}, u32[]{:S(2)}, u32[]{:S(2)}) collective-permute-start(bf16[208,128]{1,0:T(8,128)(2,1)S(1)} %get-tuple-element.62.a0), channel_id=1, source_target_pairs={{0,48},{4,52},{8,56},{12,60},{16,0},{20,4},{24,8},{28,12},{32,16},... | collective-permute-start | bytes 159752 | tf_op jit(solution)/shard_map/ppermute | solution.py:698
  28.2 23.2 %collective-permute-start.9 = (bf16[528,768]{1,0:T(8,128)(2,1)S(1)}, bf16[528,768]{1,0:T(8,128)(2,1)}, u32[]{:S(2)}, u32[]{:S(2)}) collective-permute-start(bf16[528,768]{1,0:T(8,128)(2,1)S(1)} %pack.1), channel_id=1, source_target_pairs={{0,4},{4,0},{8,12},{12,8},{16,20},{20,16},{24,28},{28,24},{32,36},... | collective-permute-start | bytes 2433032 | tf_op jit(solution)/shard_map/ppermute | solution.py:693
  31.0 27.0 %collective-permute-start.10 = (bf16[528,768]{1,0:T(8,128)(2,1)S(1)}, bf16[528,768]{1,0:T(8,128)(2,1)}, u32[]{:S(2)}, u32[]{:S(2)}) collective-permute-start(bf16[528,768]{1,0:T(8,128)(2,1)S(1)} %pack.1), channel_id=1, source_target_pairs={{0,8},{4,12},{8,0},{12,4},{16,24},{20,28},{24,16},{28,20},{32,40},... | collective-permute-start | bytes 2433032 | tf_op jit(solution)/shard_map/ppermute | solution.py:693
  32.0 39.6 %collective-permute-start.11 = (bf16[528,768]{1,0:T(8,128)(2,1)S(1)}, bf16[528,768]{1,0:T(8,128)(2,1)S(1)}, u32[]{:S(2)}, u32[]{:S(2)}) collective-permute-start(bf16[528,768]{1,0:T(8,128)(2,1)S(1)} %pack.1), channel_id=1, source_target_pairs={{0,12},{4,8},{8,4},{12,0},{16,28},{20,24},{24,20},{28,16},{32,44},... | collective-permute-start | bytes 2433032 | tf_op jit(solution)/shard_map/ppermute | solution.py:693
  33.9 4.2 %collective-permute-start.6 = (bf16[208,128]{1,0:T(8,128)(2,1)S(1)}, bf16[208,128]{1,0:T(8,128)(2,1)S(1)}, u32[]{:S(2)}, u32[]{:S(2)}) collective-permute-start(bf16[208,128]{1,0:T(8,128)(2,1)S(1)} %get-tuple-element.74.a0), channel_id=1, source_target_pairs={{0,64},{4,68},{8,72},{12,76},{16,80},{20,84},{24,88},{28,92},{32,9... | collective-permute-start | bytes 159752 | tf_op jit(solution)/shard_map/ppermute | solution.py:698
  35.3 11.6 %collective-permute-start.7 = (bf16[208,128]{1,0:T(8,128)(2,1)S(1)}, bf16[208,128]{1,0:T(8,128)(2,1)S(1)}, u32[]{:S(2)}, u32[]{:S(2)}) collective-permute-start(bf16[208,128]{1,0:T(8,128)(2,1)S(1)} %get-tuple-element.74.a0), channel_id=1, source_target_pairs={{0,128},{4,132},{8,136},{12,140},{16,144},{20,148},{24,152},{28,15... | collective-permute-start | bytes 159752 | tf_op jit(solution)/shard_map/ppermute | solution.py:698
  38.1 8.7 %collective-permute-start.8 = (bf16[208,128]{1,0:T(8,128)(2,1)S(1)}, bf16[208,128]{1,0:T(8,128)(2,1)S(1)}, u32[]{:S(2)}, u32[]{:S(2)}) collective-permute-start(bf16[208,128]{1,0:T(8,128)(2,1)S(1)} %get-tuple-element.74.a0), channel_id=1, source_target_pairs={{0,192},{4,196},{8,200},{12,204},{16,208},{20,212},{24,216},{28,22... | collective-permute-start | bytes 159752 | tf_op jit(solution)/shard_map/ppermute | solution.py:698
  38.6 0.7 copy-start.15
  38.6 0.7 copy-start.14
  39.2 1.1 %copy-start.4 = (bf16[512,768]{1,0:T(8,128)(2,1)S(1)}, bf16[512,768]{1,0:T(8,128)(2,1)}, u32[]{:S(2)}) copy-start(bf16[512,768]{1,0:T(8,128)(2,1)} %q_ref.1) | copy-start | bytes 2359300
  40.4 6.4 %copy-start.8 = (f32[4,192,128]{2,1,0:T(8,128)S(1)}, f32[4,192,128]{2,1,0:T(8,128)}, u32[]{:S(2)}) copy-start(f32[4,192,128]{2,1,0:T(8,128)} %copy-done.7) | copy-start | bytes 1179652
  40.4 12.3 %copy-start.3 = (bf16[512,768]{1,0:T(8,128)(2,1)S(1)}, bf16[512,768]{1,0:T(8,128)(2,1)}, u32[]{:S(2)}) copy-start(bf16[512,768]{1,0:T(8,128)(2,1)} %gate_ref.1) | copy-start | bytes 2359300
  46.8 5.8 %copy-start.5 = (bf16[512,128]{1,0:T(8,128)(2,1)S(1)}, bf16[512,128]{1,0:T(8,128)(2,1)}, u32[]{:S(2)}) copy-start(bf16[512,128]{1,0:T(8,128)(2,1)} %into_ref.1) | copy-start | bytes 393220
  46.8 5.8 %copy-start.6 = (bf16[512,128]{1,0:T(8,128)(2,1)S(1)}, bf16[512,128]{1,0:T(8,128)(2,1)}, u32[]{:S(2)}) copy-start(bf16[512,128]{1,0:T(8,128)(2,1)} %read_ref.3) | copy-start | bytes 393220
  46.9 5.8 %copy-start.9 = (f32[12,512]{1,0:T(8,128)S(1)}, f32[12,512]{1,0:T(8,128)}, u32[]{:S(2)}) copy-start(f32[12,512]{1,0:T(8,128)} %steps_ref.1) | copy-start | bytes 73732
  46.9 5.8 %copy-start.10 = (f32[12,512]{1,0:T(8,128)S(1)}, f32[12,512]{1,0:T(8,128)}, u32[]{:S(2)}) copy-start(f32[12,512]{1,0:T(8,128)} %rates_ref.1) | copy-start | bytes 73732
  47.5 5.1 %copy-start.17 = (f32[768]{0:T(1024)S(1)}, f32[768]{0:T(1024)}, u32[]{:S(2)}) copy-start(f32[768]{0:T(1024)} %param.25) | copy-start | bytes 9220
  47.6 16.5 %collective-permute-start.12 = (bf16[192,128]{1,0:T(8,128)(2,1)S(1)}, bf16[192,128]{1,0:T(8,128)(2,1)S(1)}, u32[]{:S(2)}, u32[]{:S(2)}) collective-permute-start(bf16[192,128]{1,0:T(8,128)(2,1)S(1)} %get-tuple-element.83), channel_id=1, source_target_pairs={{0,4},{4,0},{8,12},{12,8},{16,20},{20,16},{24,28},{28,24},{32,36},... | collective-permute-start | bytes 147464 | tf_op jit(solution)/shard_map/ppermute | solution.py:693
  50.4 17.2 %collective-permute-start.13 = (bf16[192,128]{1,0:T(8,128)(2,1)S(1)}, bf16[192,128]{1,0:T(8,128)(2,1)S(1)}, u32[]{:S(2)}, u32[]{:S(2)}) collective-permute-start(bf16[192,128]{1,0:T(8,128)(2,1)S(1)} %get-tuple-element.84), channel_id=1, source_target_pairs={{0,8},{4,12},{8,0},{12,4},{16,24},{20,28},{24,16},{28,20},{32,40},... | collective-permute-start | bytes 147464 | tf_op jit(solution)/shard_map/ppermute | solution.py:693
  51.4 17.1 %collective-permute-start.14 = (bf16[192,128]{1,0:T(8,128)(2,1)S(1)}, bf16[192,128]{1,0:T(8,128)(2,1)S(1)}, u32[]{:S(2)}, u32[]{:S(2)}) collective-permute-start(bf16[192,128]{1,0:T(8,128)(2,1)S(1)} %get-tuple-element.85), channel_id=1, source_target_pairs={{0,12},{4,8},{8,4},{12,0},{16,28},{20,24},{24,20},{28,16},{32,44},... | collective-permute-start | bytes 147464 | tf_op jit(solution)/shard_map/ppermute | solution.py:693
  52.6 0.7 copy-start.16

commit v6 on v5

--- a/solution.py
+++ b/solution.py
@@ -479,13 +479,16 @@
             held[pl.ds(pl.multiple_of(part * QUARTER, 64), QUARTER), :] = ref[...]
 
     together = one((iota((128, 128), 0) >> 6) == (iota((128, 128), 1) >> 6), BF16)
-    for pair in range(PAIRS):
-        now = slice(pair * 128, (pair + 1) * 128)
-        carried = dot_t(read_ref[...], held[now, :])
-        gated = base_ref[:, now].astype(F32) + lift_ref[:, now].astype(F32) * carried
-        high, low = split(gated * gated, 2)
-        mean = (dot(high, together) + dot(low, together)) * (1.0 / HEAD_DIM)
-        out_ref[:, now] = (gated * lax.rsqrt(mean + 1e-05) * gain_ref[:, now]).astype(BF16)
+    pairs = [slice(pair * 128, (pair + 1) * 128) for pair in range(PAIRS)]
+    carried = [dot_t(read_ref[...], held[now, :]) for now in pairs]
+    gated = [
+        base_ref[:, now].astype(F32) + lift_ref[:, now].astype(F32) * state
+        for now, state in zip(pairs, carried)
+    ]
+    squares = [split(x * x, 2) for x in gated]
+    means = [(dot(high, together) + dot(low, together)) * (1.0 / HEAD_DIM) for high, low in squares]
+    for now, x, mean in zip(pairs, gated, means):
+        out_ref[:, now] = (x * lax.rsqrt(mean + 1e-05) * gain_ref[:, now]).astype(BF16)
 
 
 def shape(*dims, kind=BF16):

time: 75 us -> 74.4 us (level)
  no operation moved by 1% of the time
where the time goes in v6:
time: 74.4 us; the launch traced here: 74.1 us
  Pallas kernels  26.9 us (36%)
  starting transfers between devices  25.8 us (35%)
  waiting for transfers between devices  15.6 us (21%)
  local copies, waits for them, and re-layouts  4.37 us (6%)
  between operations  0.85 us (1%)
    ppermute x9, starting transfers between devices, cross(): return lax.ppermute(block, 'seq', [(i, i ^ mask) for i in range(count)])  12.9 us
    ppermute x6, starting transfers between devices, turn(): return lax.ppermute(block, 'seq', route)  12.9 us
    ppermute x9, waiting for transfers between devices, cross(): return lax.ppermute(block, 'seq', [(i, i ^ mask) for i in range(count)])  11.1 us
    pallas_call x1, Pallas kernels, call_local(): pl.pallas_call(local_kernel, out_shape=KEPT, in_specs=[VMEM] * 4 + [SMEM]...  6.41 us
    pallas_call x1, Pallas kernels, call_within(): pl.pallas_call(within_kernel, grid=(PAIRS,), out_shape=[shape(ROWS, WIDTH...  4.64 us
    ppermute x6, waiting for transfers between devices, turn(): return lax.ppermute(block, 'seq', route)  4.54 us
    unnamed x36, local copies, waits for them, and re-layouts  4.36 us
    pallas_call x1, Pallas kernels, call_near(): pl.pallas_call(functools.partial(remote_kernel, True), out_shape=[KEPT[2]...  3.86 us
  transfers between devices with their start and end apart: 15, of which 8 were waited for; matrix products, arithmetic and copies ran while one was open for 0% of the time, Pallas kernels for 27%

profile of v6, /device:TPU:16, one launch (start us, length us, event | category | flops | bytes accessed | tf_op | source)
XLA Modules:
  0.0 74.1 jit_solution(12603865560395716428)
XLA Ops:
  0.6 0.0 copy-start
  0.6 0.7 pad_add_fusion.place_ref
  1.3 3.3 %state.1 = (bf16[208,128]{1,0:T(8,128)(2,1)}, bf16[208,128]{1,0:T(8,128)(2,1)}, bf16[208,128]{1,0:T(8,128)(2,1)}, bf16[208,128]{1,0:T(8,128)(2,1)}) custom-call(bf16[512,768]{1,0:T(8,128)(2,1)} %v_ref.5, f32[12,512]{1,0:T(8,128)} %steps_ref.1, f32[12,512]{1,0:T(8,128)} %rates_ref.1, s32[1,512]{1,0:T(1,128)} %bitcast.5, bf16[512,128]{1,0:T(8,128)(2,1)} %into_ref.1, ...), custom_call_target="tpu_custom_call" | custom-call | flops 1 | bytes 1 | tf_op jit(solution)/shard_map/state/pallas_call | solution.py:520
  4.6 3.1 %collective-permute-start = (bf16[208,128]{1,0:T(8,128)(2,1)}, bf16[208,128]{1,0:T(8,128)(2,1)S(1)}, u32[]{:S(2)}, u32[]{:S(2)}) collective-permute-start(bf16[208,128]{1,0:T(8,128)(2,1)} %get-tuple-element.53), channel_id=1, source_target_pairs={{0,4},{4,0},{8,12},{12,8},{16,20},{20,16},{24,28},{28,24},{32,36},... | collective-permute-start | bytes 159752 | tf_op jit(solution)/shard_map/ppermute | solution.py:696
  7.7 1.9 %collective-permute-start.1 = (bf16[208,128]{1,0:T(8,128)(2,1)}, bf16[208,128]{1,0:T(8,128)(2,1)S(1)}, u32[]{:S(2)}, u32[]{:S(2)}) collective-permute-start(bf16[208,128]{1,0:T(8,128)(2,1)} %get-tuple-element.54), channel_id=1, source_target_pairs={{0,8},{4,12},{8,0},{12,4},{16,24},{20,28},{24,16},{28,20},{32,40},... | collective-permute-start | bytes 159752 | tf_op jit(solution)/shard_map/ppermute | solution.py:696
  9.6 0.1 collective-permute-start.2
  9.7 1.1 %copy-done.1 = bf16[512,768]{1,0:T(8,128)(2,1)S(1)} copy-done((bf16[512,768]{1,0:T(8,128)(2,1)S(1)}, bf16[512,768]{1,0:T(8,128)(2,1)}, u32[]{:S(2)}) %copy-start.1) | copy-done | bytes 786456
  10.8 1.1 %pack.1 = bf16[528,768]{1,0:T(8,128)(2,1)S(1)} custom-call(bf16[512,768]{1,0:T(8,128)(2,1)S(1)} %copy-done.1, bf16[512,768]{1,0:T(8,128)(2,1)S(1)} %copy-done, s32[1,512]{1,0:T(1,128)S(1)} %bitcast.6), custom_call_target="tpu_custom_call" | custom-call | flops 1 | bytes 1 | tf_op jit(solution)/shard_map/pack/pallas_call | solution.py:507
  11.9 0.0 collective-permute-done.a1
  12.0 0.5 collective-permute-done.1.a2
  12.4 3.9 %collective-permute-done.2.a3 = bf16[208,128]{1,0:T(8,128)(2,1)S(1)} collective-permute-done((bf16[208,128]{1,0:T(8,128)(2,1)}, bf16[208,128]{1,0:T(8,128)(2,1)S(1)}, u32[]{:S(2)}, u32[]{:S(2)}) %collective-permute-start.2) | collective-permute-done | bytes 53280 | tf_op jit(solution)/shard_map/ppermute | solution.py:696
  16.4 0.6 block.1
  17.0 0.0 copy-start.7
  17.0 0.7 copy-done.7
  17.7 3.3 %collective-permute-start.3 = (bf16[208,128]{1,0:T(8,128)(2,1)S(1)}, bf16[208,128]{1,0:T(8,128)(2,1)S(1)}, u32[]{:S(2)}, u32[]{:S(2)}) collective-permute-start(bf16[208,128]{1,0:T(8,128)(2,1)S(1)} %get-tuple-element.62.a0), channel_id=1, source_target_pairs={{0,16},{4,20},{8,24},{12,28},{16,32},{20,36},{24,40},{28,44},{32,4... | collective-permute-start | bytes 159752 | tf_op jit(solution)/shard_map/ppermute | solution.py:701
  21.0 4.5 %collective-permute-start.4 = (bf16[208,128]{1,0:T(8,128)(2,1)S(1)}, bf16[208,128]{1,0:T(8,128)(2,1)S(1)}, u32[]{:S(2)}, u32[]{:S(2)}) collective-permute-start(bf16[208,128]{1,0:T(8,128)(2,1)S(1)} %get-tuple-element.62.a0), channel_id=1, source_target_pairs={{0,32},{4,36},{8,40},{12,44},{16,48},{20,52},{24,56},{28,60},{32,0... | collective-permute-start | bytes 159752 | tf_op jit(solution)/shard_map/ppermute | solution.py:701
  25.5 2.7 %collective-permute-start.5 = (bf16[208,128]{1,0:T(8,128)(2,1)S(1)}, bf16[208,128]{1,0:T(8,128)(2,1)S(1)}, u32[]{:S(2)}, u32[]{:S(2)}) collective-permute-start(bf16[208,128]{1,0:T(8,128)(2,1)S(1)} %get-tuple-element.62.a0), channel_id=1, source_target_pairs={{0,48},{4,52},{8,56},{12,60},{16,0},{20,4},{24,8},{28,12},{32,16},... | collective-permute-start | bytes 159752 | tf_op jit(solution)/shard_map/ppermute | solution.py:701
  28.2 0.5 collective-permute-start.9
  28.7 0.9 %collective-permute-done.4.a2 = bf16[208,128]{1,0:T(8,128)(2,1)S(1)} collective-permute-done((bf16[208,128]{1,0:T(8,128)(2,1)S(1)}, bf16[208,128]{1,0:T(8,128)(2,1)S(1)}, u32[]{:S(2)}, u32[]{:S(2)}) %collective-permute-start.4) | collective-permute-done | bytes 53280 | tf_op jit(solution)/shard_map/ppermute | solution.py:701
  29.6 1.4 %collective-permute-done.5.a3 = bf16[208,128]{1,0:T(8,128)(2,1)S(1)} collective-permute-done((bf16[208,128]{1,0:T(8,128)(2,1)S(1)}, bf16[208,128]{1,0:T(8,128)(2,1)S(1)}, u32[]{:S(2)}, u32[]{:S(2)}) %collective-permute-start.5) | collective-permute-done | bytes 53280 | tf_op jit(solution)/shard_map/ppermute | solution.py:701
  31.0 1.0 %collective-permute-start.10 = (bf16[528,768]{1,0:T(8,128)(2,1)S(1)}, bf16[528,768]{1,0:T(8,128)(2,1)}, u32[]{:S(2)}, u32[]{:S(2)}) collective-permute-start(bf16[528,768]{1,0:T(8,128)(2,1)S(1)} %pack.1), channel_id=1, source_target_pairs={{0,8},{4,12},{8,0},{12,4},{16,24},{20,28},{24,16},{28,20},{32,40},... | collective-permute-start | bytes 2433032 | tf_op jit(solution)/shard_map/ppermute | solution.py:696
  32.0 1.3 %collective-permute-start.11 = (bf16[528,768]{1,0:T(8,128)(2,1)S(1)}, bf16[528,768]{1,0:T(8,128)(2,1)S(1)}, u32[]{:S(2)}, u32[]{:S(2)}) collective-permute-start(bf16[528,768]{1,0:T(8,128)(2,1)S(1)} %pack.1), channel_id=1, source_target_pairs={{0,12},{4,8},{8,4},{12,0},{16,28},{20,24},{24,20},{28,16},{32,44},... | collective-permute-start | bytes 2433032 | tf_op jit(solution)/shard_map/ppermute | solution.py:696
  33.3 0.6 line.1
  33.9 1.4 %collective-permute-start.6 = (bf16[208,128]{1,0:T(8,128)(2,1)S(1)}, bf16[208,128]{1,0:T(8,128)(2,1)S(1)}, u32[]{:S(2)}, u32[]{:S(2)}) collective-permute-start(bf16[208,128]{1,0:T(8,128)(2,1)S(1)} %get-tuple-element.74.a0), channel_id=1, source_target_pairs={{0,64},{4,68},{8,72},{12,76},{16,80},{20,84},{24,88},{28,92},{32,9... | collective-permute-start | bytes 159752 | tf_op jit(solution)/shard_map/ppermute | solution.py:701
  35.3 0.6 collective-permute-start.7
  35.9 2.2 %collective-permute-done.6.a1 = bf16[208,128]{1,0:T(8,128)(2,1)S(1)} collective-permute-done((bf16[208,128]{1,0:T(8,128)(2,1)S(1)}, bf16[208,128]{1,0:T(8,128)(2,1)S(1)}, u32[]{:S(2)}, u32[]{:S(2)}) %collective-permute-start.6) | collective-permute-done | bytes 53280 | tf_op jit(solution)/shard_map/ppermute | solution.py:701
  38.1 0.4 collective-permute-start.8
  38.6 0.7 copy-done.15
  39.2 0.0 copy-done.14
  39.3 1.1 %copy-done.4 = bf16[512,768]{1,0:T(8,128)(2,1)S(1)} copy-done((bf16[512,768]{1,0:T(8,128)(2,1)S(1)}, bf16[512,768]{1,0:T(8,128)(2,1)}, u32[]{:S(2)}) %copy-start.4) | copy-done | bytes 786456
  40.4 6.4 %local.1 = (bf16[768,256]{1,0:T(8,128)(2,1)S(1)}, bf16[384,256]{1,0:T(8,128)(2,1)S(1)}, f32[768,256]{1,0:T(8,128)S(1)}, f32[48,256]{1,0:T(8,128)S(1)}, bf16[768,...) custom-call(bf16[512,768]{1,0:T(8,128)(2,1)S(1)} %copy-done.4, bf16[512,768]{1,0:T(8,128)(2,1)S(1)} %copy-done.2, ...), custom_call_target="tpu_custom_call" | custom-call | flops 1 | bytes 1 | tf_op jit(solution)/shard_map/local/pallas_call | solution.py:593
  46.8 0.0 copy-start.5
  46.8 0.0 copy-start.6
  46.9 0.0 copy-start.9
  46.9 0.0 copy-start.10
  46.9 0.7 plane.1
  47.5 0.0 copy-start.17
  47.6 2.8 %collective-permute-start.12 = (bf16[192,128]{1,0:T(8,128)(2,1)S(1)}, bf16[192,128]{1,0:T(8,128)(2,1)S(1)}, u32[]{:S(2)}, u32[]{:S(2)}) collective-permute-start(bf16[192,128]{1,0:T(8,128)(2,1)S(1)} %get-tuple-element.83), channel_id=1, source_target_pairs={{0,4},{4,0},{8,12},{12,8},{16,20},{20,16},{24,28},{28,24},{32,36},... | collective-permute-start | bytes 147464 | tf_op jit(solution)/shard_map/ppermute | solution.py:696
  50.4 1.0 %collective-permute-start.13 = (bf16[192,128]{1,0:T(8,128)(2,1)S(1)}, bf16[192,128]{1,0:T(8,128)(2,1)S(1)}, u32[]{:S(2)}, u32[]{:S(2)}) collective-permute-start(bf16[192,128]{1,0:T(8,128)(2,1)S(1)} %get-tuple-element.84), channel_id=1, source_target_pairs={{0,8},{4,12},{8,0},{12,4},{16,24},{20,28},{24,16},{28,20},{32,40},... | collective-permute-start | bytes 147464 | tf_op jit(solution)/shard_map/ppermute | solution.py:696
  51.4 1.3 %collective-permute-start.14 = (bf16[192,128]{1,0:T(8,128)(2,1)S(1)}, bf16[192,128]{1,0:T(8,128)(2,1)S(1)}, u32[]{:S(2)}, u32[]{:S(2)}) collective-permute-start(bf16[192,128]{1,0:T(8,128)(2,1)S(1)} %get-tuple-element.85), channel_id=1, source_target_pairs={{0,12},{4,8},{8,4},{12,0},{16,28},{20,24},{24,20},{28,16},{32,44},... | collective-permute-start | bytes 147464 | tf_op jit(solution)/shard_map/ppermute | solution.py:696
  52.7 0.6 copy-done.16
  53.3 4.6 %within.1 = (bf16[512,768]{1,0:T(8,128)(2,1)S(1)}, bf16[512,768]{1,0:T(8,128)(2,1)S(1)}) custom-call(bf16[512,768]{1,0:T(8,128)(2,1)S(1)} %copy-done, bf16[512,768]{1,0:T(8,128)(2,1)S(1)} %copy-done.3, f32[12,512]{1,0:T(8,128)S(1)} %copy-done.9, f32[12,512]{1,0:T(8,128)S(1)} %copy-done.10, s32[1,512]{1,0:T(1,128)S(1)} %bitcast.8, ...), custom_call_target="tpu_custom_call" | custom-call | flops 1 | bytes 1 | tf_op jit(solution)/shard_map/within/pallas_call | solution.py:611
  58.0 3.9 %near.1 = (f32[768,256]{1,0:T(8,128)S(1)}, f32[48,256]{1,0:T(8,128)S(1)}) custom-call(bf16[768,256]{1,0:T(8,128)(2,1)S(1)} %get-tuple-element.89.qe_ref, bf16[384,256]{1,0:T(8,128)(2,1)S(1)} %get-tuple-element.90.plan_ref, f32[768,256]{1,0:T(8,128)S(1)} %get-tuple-element.91.oe_ref, f32[48,256]{1,0:T(8,128)S(1)} %get-tuple-element.92.stat_ref, ...), custom_call_target="tpu_custom_call" | custom-call | flops 1 | bytes 1 | tf_op jit(solution)/shard_map/near/pallas_call | solution.py:648
  61.8 2.2 %collective-permute-done.12.f1 = bf16[192,128]{1,0:T(8,128)(2,1)S(1)} collective-permute-done((bf16[192,128]{1,0:T(8,128)(2,1)S(1)}, bf16[192,128]{1,0:T(8,128)(2,1)S(1)}, u32[]{:S(2)}, u32[]{:S(2)}) %collective-permute-start.12) | collective-permute-done | bytes 49184 | tf_op jit(solution)/shard_map/ppermute | solution.py:696
  64.0 3.5 %collective-permute-done.13.f2 = bf16[192,128]{1,0:T(8,128)(2,1)S(1)} collective-permute-done((bf16[192,128]{1,0:T(8,128)(2,1)S(1)}, bf16[192,128]{1,0:T(8,128)(2,1)S(1)}, u32[]{:S(2)}, u32[]{:S(2)}) %collective-permute-start.13) | collective-permute-done | bytes 49184 | tf_op jit(solution)/shard_map/ppermute | solution.py:696
  67.6 0.9 %collective-permute-done.14.f3 = bf16[192,128]{1,0:T(8,128)(2,1)S(1)} collective-permute-done((bf16[192,128]{1,0:T(8,128)(2,1)S(1)}, bf16[192,128]{1,0:T(8,128)(2,1)S(1)}, u32[]{:S(2)}, u32[]{:S(2)}) %collective-permute-start.14) | collective-permute-done | bytes 49184 | tf_op jit(solution)/shard_map/ppermute | solution.py:696
  68.5 2.5 %finish.1 = bf16[512,768]{1,0:T(8,128)(2,1)} custom-call(s32[3]{0:T(128)S(1)} %copy-done.13, bf16[192,128]{1,0:T(8,128)(2,1)S(1)} %get-tuple-element.98.f0, bf16[192,128]{1,0:T(8,128)(2,1)S(1)} %collective-permute-done.12.f1, bf16[192,128]{1,0:T(8,128)(2,1)S(1)} %collective-permute-done.13.f2, bf16[192,128]{1,0:T(8,128)(2,1)S(1)} %collective-permute-done.14.f3, ...), custom_call_target="tpu_custom_call" | custom-call | flops 1 | bytes 1 | tf_op jit(solution)/shard_map/finish/pallas_call | solution.py:630
  71.0 3.1 %remote.1 = bf16[512,768]{1,0:T(8,128)(2,1)} custom-call(bf16[768,256]{1,0:T(8,128)(2,1)S(1)} %get-tuple-element.89.qe_ref, bf16[384,256]{1,0:T(8,128)(2,1)S(1)} %get-tuple-element.90.plan_ref, f32[768,256]{1,0:T(8,128)S(1)} %get-tuple-element.96.oe_ref, f32[48,256]{1,0:T(8,128)S(1)} %get-tuple-element.97.stat_ref, ...), custom_call_target="tpu_custom_call" | custom-call | flops 1 | bytes 1 | tf_op jit(solution)/shard_map/remote/pallas_call | solution.py:661
  (30 shorter events, 0.1 us)
Async XLA Ops:
  0.6 9.0 %copy-start = (bf16[512,768]{1,0:T(8,128)(2,1)S(1)}, bf16[512,768]{1,0:T(8,128)(2,1)}, u32[]{:S(2)}) copy-start(bf16[512,768]{1,0:T(8,128)(2,1)} %v_ref.5) | copy-start | bytes 2359300
  4.6 7.4 %collective-permute-start = (bf16[208,128]{1,0:T(8,128)(2,1)}, bf16[208,128]{1,0:T(8,128)(2,1)S(1)}, u32[]{:S(2)}, u32[]{:S(2)}) collective-permute-start(bf16[208,128]{1,0:T(8,128)(2,1)} %get-tuple-element.53), channel_id=1, source_target_pairs={{0,4},{4,0},{8,12},{12,8},{16,20},{20,16},{24,28},{28,24},{32,36},... | collective-permute-start | bytes 159752 | tf_op jit(solution)/shard_map/ppermute | solution.py:696
  7.7 2.0 %copy-start.12 = (s32[512]{0:T(512)S(1)}, s32[512]{0:T(512)}, u32[]{:S(2)}) copy-start(s32[512]{0:T(512)} %param.16) | copy-start | bytes 6148
  7.7 4.7 %collective-permute-start.1 = (bf16[208,128]{1,0:T(8,128)(2,1)}, bf16[208,128]{1,0:T(8,128)(2,1)S(1)}, u32[]{:S(2)}, u32[]{:S(2)}) collective-permute-start(bf16[208,128]{1,0:T(8,128)(2,1)} %get-tuple-element.54), channel_id=1, source_target_pairs={{0,8},{4,12},{8,0},{12,4},{16,24},{20,28},{24,16},{28,20},{32,40},... | collective-permute-start | bytes 159752 | tf_op jit(solution)/shard_map/ppermute | solution.py:696
  9.6 6.7 %collective-permute-start.2 = (bf16[208,128]{1,0:T(8,128)(2,1)}, bf16[208,128]{1,0:T(8,128)(2,1)S(1)}, u32[]{:S(2)}, u32[]{:S(2)}) collective-permute-start(bf16[208,128]{1,0:T(8,128)(2,1)} %get-tuple-element.55), channel_id=1, source_target_pairs={{0,12},{4,8},{8,4},{12,0},{16,28},{20,24},{24,20},{28,16},{32,44},... | collective-permute-start | bytes 159752 | tf_op jit(solution)/shard_map/ppermute | solution.py:696
  9.7 1.1 %copy-start.1 = (bf16[512,768]{1,0:T(8,128)(2,1)S(1)}, bf16[512,768]{1,0:T(8,128)(2,1)}, u32[]{:S(2)}) copy-start(bf16[512,768]{1,0:T(8,128)(2,1)} %k_ref.3) | copy-start | bytes 2359300
  10.8 5.6 %copy-start.11 = (bf16[208,128]{1,0:T(8,128)(2,1)S(1)}, bf16[208,128]{1,0:T(8,128)(2,1)}, u32[]{:S(2)}) copy-start(bf16[208,128]{1,0:T(8,128)(2,1)} %get-tuple-element.57.a0) | copy-start | bytes 159748
  10.8 5.6 %copy-start.13 = (s32[3]{0:T(128)S(1)}, s32[3]{0:T(128)}, u32[]{:S(2)}) copy-start(s32[3]{0:T(128)} %pad_add_fusion.place_ref) | copy-start | bytes 40
  10.8 27.7 %copy-start.2 = (bf16[512,768]{1,0:T(8,128)(2,1)S(1)}, bf16[512,768]{1,0:T(8,128)(2,1)}, u32[]{:S(2)}) copy-start(bf16[512,768]{1,0:T(8,128)(2,1)} %k_ref.3) | copy-start | bytes 2359300
  17.0 0.7 %copy-start.7 = (f32[4,192,128]{2,1,0:T(8,128)}, f32[4,192,128]{2,1,0:T(8,128)S(1)}, u32[]{:S(2)}) copy-start(f32[4,192,128]{2,1,0:T(8,128)S(1)} %get-tuple-element.80.block_before) | copy-start | bytes 1179652
  17.7 10.9 %collective-permute-start.3 = (bf16[208,128]{1,0:T(8,128)(2,1)S(1)}, bf16[208,128]{1,0:T(8,128)(2,1)S(1)}, u32[]{:S(2)}, u32[]{:S(2)}) collective-permute-start(bf16[208,128]{1,0:T(8,128)(2,1)S(1)} %get-tuple-element.62.a0), channel_id=1, source_target_pairs={{0,16},{4,20},{8,24},{12,28},{16,32},{20,36},{24,40},{28,44},{32,4... | collective-permute-start | bytes 159752 | tf_op jit(solution)/shard_map/ppermute | solution.py:701
  21.0 8.6 %collective-permute-start.4 = (bf16[208,128]{1,0:T(8,128)(2,1)S(1)}, bf16[208,128]{1,0:T(8,128)(2,1)S(1)}, u32[]{:S(2)}, u32[]{:S(2)}) collective-permute-start(bf16[208,128]{1,0:T(8,128)(2,1)S(1)} %get-tuple-element.62.a0), channel_id=1, source_target_pairs={{0,32},{4,36},{8,40},{12,44},{16,48},{20,52},{24,56},{28,60},{32,0... | collective-permute-start | bytes 159752 | tf_op jit(solution)/shard_map/ppermute | solution.py:701
  25.5 5.5 %collective-permute-start.5 = (bf16[208,128]{1,0:T(8,128)(2,1)S(1)}, bf16[208,128]{1,0:T(8,128)(2,1)S(1)}, u32[]{:S(2)}, u32[]{:S(2)}) collective-permute-start(bf16[208,128]{1,0:T(8,128)(2,1)S(1)} %get-tuple-element.62.a0), channel_id=1, source_target_pairs={{0,48},{4,52},{8,56},{12,60},{16,0},{20,4},{24,8},{28,12},{32,16},... | collective-permute-start | bytes 159752 | tf_op jit(solution)/shard_map/ppermute | solution.py:701
  28.2 23.2 %collective-permute-start.9 = (bf16[528,768]{1,0:T(8,128)(2,1)S(1)}, bf16[528,768]{1,0:T(8,128)(2,1)}, u32[]{:S(2)}, u32[]{:S(2)}) collective-permute-start(bf16[528,768]{1,0:T(8,128)(2,1)S(1)} %pack.1), channel_id=1, source_target_pairs={{0,4},{4,0},{8,12},{12,8},{16,20},{20,16},{24,28},{28,24},{32,36},... | collective-permute-start | bytes 2433032 | tf_op jit(solution)/shard_map/ppermute | solution.py:696
  31.0 27.0 %collective-permute-start.10 = (bf16[528,768]{1,0:T(8,128)(2,1)S(1)}, bf16[528,768]{1,0:T(8,128)(2,1)}, u32[]{:S(2)}, u32[]{:S(2)}) collective-permute-start(bf16[528,768]{1,0:T(8,128)(2,1)S(1)} %pack.1), channel_id=1, source_target_pairs={{0,8},{4,12},{8,0},{12,4},{16,24},{20,28},{24,16},{28,20},{32,40},... | collective-permute-start | bytes 2433032 | tf_op jit(solution)/shard_map/ppermute | solution.py:696
  32.0 39.0 %collective-permute-start.11 = (bf16[528,768]{1,0:T(8,128)(2,1)S(1)}, bf16[528,768]{1,0:T(8,128)(2,1)S(1)}, u32[]{:S(2)}, u32[]{:S(2)}) collective-permute-start(bf16[528,768]{1,0:T(8,128)(2,1)S(1)} %pack.1), channel_id=1, source_target_pairs={{0,12},{4,8},{8,4},{12,0},{16,28},{20,24},{24,20},{28,16},{32,44},... | collective-permute-start | bytes 2433032 | tf_op jit(solution)/shard_map/ppermute | solution.py:696
  33.9 4.2 %collective-permute-start.6 = (bf16[208,128]{1,0:T(8,128)(2,1)S(1)}, bf16[208,128]{1,0:T(8,128)(2,1)S(1)}, u32[]{:S(2)}, u32[]{:S(2)}) collective-permute-start(bf16[208,128]{1,0:T(8,128)(2,1)S(1)} %get-tuple-element.74.a0), channel_id=1, source_target_pairs={{0,64},{4,68},{8,72},{12,76},{16,80},{20,84},{24,88},{28,92},{32,9... | collective-permute-start | bytes 159752 | tf_op jit(solution)/shard_map/ppermute | solution.py:701
  35.3 11.6 %collective-permute-start.7 = (bf16[208,128]{1,0:T(8,128)(2,1)S(1)}, bf16[208,128]{1,0:T(8,128)(2,1)S(1)}, u32[]{:S(2)}, u32[]{:S(2)}) collective-permute-start(bf16[208,128]{1,0:T(8,128)(2,1)S(1)} %get-tuple-element.74.a0), channel_id=1, source_target_pairs={{0,128},{4,132},{8,136},{12,140},{16,144},{20,148},{24,152},{28,15... | collective-permute-start | bytes 159752 | tf_op jit(solution)/shard_map/ppermute | solution.py:701
  38.1 8.7 %collective-permute-start.8 = (bf16[208,128]{1,0:T(8,128)(2,1)S(1)}, bf16[208,128]{1,0:T(8,128)(2,1)S(1)}, u32[]{:S(2)}, u32[]{:S(2)}) collective-permute-start(bf16[208,128]{1,0:T(8,128)(2,1)S(1)} %get-tuple-element.74.a0), channel_id=1, source_target_pairs={{0,192},{4,196},{8,200},{12,204},{16,208},{20,212},{24,216},{28,22... | collective-permute-start | bytes 159752 | tf_op jit(solution)/shard_map/ppermute | solution.py:701
  38.6 0.7 copy-start.15
  38.6 0.7 copy-start.14
  39.2 1.1 %copy-start.4 = (bf16[512,768]{1,0:T(8,128)(2,1)S(1)}, bf16[512,768]{1,0:T(8,128)(2,1)}, u32[]{:S(2)}) copy-start(bf16[512,768]{1,0:T(8,128)(2,1)} %q_ref.1) | copy-start | bytes 2359300
  40.4 6.4 %copy-start.8 = (f32[4,192,128]{2,1,0:T(8,128)S(1)}, f32[4,192,128]{2,1,0:T(8,128)}, u32[]{:S(2)}) copy-start(f32[4,192,128]{2,1,0:T(8,128)} %copy-done.7) | copy-start | bytes 1179652
  40.4 12.3 %copy-start.3 = (bf16[512,768]{1,0:T(8,128)(2,1)S(1)}, bf16[512,768]{1,0:T(8,128)(2,1)}, u32[]{:S(2)}) copy-start(bf16[512,768]{1,0:T(8,128)(2,1)} %gate_ref.1) | copy-start | bytes 2359300
  46.8 5.8 %copy-start.5 = (bf16[512,128]{1,0:T(8,128)(2,1)S(1)}, bf16[512,128]{1,0:T(8,128)(2,1)}, u32[]{:S(2)}) copy-start(bf16[512,128]{1,0:T(8,128)(2,1)} %into_ref.1) | copy-start | bytes 393220
  46.8 5.8 %copy-start.6 = (bf16[512,128]{1,0:T(8,128)(2,1)S(1)}, bf16[512,128]{1,0:T(8,128)(2,1)}, u32[]{:S(2)}) copy-start(bf16[512,128]{1,0:T(8,128)(2,1)} %read_ref.3) | copy-start | bytes 393220
  46.9 5.8 %copy-start.9 = (f32[12,512]{1,0:T(8,128)S(1)}, f32[12,512]{1,0:T(8,128)}, u32[]{:S(2)}) copy-start(f32[12,512]{1,0:T(8,128)} %steps_ref.1) | copy-start | bytes 73732
  46.9 5.8 %copy-start.10 = (f32[12,512]{1,0:T(8,128)S(1)}, f32[12,512]{1,0:T(8,128)}, u32[]{:S(2)}) copy-start(f32[12,512]{1,0:T(8,128)} %rates_ref.1) | copy-start | bytes 73732
  47.5 5.1 %copy-start.17 = (f32[768]{0:T(1024)S(1)}, f32[768]{0:T(1024)}, u32[]{:S(2)}) copy-start(f32[768]{0:T(1024)} %param.25) | copy-start | bytes 9220
  47.6 16.5 %collective-permute-start.12 = (bf16[192,128]{1,0:T(8,128)(2,1)S(1)}, bf16[192,128]{1,0:T(8,128)(2,1)S(1)}, u32[]{:S(2)}, u32[]{:S(2)}) collective-permute-start(bf16[192,128]{1,0:T(8,128)(2,1)S(1)} %get-tuple-element.83), channel_id=1, source_target_pairs={{0,4},{4,0},{8,12},{12,8},{16,20},{20,16},{24,28},{28,24},{32,36},... | collective-permute-start | bytes 147464 | tf_op jit(solution)/shard_map/ppermute | solution.py:696
  50.4 17.2 %collective-permute-start.13 = (bf16[192,128]{1,0:T(8,128)(2,1)S(1)}, bf16[192,128]{1,0:T(8,128)(2,1)S(1)}, u32[]{:S(2)}, u32[]{:S(2)}) collective-permute-start(bf16[192,128]{1,0:T(8,128)(2,1)S(1)} %get-tuple-element.84), channel_id=1, source_target_pairs={{0,8},{4,12},{8,0},{12,4},{16,24},{20,28},{24,16},{28,20},{32,40},... | collective-permute-start | bytes 147464 | tf_op jit(solution)/shard_map/ppermute | solution.py:696
  51.4 17.1 %collective-permute-start.14 = (bf16[192,128]{1,0:T(8,128)(2,1)S(1)}, bf16[192,128]{1,0:T(8,128)(2,1)S(1)}, u32[]{:S(2)}, u32[]{:S(2)}) collective-permute-start(bf16[192,128]{1,0:T(8,128)(2,1)S(1)} %get-tuple-element.85), channel_id=1, source_target_pairs={{0,12},{4,8},{8,4},{12,0},{16,28},{20,24},{24,20},{28,16},{32,44},... | collective-permute-start | bytes 147464 | tf_op jit(solution)/shard_map/ppermute | solution.py:696
  52.6 0.7 copy-start.16

commit v7 on v6

--- a/solution.py
+++ b/solution.py
@@ -625,11 +625,11 @@
 
 def call_finish(*args):
     def rows(width):
-        return pl.BlockSpec((HALF, width), lambda at: (at, 0))
+        return pl.BlockSpec((ROWS, width), lambda at: (at, 0))
 
     return pl.pallas_call(
         finish_kernel,
-        grid=(ROWS // HALF,),
+        grid=(1,),
         out_shape=shape(ROWS, WIDTH),
         in_specs=[SMEM]
         + [whole(QUARTER, STATE)] * 4
@@ -639,7 +639,7 @@
         out_specs=rows(WIDTH),
         scratch_shapes=[pltpu.VMEM((WIDTH, STATE), BF16)],
         cost_estimate=FREE,
-        compiler_params=params(),
+        compiler_params=params(20),
         name="finish",
     )(*args)
 

time: 74.4 us -> 74.3 us (level)
  no operation moved by 1% of the time
where the time goes in v7:
time: 74.3 us; the launch traced here: 74.1 us
  Pallas kernels  26.8 us (36%)
  starting transfers between devices  25.8 us (35%)
  waiting for transfers between devices  15.6 us (21%)
  local copies, waits for them, and re-layouts  4.37 us (6%)
  between operations  0.85 us (1%)
    ppermute x9, starting transfers between devices, cross(): return lax.ppermute(block, 'seq', [(i, i ^ mask) for i in range(count)])  12.9 us
    ppermute x6, starting transfers between devices, turn(): return lax.ppermute(block, 'seq', route)  12.9 us
    ppermute x9, waiting for transfers between devices, cross(): return lax.ppermute(block, 'seq', [(i, i ^ mask) for i in range(count)])  11 us
    pallas_call x1, Pallas kernels, call_local(): pl.pallas_call(local_kernel, out_shape=KEPT, in_specs=[VMEM] * 4 + [SMEM]...  6.43 us
    pallas_call x1, Pallas kernels, call_within(): pl.pallas_call(within_kernel, grid=(PAIRS,), out_shape=[shape(ROWS, WIDTH...  4.64 us
    ppermute x6, waiting for transfers between devices, turn(): return lax.ppermute(block, 'seq', route)  4.54 us
    unnamed x36, local copies, waits for them, and re-layouts  4.36 us
    pallas_call x1, Pallas kernels, call_near(): pl.pallas_call(functools.partial(remote_kernel, True), out_shape=[KEPT[2]...  3.87 us
  transfers between devices with their start and end apart: 15, of which 8 were waited for; matrix products, arithmetic and copies ran while one was open for 0% of the time, Pallas kernels for 27%

profile of v7, /device:TPU:16, one launch (start us, length us, event | category | flops | bytes accessed | tf_op | source)
XLA Modules:
  0.0 74.1 jit_solution(2633176324645234513)
XLA Ops:
  0.6 0.0 copy-start
  0.6 0.7 pad_add_fusion.place_ref
  1.3 3.3 %state.1 = (bf16[208,128]{1,0:T(8,128)(2,1)}, bf16[208,128]{1,0:T(8,128)(2,1)}, bf16[208,128]{1,0:T(8,128)(2,1)}, bf16[208,128]{1,0:T(8,128)(2,1)}) custom-call(bf16[512,768]{1,0:T(8,128)(2,1)} %v_ref.5, f32[12,512]{1,0:T(8,128)} %steps_ref.1, f32[12,512]{1,0:T(8,128)} %rates_ref.1, s32[1,512]{1,0:T(1,128)} %bitcast.5, bf16[512,128]{1,0:T(8,128)(2,1)} %into_ref.1, ...), custom_call_target="tpu_custom_call" | custom-call | flops 1 | bytes 1 | tf_op jit(solution)/shard_map/state/pallas_call | solution.py:520
  4.6 3.1 %collective-permute-start = (bf16[208,128]{1,0:T(8,128)(2,1)}, bf16[208,128]{1,0:T(8,128)(2,1)S(1)}, u32[]{:S(2)}, u32[]{:S(2)}) collective-permute-start(bf16[208,128]{1,0:T(8,128)(2,1)} %get-tuple-element.53), channel_id=1, source_target_pairs={{0,4},{4,0},{8,12},{12,8},{16,20},{20,16},{24,28},{28,24},{32,36},... | collective-permute-start | bytes 159752 | tf_op jit(solution)/shard_map/ppermute | solution.py:696
  7.7 1.9 %collective-permute-start.1 = (bf16[208,128]{1,0:T(8,128)(2,1)}, bf16[208,128]{1,0:T(8,128)(2,1)S(1)}, u32[]{:S(2)}, u32[]{:S(2)}) collective-permute-start(bf16[208,128]{1,0:T(8,128)(2,1)} %get-tuple-element.54), channel_id=1, source_target_pairs={{0,8},{4,12},{8,0},{12,4},{16,24},{20,28},{24,16},{28,20},{32,40},... | collective-permute-start | bytes 159752 | tf_op jit(solution)/shard_map/ppermute | solution.py:696
  9.6 0.1 collective-permute-start.2
  9.7 1.1 %copy-done.1 = bf16[512,768]{1,0:T(8,128)(2,1)S(1)} copy-done((bf16[512,768]{1,0:T(8,128)(2,1)S(1)}, bf16[512,768]{1,0:T(8,128)(2,1)}, u32[]{:S(2)}) %copy-start.1) | copy-done | bytes 786456
  10.8 1.1 %pack.1 = bf16[528,768]{1,0:T(8,128)(2,1)S(1)} custom-call(bf16[512,768]{1,0:T(8,128)(2,1)S(1)} %copy-done.1, bf16[512,768]{1,0:T(8,128)(2,1)S(1)} %copy-done, s32[1,512]{1,0:T(1,128)S(1)} %bitcast.6), custom_call_target="tpu_custom_call" | custom-call | flops 1 | bytes 1 | tf_op jit(solution)/shard_map/pack/pallas_call | solution.py:507
  11.9 0.0 collective-permute-done.a1
  12.0 0.5 collective-permute-done.1.a2
  12.4 3.9 %collective-permute-done.2.a3 = bf16[208,128]{1,0:T(8,128)(2,1)S(1)} collective-permute-done((bf16[208,128]{1,0:T(8,128)(2,1)}, bf16[208,128]{1,0:T(8,128)(2,1)S(1)}, u32[]{:S(2)}, u32[]{:S(2)}) %collective-permute-start.2) | collective-permute-done | bytes 53280 | tf_op jit(solution)/shard_map/ppermute | solution.py:696
  16.4 0.6 block.1
  17.0 0.0 copy-start.7
  17.0 0.7 copy-done.7
  17.7 3.3 %collective-permute-start.3 = (bf16[208,128]{1,0:T(8,128)(2,1)S(1)}, bf16[208,128]{1,0:T(8,128)(2,1)S(1)}, u32[]{:S(2)}, u32[]{:S(2)}) collective-permute-start(bf16[208,128]{1,0:T(8,128)(2,1)S(1)} %get-tuple-element.62.a0), channel_id=1, source_target_pairs={{0,16},{4,20},{8,24},{12,28},{16,32},{20,36},{24,40},{28,44},{32,4... | collective-permute-start | bytes 159752 | tf_op jit(solution)/shard_map/ppermute | solution.py:701
  21.0 4.5 %collective-permute-start.4 = (bf16[208,128]{1,0:T(8,128)(2,1)S(1)}, bf16[208,128]{1,0:T(8,128)(2,1)S(1)}, u32[]{:S(2)}, u32[]{:S(2)}) collective-permute-start(bf16[208,128]{1,0:T(8,128)(2,1)S(1)} %get-tuple-element.62.a0), channel_id=1, source_target_pairs={{0,32},{4,36},{8,40},{12,44},{16,48},{20,52},{24,56},{28,60},{32,0... | collective-permute-start | bytes 159752 | tf_op jit(solution)/shard_map/ppermute | solution.py:701
  25.5 2.7 %collective-permute-start.5 = (bf16[208,128]{1,0:T(8,128)(2,1)S(1)}, bf16[208,128]{1,0:T(8,128)(2,1)S(1)}, u32[]{:S(2)}, u32[]{:S(2)}) collective-permute-start(bf16[208,128]{1,0:T(8,128)(2,1)S(1)} %get-tuple-element.62.a0), channel_id=1, source_target_pairs={{0,48},{4,52},{8,56},{12,60},{16,0},{20,4},{24,8},{28,12},{32,16},... | collective-permute-start | bytes 159752 | tf_op jit(solution)/shard_map/ppermute | solution.py:701
  28.2 0.5 collective-permute-start.9
  28.7 0.9 %collective-permute-done.4.a2 = bf16[208,128]{1,0:T(8,128)(2,1)S(1)} collective-permute-done((bf16[208,128]{1,0:T(8,128)(2,1)S(1)}, bf16[208,128]{1,0:T(8,128)(2,1)S(1)}, u32[]{:S(2)}, u32[]{:S(2)}) %collective-permute-start.4) | collective-permute-done | bytes 53280 | tf_op jit(solution)/shard_map/ppermute | solution.py:701
  29.6 1.4 %collective-permute-done.5.a3 = bf16[208,128]{1,0:T(8,128)(2,1)S(1)} collective-permute-done((bf16[208,128]{1,0:T(8,128)(2,1)S(1)}, bf16[208,128]{1,0:T(8,128)(2,1)S(1)}, u32[]{:S(2)}, u32[]{:S(2)}) %collective-permute-start.5) | collective-permute-done | bytes 53280 | tf_op jit(solution)/shard_map/ppermute | solution.py:701
  31.0 1.0 %collective-permute-start.10 = (bf16[528,768]{1,0:T(8,128)(2,1)S(1)}, bf16[528,768]{1,0:T(8,128)(2,1)}, u32[]{:S(2)}, u32[]{:S(2)}) collective-permute-start(bf16[528,768]{1,0:T(8,128)(2,1)S(1)} %pack.1), channel_id=1, source_target_pairs={{0,8},{4,12},{8,0},{12,4},{16,24},{20,28},{24,16},{28,20},{32,40},... | collective-permute-start | bytes 2433032 | tf_op jit(solution)/shard_map/ppermute | solution.py:696
  32.0 1.3 %collective-permute-start.11 = (bf16[528,768]{1,0:T(8,128)(2,1)S(1)}, bf16[528,768]{1,0:T(8,128)(2,1)S(1)}, u32[]{:S(2)}, u32[]{:S(2)}) collective-permute-start(bf16[528,768]{1,0:T(8,128)(2,1)S(1)} %pack.1), channel_id=1, source_target_pairs={{0,12},{4,8},{8,4},{12,0},{16,28},{20,24},{24,20},{28,16},{32,44},... | collective-permute-start | bytes 2433032 | tf_op jit(solution)/shard_map/ppermute | solution.py:696
  33.3 0.6 line.1
  33.9 1.4 %collective-permute-start.6 = (bf16[208,128]{1,0:T(8,128)(2,1)S(1)}, bf16[208,128]{1,0:T(8,128)(2,1)S(1)}, u32[]{:S(2)}, u32[]{:S(2)}) collective-permute-start(bf16[208,128]{1,0:T(8,128)(2,1)S(1)} %get-tuple-element.74.a0), channel_id=1, source_target_pairs={{0,64},{4,68},{8,72},{12,76},{16,80},{20,84},{24,88},{28,92},{32,9... | collective-permute-start | bytes 159752 | tf_op jit(solution)/shard_map/ppermute | solution.py:701
  35.3 0.6 collective-permute-start.7
  35.9 2.2 %collective-permute-done.6.a1 = bf16[208,128]{1,0:T(8,128)(2,1)S(1)} collective-permute-done((bf16[208,128]{1,0:T(8,128)(2,1)S(1)}, bf16[208,128]{1,0:T(8,128)(2,1)S(1)}, u32[]{:S(2)}, u32[]{:S(2)}) %collective-permute-start.6) | collective-permute-done | bytes 53280 | tf_op jit(solution)/shard_map/ppermute | solution.py:701
  38.1 0.4 collective-permute-start.8
  38.6 0.7 copy-done.15
  39.2 0.0 copy-done.14
  39.3 1.1 %copy-done.4 = bf16[512,768]{1,0:T(8,128)(2,1)S(1)} copy-done((bf16[512,768]{1,0:T(8,128)(2,1)S(1)}, bf16[512,768]{1,0:T(8,128)(2,1)}, u32[]{:S(2)}) %copy-start.4) | copy-done | bytes 786456
  40.4 6.4 %local.1 = (bf16[768,256]{1,0:T(8,128)(2,1)S(1)}, bf16[384,256]{1,0:T(8,128)(2,1)S(1)}, f32[768,256]{1,0:T(8,128)S(1)}, f32[48,256]{1,0:T(8,128)S(1)}, bf16[768,...) custom-call(bf16[512,768]{1,0:T(8,128)(2,1)S(1)} %copy-done.4, bf16[512,768]{1,0:T(8,128)(2,1)S(1)} %copy-done.2, ...), custom_call_target="tpu_custom_call" | custom-call | flops 1 | bytes 1 | tf_op jit(solution)/shard_map/local/pallas_call | solution.py:593
  46.9 0.0 copy-start.5
  46.9 0.0 copy-start.6
  46.9 0.0 copy-start.9
  46.9 0.0 copy-start.10
  46.9 0.7 plane.1
  47.6 0.0 copy-start.17
  47.6 2.8 %collective-permute-start.12 = (bf16[192,128]{1,0:T(8,128)(2,1)S(1)}, bf16[192,128]{1,0:T(8,128)(2,1)S(1)}, u32[]{:S(2)}, u32[]{:S(2)}) collective-permute-start(bf16[192,128]{1,0:T(8,128)(2,1)S(1)} %get-tuple-element.83), channel_id=1, source_target_pairs={{0,4},{4,0},{8,12},{12,8},{16,20},{20,16},{24,28},{28,24},{32,36},... | collective-permute-start | bytes 147464 | tf_op jit(solution)/shard_map/ppermute | solution.py:696
  50.4 1.0 %collective-permute-start.13 = (bf16[192,128]{1,0:T(8,128)(2,1)S(1)}, bf16[192,128]{1,0:T(8,128)(2,1)S(1)}, u32[]{:S(2)}, u32[]{:S(2)}) collective-permute-start(bf16[192,128]{1,0:T(8,128)(2,1)S(1)} %get-tuple-element.84), channel_id=1, source_target_pairs={{0,8},{4,12},{8,0},{12,4},{16,24},{20,28},{24,16},{28,20},{32,40},... | collective-permute-start | bytes 147464 | tf_op jit(solution)/shard_map/ppermute | solution.py:696
  51.4 1.3 %collective-permute-start.14 = (bf16[192,128]{1,0:T(8,128)(2,1)S(1)}, bf16[192,128]{1,0:T(8,128)(2,1)S(1)}, u32[]{:S(2)}, u32[]{:S(2)}) collective-permute-start(bf16[192,128]{1,0:T(8,128)(2,1)S(1)} %get-tuple-element.85), channel_id=1, source_target_pairs={{0,12},{4,8},{8,4},{12,0},{16,28},{20,24},{24,20},{28,16},{32,44},... | collective-permute-start | bytes 147464 | tf_op jit(solution)/shard_map/ppermute | solution.py:696
  52.7 0.6 copy-done.16
  53.3 4.6 %within.1 = (bf16[512,768]{1,0:T(8,128)(2,1)S(1)}, bf16[512,768]{1,0:T(8,128)(2,1)S(1)}) custom-call(bf16[512,768]{1,0:T(8,128)(2,1)S(1)} %copy-done, bf16[512,768]{1,0:T(8,128)(2,1)S(1)} %copy-done.3, f32[12,512]{1,0:T(8,128)S(1)} %copy-done.9, f32[12,512]{1,0:T(8,128)S(1)} %copy-done.10, s32[1,512]{1,0:T(1,128)S(1)} %bitcast.8, ...), custom_call_target="tpu_custom_call" | custom-call | flops 1 | bytes 1 | tf_op jit(solution)/shard_map/within/pallas_call | solution.py:611
  58.0 3.9 %near.1 = (f32[768,256]{1,0:T(8,128)S(1)}, f32[48,256]{1,0:T(8,128)S(1)}) custom-call(bf16[768,256]{1,0:T(8,128)(2,1)S(1)} %get-tuple-element.89.qe_ref, bf16[384,256]{1,0:T(8,128)(2,1)S(1)} %get-tuple-element.90.plan_ref, f32[768,256]{1,0:T(8,128)S(1)} %get-tuple-element.91.oe_ref, f32[48,256]{1,0:T(8,128)S(1)} %get-tuple-element.92.stat_ref, ...), custom_call_target="tpu_custom_call" | custom-call | flops 1 | bytes 1 | tf_op jit(solution)/shard_map/near/pallas_call | solution.py:648
  61.9 2.2 %collective-permute-done.12.f1 = bf16[192,128]{1,0:T(8,128)(2,1)S(1)} collective-permute-done((bf16[192,128]{1,0:T(8,128)(2,1)S(1)}, bf16[192,128]{1,0:T(8,128)(2,1)S(1)}, u32[]{:S(2)}, u32[]{:S(2)}) %collective-permute-start.12) | collective-permute-done | bytes 49184 | tf_op jit(solution)/shard_map/ppermute | solution.py:696
  64.0 3.5 %collective-permute-done.13.f2 = bf16[192,128]{1,0:T(8,128)(2,1)S(1)} collective-permute-done((bf16[192,128]{1,0:T(8,128)(2,1)S(1)}, bf16[192,128]{1,0:T(8,128)(2,1)S(1)}, u32[]{:S(2)}, u32[]{:S(2)}) %collective-permute-start.13) | collective-permute-done | bytes 49184 | tf_op jit(solution)/shard_map/ppermute | solution.py:696
  67.6 0.9 %collective-permute-done.14.f3 = bf16[192,128]{1,0:T(8,128)(2,1)S(1)} collective-permute-done((bf16[192,128]{1,0:T(8,128)(2,1)S(1)}, bf16[192,128]{1,0:T(8,128)(2,1)S(1)}, u32[]{:S(2)}, u32[]{:S(2)}) %collective-permute-start.14) | collective-permute-done | bytes 49184 | tf_op jit(solution)/shard_map/ppermute | solution.py:696
  68.5 2.5 %finish.1 = bf16[512,768]{1,0:T(8,128)(2,1)} custom-call(s32[3]{0:T(128)S(1)} %copy-done.13, bf16[192,128]{1,0:T(8,128)(2,1)S(1)} %get-tuple-element.98.f0, bf16[192,128]{1,0:T(8,128)(2,1)S(1)} %collective-permute-done.12.f1, bf16[192,128]{1,0:T(8,128)(2,1)S(1)} %collective-permute-done.13.f2, bf16[192,128]{1,0:T(8,128)(2,1)S(1)} %collective-permute-done.14.f3, ...), custom_call_target="tpu_custom_call" | custom-call | flops 1 | bytes 1 | tf_op jit(solution)/shard_map/finish/pallas_call | solution.py:630
  70.9 3.1 %remote.1 = bf16[512,768]{1,0:T(8,128)(2,1)} custom-call(bf16[768,256]{1,0:T(8,128)(2,1)S(1)} %get-tuple-element.89.qe_ref, bf16[384,256]{1,0:T(8,128)(2,1)S(1)} %get-tuple-element.90.plan_ref, f32[768,256]{1,0:T(8,128)S(1)} %get-tuple-element.96.oe_ref, f32[48,256]{1,0:T(8,128)S(1)} %get-tuple-element.97.stat_ref, ...), custom_call_target="tpu_custom_call" | custom-call | flops 1 | bytes 1 | tf_op jit(solution)/shard_map/remote/pallas_call | solution.py:661
  (30 shorter events, 0.1 us)
Async XLA Ops:
  0.6 9.0 %copy-start = (bf16[512,768]{1,0:T(8,128)(2,1)S(1)}, bf16[512,768]{1,0:T(8,128)(2,1)}, u32[]{:S(2)}) copy-start(bf16[512,768]{1,0:T(8,128)(2,1)} %v_ref.5) | copy-start | bytes 2359300
  4.6 7.4 %collective-permute-start = (bf16[208,128]{1,0:T(8,128)(2,1)}, bf16[208,128]{1,0:T(8,128)(2,1)S(1)}, u32[]{:S(2)}, u32[]{:S(2)}) collective-permute-start(bf16[208,128]{1,0:T(8,128)(2,1)} %get-tuple-element.53), channel_id=1, source_target_pairs={{0,4},{4,0},{8,12},{12,8},{16,20},{20,16},{24,28},{28,24},{32,36},... | collective-permute-start | bytes 159752 | tf_op jit(solution)/shard_map/ppermute | solution.py:696
  7.7 2.0 %copy-start.12 = (s32[512]{0:T(512)S(1)}, s32[512]{0:T(512)}, u32[]{:S(2)}) copy-start(s32[512]{0:T(512)} %param.16) | copy-start | bytes 6148
  7.7 4.7 %collective-permute-start.1 = (bf16[208,128]{1,0:T(8,128)(2,1)}, bf16[208,128]{1,0:T(8,128)(2,1)S(1)}, u32[]{:S(2)}, u32[]{:S(2)}) collective-permute-start(bf16[208,128]{1,0:T(8,128)(2,1)} %get-tuple-element.54), channel_id=1, source_target_pairs={{0,8},{4,12},{8,0},{12,4},{16,24},{20,28},{24,16},{28,20},{32,40},... | collective-permute-start | bytes 159752 | tf_op jit(solution)/shard_map/ppermute | solution.py:696
  9.6 6.7 %collective-permute-start.2 = (bf16[208,128]{1,0:T(8,128)(2,1)}, bf16[208,128]{1,0:T(8,128)(2,1)S(1)}, u32[]{:S(2)}, u32[]{:S(2)}) collective-permute-start(bf16[208,128]{1,0:T(8,128)(2,1)} %get-tuple-element.55), channel_id=1, source_target_pairs={{0,12},{4,8},{8,4},{12,0},{16,28},{20,24},{24,20},{28,16},{32,44},... | collective-permute-start | bytes 159752 | tf_op jit(solution)/shard_map/ppermute | solution.py:696
  9.7 1.1 %copy-start.1 = (bf16[512,768]{1,0:T(8,128)(2,1)S(1)}, bf16[512,768]{1,0:T(8,128)(2,1)}, u32[]{:S(2)}) copy-start(bf16[512,768]{1,0:T(8,128)(2,1)} %k_ref.3) | copy-start | bytes 2359300
  10.8 5.6 %copy-start.11 = (bf16[208,128]{1,0:T(8,128)(2,1)S(1)}, bf16[208,128]{1,0:T(8,128)(2,1)}, u32[]{:S(2)}) copy-start(bf16[208,128]{1,0:T(8,128)(2,1)} %get-tuple-element.57.a0) | copy-start | bytes 159748
  10.8 5.6 %copy-start.13 = (s32[3]{0:T(128)S(1)}, s32[3]{0:T(128)}, u32[]{:S(2)}) copy-start(s32[3]{0:T(128)} %pad_add_fusion.place_ref) | copy-start | bytes 40
  10.8 27.7 %copy-start.2 = (bf16[512,768]{1,0:T(8,128)(2,1)S(1)}, bf16[512,768]{1,0:T(8,128)(2,1)}, u32[]{:S(2)}) copy-start(bf16[512,768]{1,0:T(8,128)(2,1)} %k_ref.3) | copy-start | bytes 2359300
  17.0 0.7 %copy-start.7 = (f32[4,192,128]{2,1,0:T(8,128)}, f32[4,192,128]{2,1,0:T(8,128)S(1)}, u32[]{:S(2)}) copy-start(f32[4,192,128]{2,1,0:T(8,128)S(1)} %get-tuple-element.80.block_before) | copy-start | bytes 1179652
  17.7 10.9 %collective-permute-start.3 = (bf16[208,128]{1,0:T(8,128)(2,1)S(1)}, bf16[208,128]{1,0:T(8,128)(2,1)S(1)}, u32[]{:S(2)}, u32[]{:S(2)}) collective-permute-start(bf16[208,128]{1,0:T(8,128)(2,1)S(1)} %get-tuple-element.62.a0), channel_id=1, source_target_pairs={{0,16},{4,20},{8,24},{12,28},{16,32},{20,36},{24,40},{28,44},{32,4... | collective-permute-start | bytes 159752 | tf_op jit(solution)/shard_map/ppermute | solution.py:701
  21.0 8.6 %collective-permute-start.4 = (bf16[208,128]{1,0:T(8,128)(2,1)S(1)}, bf16[208,128]{1,0:T(8,128)(2,1)S(1)}, u32[]{:S(2)}, u32[]{:S(2)}) collective-permute-start(bf16[208,128]{1,0:T(8,128)(2,1)S(1)} %get-tuple-element.62.a0), channel_id=1, source_target_pairs={{0,32},{4,36},{8,40},{12,44},{16,48},{20,52},{24,56},{28,60},{32,0... | collective-permute-start | bytes 159752 | tf_op jit(solution)/shard_map/ppermute | solution.py:701
  25.5 5.5 %collective-permute-start.5 = (bf16[208,128]{1,0:T(8,128)(2,1)S(1)}, bf16[208,128]{1,0:T(8,128)(2,1)S(1)}, u32[]{:S(2)}, u32[]{:S(2)}) collective-permute-start(bf16[208,128]{1,0:T(8,128)(2,1)S(1)} %get-tuple-element.62.a0), channel_id=1, source_target_pairs={{0,48},{4,52},{8,56},{12,60},{16,0},{20,4},{24,8},{28,12},{32,16},... | collective-permute-start | bytes 159752 | tf_op jit(solution)/shard_map/ppermute | solution.py:701
  28.2 23.2 %collective-permute-start.9 = (bf16[528,768]{1,0:T(8,128)(2,1)S(1)}, bf16[528,768]{1,0:T(8,128)(2,1)}, u32[]{:S(2)}, u32[]{:S(2)}) collective-permute-start(bf16[528,768]{1,0:T(8,128)(2,1)S(1)} %pack.1), channel_id=1, source_target_pairs={{0,4},{4,0},{8,12},{12,8},{16,20},{20,16},{24,28},{28,24},{32,36},... | collective-permute-start | bytes 2433032 | tf_op jit(solution)/shard_map/ppermute | solution.py:696
  31.0 27.0 %collective-permute-start.10 = (bf16[528,768]{1,0:T(8,128)(2,1)S(1)}, bf16[528,768]{1,0:T(8,128)(2,1)}, u32[]{:S(2)}, u32[]{:S(2)}) collective-permute-start(bf16[528,768]{1,0:T(8,128)(2,1)S(1)} %pack.1), channel_id=1, source_target_pairs={{0,8},{4,12},{8,0},{12,4},{16,24},{20,28},{24,16},{28,20},{32,40},... | collective-permute-start | bytes 2433032 | tf_op jit(solution)/shard_map/ppermute | solution.py:696
  32.0 38.9 %collective-permute-start.11 = (bf16[528,768]{1,0:T(8,128)(2,1)S(1)}, bf16[528,768]{1,0:T(8,128)(2,1)S(1)}, u32[]{:S(2)}, u32[]{:S(2)}) collective-permute-start(bf16[528,768]{1,0:T(8,128)(2,1)S(1)} %pack.1), channel_id=1, source_target_pairs={{0,12},{4,8},{8,4},{12,0},{16,28},{20,24},{24,20},{28,16},{32,44},... | collective-permute-start | bytes 2433032 | tf_op jit(solution)/shard_map/ppermute | solution.py:696
  33.9 4.2 %collective-permute-start.6 = (bf16[208,128]{1,0:T(8,128)(2,1)S(1)}, bf16[208,128]{1,0:T(8,128)(2,1)S(1)}, u32[]{:S(2)}, u32[]{:S(2)}) collective-permute-start(bf16[208,128]{1,0:T(8,128)(2,1)S(1)} %get-tuple-element.74.a0), channel_id=1, source_target_pairs={{0,64},{4,68},{8,72},{12,76},{16,80},{20,84},{24,88},{28,92},{32,9... | collective-permute-start | bytes 159752 | tf_op jit(solution)/shard_map/ppermute | solution.py:701
  35.3 11.6 %collective-permute-start.7 = (bf16[208,128]{1,0:T(8,128)(2,1)S(1)}, bf16[208,128]{1,0:T(8,128)(2,1)S(1)}, u32[]{:S(2)}, u32[]{:S(2)}) collective-permute-start(bf16[208,128]{1,0:T(8,128)(2,1)S(1)} %get-tuple-element.74.a0), channel_id=1, source_target_pairs={{0,128},{4,132},{8,136},{12,140},{16,144},{20,148},{24,152},{28,15... | collective-permute-start | bytes 159752 | tf_op jit(solution)/shard_map/ppermute | solution.py:701
  38.1 8.7 %collective-permute-start.8 = (bf16[208,128]{1,0:T(8,128)(2,1)S(1)}, bf16[208,128]{1,0:T(8,128)(2,1)S(1)}, u32[]{:S(2)}, u32[]{:S(2)}) collective-permute-start(bf16[208,128]{1,0:T(8,128)(2,1)S(1)} %get-tuple-element.74.a0), channel_id=1, source_target_pairs={{0,192},{4,196},{8,200},{12,204},{16,208},{20,212},{24,216},{28,22... | collective-permute-start | bytes 159752 | tf_op jit(solution)/shard_map/ppermute | solution.py:701
  38.6 0.7 copy-start.15
  38.6 0.7 copy-start.14
  39.2 1.1 %copy-start.4 = (bf16[512,768]{1,0:T(8,128)(2,1)S(1)}, bf16[512,768]{1,0:T(8,128)(2,1)}, u32[]{:S(2)}) copy-start(bf16[512,768]{1,0:T(8,128)(2,1)} %q_ref.1) | copy-start | bytes 2359300
  40.4 6.5 %copy-start.8 = (f32[4,192,128]{2,1,0:T(8,128)S(1)}, f32[4,192,128]{2,1,0:T(8,128)}, u32[]{:S(2)}) copy-start(f32[4,192,128]{2,1,0:T(8,128)} %copy-done.7) | copy-start | bytes 1179652
  40.4 12.3 %copy-start.3 = (bf16[512,768]{1,0:T(8,128)(2,1)S(1)}, bf16[512,768]{1,0:T(8,128)(2,1)}, u32[]{:S(2)}) copy-start(bf16[512,768]{1,0:T(8,128)(2,1)} %gate_ref.1) | copy-start | bytes 2359300
  46.9 5.8 %copy-start.5 = (bf16[512,128]{1,0:T(8,128)(2,1)S(1)}, bf16[512,128]{1,0:T(8,128)(2,1)}, u32[]{:S(2)}) copy-start(bf16[512,128]{1,0:T(8,128)(2,1)} %into_ref.1) | copy-start | bytes 393220
  46.9 5.8 %copy-start.6 = (bf16[512,128]{1,0:T(8,128)(2,1)S(1)}, bf16[512,128]{1,0:T(8,128)(2,1)}, u32[]{:S(2)}) copy-start(bf16[512,128]{1,0:T(8,128)(2,1)} %read_ref.3) | copy-start | bytes 393220
  46.9 5.8 %copy-start.9 = (f32[12,512]{1,0:T(8,128)S(1)}, f32[12,512]{1,0:T(8,128)}, u32[]{:S(2)}) copy-start(f32[12,512]{1,0:T(8,128)} %steps_ref.1) | copy-start | bytes 73732
  46.9 5.8 %copy-start.10 = (f32[12,512]{1,0:T(8,128)S(1)}, f32[12,512]{1,0:T(8,128)}, u32[]{:S(2)}) copy-start(f32[12,512]{1,0:T(8,128)} %rates_ref.1) | copy-start | bytes 73732
  47.6 5.1 %copy-start.17 = (f32[768]{0:T(1024)S(1)}, f32[768]{0:T(1024)}, u32[]{:S(2)}) copy-start(f32[768]{0:T(1024)} %param.25) | copy-start | bytes 9220
  47.6 16.5 %collective-permute-start.12 = (bf16[192,128]{1,0:T(8,128)(2,1)S(1)}, bf16[192,128]{1,0:T(8,128)(2,1)S(1)}, u32[]{:S(2)}, u32[]{:S(2)}) collective-permute-start(bf16[192,128]{1,0:T(8,128)(2,1)S(1)} %get-tuple-element.83), channel_id=1, source_target_pairs={{0,4},{4,0},{8,12},{12,8},{16,20},{20,16},{24,28},{28,24},{32,36},... | collective-permute-start | bytes 147464 | tf_op jit(solution)/shard_map/ppermute | solution.py:696
  50.4 17.2 %collective-permute-start.13 = (bf16[192,128]{1,0:T(8,128)(2,1)S(1)}, bf16[192,128]{1,0:T(8,128)(2,1)S(1)}, u32[]{:S(2)}, u32[]{:S(2)}) collective-permute-start(bf16[192,128]{1,0:T(8,128)(2,1)S(1)} %get-tuple-element.84), channel_id=1, source_target_pairs={{0,8},{4,12},{8,0},{12,4},{16,24},{20,28},{24,16},{28,20},{32,40},... | collective-permute-start | bytes 147464 | tf_op jit(solution)/shard_map/ppermute | solution.py:696
  51.4 17.1 %collective-permute-start.14 = (bf16[192,128]{1,0:T(8,128)(2,1)S(1)}, bf16[192,128]{1,0:T(8,128)(2,1)S(1)}, u32[]{:S(2)}, u32[]{:S(2)}) collective-permute-start(bf16[192,128]{1,0:T(8,128)(2,1)S(1)} %get-tuple-element.85), channel_id=1, source_target_pairs={{0,12},{4,8},{8,4},{12,0},{16,28},{20,24},{24,20},{28,16},{32,44},... | collective-permute-start | bytes 147464 | tf_op jit(solution)/shard_map/ppermute | solution.py:696
  52.7 0.7 copy-start.16
